TPU v7x, 128 devices: a whole 4x4x4 slice. The times are simulated.
128 devices in a mesh: op: 8 (over z, core), sec: 16 (over y, x).
Axes of the slice: x: 4, y: 4, z: 4, core: 2. Of those that a mesh axis runs over, the one named last changes fastest.
Arguments:
- psi: bfloat16 [256, 256, 256], P('sec'), may hold values from -2 to 2
- left_ops: bfloat16 [64, 256, 256], P('op', 'sec'), may hold values from -0.375 to 0.375
- right_ops: bfloat16 [64, 256, 256], P('op'), may hold values from -0.375 to 0.375
- op_shift: int32 [64], P('op'), may hold values from -2 to 2, as said below
- sector_dims: int32 [256], P('sec'), may hold values from 64 to 256, as said below
Outputs:
- sigma: bfloat16 [256, 256, 256], P('sec', 'op')
Inputs may be any that keep to these rules, and one draw needn't show every extreme that they name: `op_shift`: every value from -2 to 2 occurs. `sector_dims`: some sector has 256 live rows and some has 64.
All inputs are finite; a program needn't handle non-finite values.
Results may differ from a plain program's by a relative error of at most 0.0049.
Values may be sent and summed in bfloat16 or wider, within the bound.
No kernel may reach another device: no remote copies, remote signals or barrier semaphores. Data moves between devices by JAX's collectives and lax.ppermute only.
A program may use at most 64 MiB of HBM per device.

v0:
```python
import jax
import jax.numpy as jnp
from jax import lax
from jax.sharding import PartitionSpec as P

QMAX = 2


def passed_along(block, axis, distance):
    devices = range(lax.axis_size(axis))
    route = [(i - distance, i) for i in devices if i - distance in devices]
    return lax.ppermute(block, axis, route)


def on_device(psi, left_ops, right_ops, op_shift, sector_dims):
    sectors_here = psi.shape[0]
    width_full = psi.shape[2]
    margin = QMAX
    row_index = jnp.arange(width_full, dtype=jnp.int32)
    live_mask = (row_index[None, :] < sector_dims[:, None]).astype(jnp.bfloat16)
    masked = psi * live_mask[:, :, None] * live_mask[:, None, :]
    frame_length = sectors_here + 2 * margin
    slab_rows = lax.all_gather(left_ops, "sec", axis=1, tiled=True)

    def one_operator(placed, source_item):
        left_slab, right_factor, charge = source_item
        product = jnp.einsum(
            "ai,sij->saj", left_slab, masked, preferred_element_type=jnp.float32
        ).astype(jnp.bfloat16)
        images = jnp.einsum(
            "saj,bj->sab", product, right_factor, preferred_element_type=jnp.float32
        )
        padded = jnp.pad(images, ((margin, margin), (0, 0), (0, 0)))
        return (placed + jnp.roll(padded, charge, axis=0), None)

    start_value = jnp.zeros((frame_length, slab_rows.shape[1], width_full), jnp.float32)
    placed, _ = lax.scan(one_operator, start_value, (slab_rows, right_ops, op_shift))
    lower_edge = placed[:margin]
    upper_edge = placed[margin + sectors_here :]
    core_blocks = placed[margin : margin + sectors_here]
    from_below = passed_along(upper_edge.astype(jnp.bfloat16), "sec", 1).astype(upper_edge.dtype)
    from_above = passed_along(lower_edge.astype(jnp.bfloat16), "sec", -1).astype(lower_edge.dtype)
    core_blocks = core_blocks.at[:margin].add(from_below)
    core_blocks = core_blocks.at[sectors_here - margin :].add(from_above)
    summed = lax.psum_scatter(core_blocks, "op", scatter_dimension=1, tiled=True)
    rows_here = summed.shape[1]
    live_wide = live_mask.astype(jnp.float32)
    row_start = lax.axis_index("op") * rows_here
    live_rows = lax.dynamic_slice_in_dim(live_wide, row_start, rows_here, 1)
    return (summed * live_rows[:, :, None] * live_wide[:, None, :]).astype(jnp.bfloat16)


def solution(mesh):
    placed = (P("sec", None, None), P("op", "sec", None), P("op", None, None), P("op"), P("sec"))
    return jax.shard_map(
        on_device, mesh=mesh, in_specs=placed, out_specs=P("sec", "op", None), check_vma=False
    )
```

profile of v0, /device:TPU:0, one launch (start us, length us, event | category | flops | bytes accessed | tf_op | source)
XLA Modules:
  0.0 234.8 jit_solution(6703938685369636132)
XLA Ops:
  6.5 0.7 all-gather.2.cloned.1.call-update
  7.3 0.7 fusion.17
  8.0 1.9 multiply_multiply_fusion
  10.0 45.2 %all-gather.2.cloned.1.call-done = bf16[8,256,256]{2,1,0:T(8,128)(2,1)} async-done(((bf16[8,16,256]{2,1,0:T(8,128)(2,1)}), bf16[8,256,256]{2,1,0:T(8,128)(2,1)}) %all-gather.2.cloned.1.call-update) | async-done | bytes 1048592 | tf_op jit(solution)/shard_map/all_gather | solution.py:23
  55.2 113.4 %while.15 = (s32[]{:T(128)}, f32[20,256,256]{2,1,0:T(8,128)}, bf16[8,256,256]{2,1,0:T(8,128)(2,1)}, bf16[16,256,256]{2,1,0:T(8,128)(2,1)S(1)}, bf16[8,256,256]{2...) while((s32[]{:T(128)}, f32[20,256,256]{2,1,0:T(8,128)}, ...), condition=%wide.region_1.2_spmd.clone, body=%wide.region_0.1_spmd.clone.sunk | while | flops 1078722560 | bytes 23332080 | solution.py:37
  55.2 0.6 dynamic_slice.64
  56.4 4.8 %fusion.30 = f32[20,256,256]{2,1,0:T(8,128)} fusion(bf16[16,256,256]{2,1,0:T(8,128)(2,1)S(1)} %get-tuple-element.209, bf16[8,256,256]{2,1,0:T(8,128)(2,1)} %get-tuple-element.210, s32[]{:T(128)} %get-tuple-element.195, bf16[8,256,256]{2,1,0:T(8,128)(2,1)} %get-tuple-element.208), kind=kOutput, calls=%fused_computation.4.clone.1 | convolution fusion | flops 1074790400 | bytes 7603200 | tf_op jit(solution)/shard_map/while/body/eval_jaxpr/jit(_pad)/pad | solution.py:33
  61.2 6.8 %fusion.31 = f32[20,256,256]{2,1,0:T(8,128)} fusion(s32[]{:T(128)S(6)} %select_n.30, f32[20,256,256]{2,1,0:T(8,128)} %fusion.30, f32[20,256,256]{2,1,0:T(8,128)} %get-tuple-element.196, pred[]{:T(512)S(6)} %compare.15), kind=kLoop, calls=%fused_computation.3.clone.1 | loop fusion | flops 3932160 | bytes 15728645 | tf_op jit(solution)/shard_map/while/body/eval_jaxpr/add | solution.py:34
  69.2 4.8 %fusion.30 = f32[20,256,256]{2,1,0:T(8,128)} fusion(bf16[16,256,256]{2,1,0:T(8,128)(2,1)S(1)} %get-tuple-element.209, bf16[8,256,256]{2,1,0:T(8,128)(2,1)} %get-tuple-element.210, s32[]{:T(128)} %get-tuple-element.195, bf16[8,256,256]{2,1,0:T(8,128)(2,1)} %get-tuple-element.208), kind=kOutput, calls=%fused_computation.4.clone.1 | convolution fusion | flops 1074790400 | bytes 7603200 | tf_op jit(solution)/shard_map/while/body/eval_jaxpr/jit(_pad)/pad | solution.py:33
  74.0 8.3 %fusion.31 = f32[20,256,256]{2,1,0:T(8,128)} fusion(s32[]{:T(128)S(6)} %select_n.30, f32[20,256,256]{2,1,0:T(8,128)} %fusion.30, f32[20,256,256]{2,1,0:T(8,128)} %get-tuple-element.196, pred[]{:T(512)S(6)} %compare.15), kind=kLoop, calls=%fused_computation.3.clone.1 | loop fusion | flops 3932160 | bytes 15728645 | tf_op jit(solution)/shard_map/while/body/eval_jaxpr/add | solution.py:34
  82.3 0.6 dynamic_slice.64
  83.6 4.8 %fusion.30 = f32[20,256,256]{2,1,0:T(8,128)} fusion(bf16[16,256,256]{2,1,0:T(8,128)(2,1)S(1)} %get-tuple-element.209, bf16[8,256,256]{2,1,0:T(8,128)(2,1)} %get-tuple-element.210, s32[]{:T(128)} %get-tuple-element.195, bf16[8,256,256]{2,1,0:T(8,128)(2,1)} %get-tuple-element.208), kind=kOutput, calls=%fused_computation.4.clone.1 | convolution fusion | flops 1074790400 | bytes 7603200 | tf_op jit(solution)/shard_map/while/body/eval_jaxpr/jit(_pad)/pad | solution.py:33
  88.4 8.3 %fusion.31 = f32[20,256,256]{2,1,0:T(8,128)} fusion(s32[]{:T(128)S(6)} %select_n.30, f32[20,256,256]{2,1,0:T(8,128)} %fusion.30, f32[20,256,256]{2,1,0:T(8,128)} %get-tuple-element.196, pred[]{:T(512)S(6)} %compare.15), kind=kLoop, calls=%fused_computation.3.clone.1 | loop fusion | flops 3932160 | bytes 15728645 | tf_op jit(solution)/shard_map/while/body/eval_jaxpr/add | solution.py:34
  98.0 4.8 %fusion.30 = f32[20,256,256]{2,1,0:T(8,128)} fusion(bf16[16,256,256]{2,1,0:T(8,128)(2,1)S(1)} %get-tuple-element.209, bf16[8,256,256]{2,1,0:T(8,128)(2,1)} %get-tuple-element.210, s32[]{:T(128)} %get-tuple-element.195, bf16[8,256,256]{2,1,0:T(8,128)(2,1)} %get-tuple-element.208), kind=kOutput, calls=%fused_computation.4.clone.1 | convolution fusion | flops 1074790400 | bytes 7603200 | tf_op jit(solution)/shard_map/while/body/eval_jaxpr/jit(_pad)/pad | solution.py:33
  102.8 8.3 %fusion.31 = f32[20,256,256]{2,1,0:T(8,128)} fusion(s32[]{:T(128)S(6)} %select_n.30, f32[20,256,256]{2,1,0:T(8,128)} %fusion.30, f32[20,256,256]{2,1,0:T(8,128)} %get-tuple-element.196, pred[]{:T(512)S(6)} %compare.15), kind=kLoop, calls=%fused_computation.3.clone.1 | loop fusion | flops 3932160 | bytes 15728645 | tf_op jit(solution)/shard_map/while/body/eval_jaxpr/add | solution.py:34
  112.3 4.8 %fusion.30 = f32[20,256,256]{2,1,0:T(8,128)} fusion(bf16[16,256,256]{2,1,0:T(8,128)(2,1)S(1)} %get-tuple-element.209, bf16[8,256,256]{2,1,0:T(8,128)(2,1)} %get-tuple-element.210, s32[]{:T(128)} %get-tuple-element.195, bf16[8,256,256]{2,1,0:T(8,128)(2,1)} %get-tuple-element.208), kind=kOutput, calls=%fused_computation.4.clone.1 | convolution fusion | flops 1074790400 | bytes 7603200 | tf_op jit(solution)/shard_map/while/body/eval_jaxpr/jit(_pad)/pad | solution.py:33
  117.1 8.3 %fusion.31 = f32[20,256,256]{2,1,0:T(8,128)} fusion(s32[]{:T(128)S(6)} %select_n.30, f32[20,256,256]{2,1,0:T(8,128)} %fusion.30, f32[20,256,256]{2,1,0:T(8,128)} %get-tuple-element.196, pred[]{:T(512)S(6)} %compare.15), kind=kLoop, calls=%fused_computation.3.clone.1 | loop fusion | flops 3932160 | bytes 15728645 | tf_op jit(solution)/shard_map/while/body/eval_jaxpr/add | solution.py:34
  126.7 4.8 %fusion.30 = f32[20,256,256]{2,1,0:T(8,128)} fusion(bf16[16,256,256]{2,1,0:T(8,128)(2,1)S(1)} %get-tuple-element.209, bf16[8,256,256]{2,1,0:T(8,128)(2,1)} %get-tuple-element.210, s32[]{:T(128)} %get-tuple-element.195, bf16[8,256,256]{2,1,0:T(8,128)(2,1)} %get-tuple-element.208), kind=kOutput, calls=%fused_computation.4.clone.1 | convolution fusion | flops 1074790400 | bytes 7603200 | tf_op jit(solution)/shard_map/while/body/eval_jaxpr/jit(_pad)/pad | solution.py:33
  131.5 8.3 %fusion.31 = f32[20,256,256]{2,1,0:T(8,128)} fusion(s32[]{:T(128)S(6)} %select_n.30, f32[20,256,256]{2,1,0:T(8,128)} %fusion.30, f32[20,256,256]{2,1,0:T(8,128)} %get-tuple-element.196, pred[]{:T(512)S(6)} %compare.15), kind=kLoop, calls=%fused_computation.3.clone.1 | loop fusion | flops 3932160 | bytes 15728645 | tf_op jit(solution)/shard_map/while/body/eval_jaxpr/add | solution.py:34
  141.1 4.8 %fusion.30 = f32[20,256,256]{2,1,0:T(8,128)} fusion(bf16[16,256,256]{2,1,0:T(8,128)(2,1)S(1)} %get-tuple-element.209, bf16[8,256,256]{2,1,0:T(8,128)(2,1)} %get-tuple-element.210, s32[]{:T(128)} %get-tuple-element.195, bf16[8,256,256]{2,1,0:T(8,128)(2,1)} %get-tuple-element.208), kind=kOutput, calls=%fused_computation.4.clone.1 | convolution fusion | flops 1074790400 | bytes 7603200 | tf_op jit(solution)/shard_map/while/body/eval_jaxpr/jit(_pad)/pad | solution.py:33
  145.8 8.3 %fusion.31 = f32[20,256,256]{2,1,0:T(8,128)} fusion(s32[]{:T(128)S(6)} %select_n.30, f32[20,256,256]{2,1,0:T(8,128)} %fusion.30, f32[20,256,256]{2,1,0:T(8,128)} %get-tuple-element.196, pred[]{:T(512)S(6)} %compare.15), kind=kLoop, calls=%fused_computation.3.clone.1 | loop fusion | flops 3932160 | bytes 15728645 | tf_op jit(solution)/shard_map/while/body/eval_jaxpr/add | solution.py:34
  155.4 4.8 %fusion.30 = f32[20,256,256]{2,1,0:T(8,128)} fusion(bf16[16,256,256]{2,1,0:T(8,128)(2,1)S(1)} %get-tuple-element.209, bf16[8,256,256]{2,1,0:T(8,128)(2,1)} %get-tuple-element.210, s32[]{:T(128)} %get-tuple-element.195, bf16[8,256,256]{2,1,0:T(8,128)(2,1)} %get-tuple-element.208), kind=kOutput, calls=%fused_computation.4.clone.1 | convolution fusion | flops 1074790400 | bytes 7603200 | tf_op jit(solution)/shard_map/while/body/eval_jaxpr/jit(_pad)/pad | solution.py:33
  160.2 8.3 %fusion.31 = f32[20,256,256]{2,1,0:T(8,128)} fusion(s32[]{:T(128)S(6)} %select_n.30, f32[20,256,256]{2,1,0:T(8,128)} %fusion.30, f32[20,256,256]{2,1,0:T(8,128)} %get-tuple-element.196, pred[]{:T(512)S(6)} %compare.15), kind=kLoop, calls=%fused_computation.3.clone.1 | loop fusion | flops 3932160 | bytes 15728645 | tf_op jit(solution)/shard_map/while/body/eval_jaxpr/add | solution.py:34
  168.5 3.0 %convert.4 = bf16[20,256,256]{2,1,0:T(8,128)(2,1)S(1)} convert(f32[20,256,256]{2,1,0:T(8,128)} %get-tuple-element.109) | non-fusion elementwise | flops 1310720 | bytes 7864320 | tf_op jit(solution)/shard_map/convert.1
  171.6 3.2 %collective-permute-start = (bf16[2,256,256]{2,1,0:T(8,128)(2,1)S(1)}, bf16[2,256,256]{2,1,0:T(8,128)(2,1)S(1)}, u32[]{:S(2)}, u32[]{:S(2)}) collective-permute-start(bf16[2,256,256]{2,1,0:T(8,128)(2,1)S(1)} %get-tuple-element.144), channel_id=1, source_target_pairs={{0,1},{1,2},{2,3},{3,4},{4,5},{5,6},{6,7},{7,8},{8,9},{9,10},{10,1... | collective-permute-start | bytes 786440 | tf_op jit(solution)/shard_map/ppermute | solution.py:12
  174.8 1.3 collective-permute-start.1
  176.1 2.2 slice.60
  178.9 0.9 add_dynamic-update-slice_fusion
  179.8 3.3 %collective-permute-done.1 = bf16[2,256,256]{2,1,0:T(8,128)(2,1)S(1)} collective-permute-done((bf16[2,256,256]{2,1,0:T(8,128)(2,1)S(1)}, bf16[2,256,256]{2,1,0:T(8,128)(2,1)S(1)}, u32[]{:S(2)}, u32[]{:S(2)}) %collective-permute-start.1) | collective-permute-done | bytes 262176 | tf_op jit(solution)/shard_map/ppermute | solution.py:12
  183.1 1.9 fusion.15
  185.1 41.0 %reduce-scatter.2.cloned.1.call-done = f32[16,32,256]{2,1,0:T(8,128)} async-done(((f32[16,256,256]{2,1,0:T(8,128)}), f32[16,32,256]{2,1,0:T(8,128)}) %reduce-scatter.2.cloned.1.call-update) | async-done | bytes 524304 | tf_op jit(solution)/shard_map/reduce_scatter | solution.py:45
  226.1 1.9 multiply_convert_fusion
  (17 shorter events, 4.4 us)
Async XLA Ops:
  6.5 48.6 %copy-start.1 = (s32[8]{0:T(128)S(1)}, s32[8]{0:T(128)}, u32[]{:S(2)}) copy-start(s32[8]{0:T(128)} %param.14) | copy-start | bytes 100
  6.5 48.6 %all-gather.2.cloned.1.call-start = ((), (), s32[]{:S(2)}) async-start(), calls=%async_computation.1 | async-start | bytes 1114112 | tf_op jit(solution)/shard_map/all_gather | solution.py:23
  7.3 218.8 %reduce-scatter.2.cloned.1.call-start = ((), (), s32[]{:S(2)}) async-start(), calls=%async_computation.2 | async-start | bytes 4718592 | tf_op jit(solution)/shard_map/reduce_scatter | solution.py:45
  168.5 7.6 %copy-start = (f32[20,256,256]{2,1,0:T(8,128)S(1)}, f32[20,256,256]{2,1,0:T(8,128)}, u32[]{:S(2)}) copy-start(f32[20,256,256]{2,1,0:T(8,128)} %get-tuple-element.109) | copy-start | bytes 15728644
  171.6 7.4 %collective-permute-start = (bf16[2,256,256]{2,1,0:T(8,128)(2,1)S(1)}, bf16[2,256,256]{2,1,0:T(8,128)(2,1)S(1)}, u32[]{:S(2)}, u32[]{:S(2)}) collective-permute-start(bf16[2,256,256]{2,1,0:T(8,128)(2,1)S(1)} %get-tuple-element.144), channel_id=1, source_target_pairs={{0,1},{1,2},{2,3},{3,4},{4,5},{5,6},{6,7},{7,8},{8,9},{9,10},{10,1... | collective-permute-start | bytes 786440 | tf_op jit(solution)/shard_map/ppermute | solution.py:12
  174.8 8.3 %collective-permute-start.1 = (bf16[2,256,256]{2,1,0:T(8,128)(2,1)S(1)}, bf16[2,256,256]{2,1,0:T(8,128)(2,1)S(1)}, u32[]{:S(2)}, u32[]{:S(2)}) collective-permute-start(bf16[2,256,256]{2,1,0:T(8,128)(2,1)S(1)} %get-tuple-element.143), channel_id=1, source_target_pairs={{1,0},{2,1},{3,2},{4,3},{5,4},{6,5},{7,6},{8,7},{9,8},{10,9},{11,1... | collective-permute-start | bytes 786440 | tf_op jit(solution)/shard_map/ppermute | solution.py:12
Sparse Core Ops, SparseCore 0:
  9.5 45.6 all-gather.1
  185.1 40.9 reduce-scatter.1
where the time goes:
time: 235 us
  waiting for transfers between devices  90.8 us (39%)
  other arithmetic  75.4 us (32%)
  matrix products  38.1 us (16%)
  between operations  13.5 us (6%)
  local copies, waits for them, and re-layouts  7.2 us (3%)
  loops' own time  5.28 us (2%)
  starting transfers between devices  4.56 us (2%)
    add x8, other arithmetic, one_operator(): return (placed + jnp.roll(padded, charge, axis=0), None)  65.1 us
    all_gather x1, waiting for transfers between devices, on_device(): slab_rows = lax.all_gather(left_ops, 'sec', axis=1, tiled=True)  45.2 us
    reduce_scatter x1, waiting for transfers between devices, on_device(): lax.psum_scatter(core_blocks, 'op', scatter_dimension=1, tiled=True)  41 us
    pad x8, matrix products, one_operator(): padded = jnp.pad(images, ((margin, margin), (0, 0), (0, 0)))  38.1 us
    another operation x1, loops' own time, on_device(): lax.scan(one_operator, start_value, (slab_rows, right_ops, op_shift))  5.28 us
    dynamic_slice x8, local copies, waits for them, and re-layouts, on_device(): lax.scan(one_operator, start_value, (slab_rows, right_ops, op_shift))  4.86 us
  transfers between devices with their start and end apart: 4, of which 4 were waited for; matrix products, arithmetic and copies ran while one was open for 2% of the time, Pallas kernels for 0%

commit v1 on v0

v1 whole, which is shorter than its diff:
```python
import functools

import jax
import jax.numpy as jnp
from jax import lax
from jax.experimental import pallas as pl
from jax.experimental.pallas import tpu as pltpu
from jax.sharding import PartitionSpec as P

NZ, NC, NY, NX = 4, 2, 4, 4
B = 256
OPS = 8
SECS = 16
QMAX = 2
BF = jnp.bfloat16
F32 = jnp.float32
NT = (((1,), (1,)), ((), ()))


def flat(z, c, y, x):
    return ((z * NC + c) * NY + y) * NX + x


def move(block, target):
    route = []
    for z in range(NZ):
        for c in range(NC):
            for y in range(NY):
                for x in range(NX):
                    to = target(z, c, y, x)
                    if to is not None:
                        route.append((flat(z, c, y, x), flat(*to)))
    return lax.ppermute(block, ("op", "sec"), route)


def gather_first(d):
    return lambda z, c, y, x: (z, c, y, (x + d) % NX) if c == 0 else (z, c, (y + d) % NY, x)


def gather_second(d):
    return lambda z, c, y, x: (z, c, (y + d) % NY, x) if c == 0 else (z, c, y, (x + d) % NX)


def edge_target(z, c, y, x):
    q = y * NX + x + (1 if c == 0 else -1)
    return (z, c, q // NX, q % NX) if 0 <= q < NX * NY else None


def other_core(z, c, y, x):
    return (z, 1 - c, y, x)


def along_z(sign):
    return lambda z, c, y, x: ((z + (sign if c == 0 else -sign)) % NZ, c, y, x)


def first_product(shift_ref, dims_ref, psi_ref, right_ref, h_ref, masked_ref):
    rows = lax.broadcasted_iota(jnp.int32, (B, B), 0)
    cols = lax.broadcasted_iota(jnp.int32, (B, B), 1)

    def mask_one(s, _):
        d = dims_ref[s]
        keep = (rows < d) & (cols < d)
        masked_ref[s] = jnp.where(keep, psi_ref[s].astype(F32), 0.0).astype(BF)
        return 0

    lax.fori_loop(0, SECS, mask_one, 0)

    def one_target(t, _):
        for o in range(OPS):
            s = t - shift_ref[o]
            inside = (s >= 0) & (s < SECS)

            @pl.when(inside)
            def _():
                h = lax.dot_general(masked_ref[s], right_ref[o], NT, preferred_element_type=F32)
                h_ref[t, o * B:(o + 1) * B, :] = h.astype(BF)

            @pl.when(jnp.logical_not(inside))
            def _():
                h_ref[t, o * B:(o + 1) * B, :] = jnp.zeros((B, B), BF)
        return 0

    lax.fori_loop(0, SECS, one_target, 0)


def second_product(shift_ref, place_ref, t0, t1, t2, t3, edge_ref, right_ref, h_ref,
                   mine_ref, other_ref, left_ref, total_ref):
    t = pl.program_id(0)
    z, core, y, x = place_ref[0], place_ref[1], place_ref[2], place_ref[3]

    @pl.when(t == 0)
    def _():
        for e, block in enumerate((t0, t1, t2, t3)):
            for d in range(4):
                back_y = jnp.where(core == 0, e, d)
                back_x = jnp.where(core == 0, d, e)
                q = ((y - back_y + NY) % NY) * NX + (x - back_x + NX) % NX
                start = pl.multiple_of(q * 16, 16)
                for o in range(OPS):
                    left_ref[pl.ds(start, 16), o * B:(o + 1) * B] = block[d, o]

    total_ref[...] = jnp.dot(left_ref[...], h_ref[0], preferred_element_type=F32)

    @pl.when((t < QMAX) | (t >= SECS - QMAX))
    def _():
        for o in range(OPS):
            s = t - shift_ref[o]

            @pl.when((s < 0) | (s >= SECS))
            def _():
                e = jnp.where(s < 0, s + QMAX, s - SECS + QMAX)
                h = lax.dot_general(edge_ref[e], right_ref[o], NT, preferred_element_type=F32)
                total_ref[...] += jnp.dot(left_ref[:, o * B:(o + 1) * B], h.astype(BF), preferred_element_type=F32)

    for p in range(NZ * NC):
        to_z, to_core = p // 2, p % 2
        ahead = (to_z - z + NZ) % NZ if to_core == 0 else (z - to_z + NZ) % NZ

        @pl.when(core == to_core)
        def _():
            mine_ref[ahead, 0] = total_ref[p * 32:(p + 1) * 32, :]

        @pl.when(core != to_core)
        def _():
            other_ref[ahead, 0] = total_ref[p * 32:(p + 1) * 32, :].astype(BF)


def on_device(psi, left_ops, right_ops, op_shift, sector_dims):
    p, q = lax.axis_index("op"), lax.axis_index("sec")
    core = p % NC
    place = jnp.stack([p // NC, core, q // NX, q % NX]).astype(jnp.int32)
    index = jnp.arange(B, dtype=jnp.int32)

    ends = jnp.where(core == 0, psi[SECS - QMAX:], psi[:QMAX])
    end_dims = jnp.where(core == 0, sector_dims[SECS - QMAX:], sector_dims[:QMAX])
    live = (index[None, :] < end_dims[:, None])
    ends = jnp.where(live[:, :, None] & live[:, None, :], ends, jnp.zeros((), BF))

    firsts = [left_ops] + [move(left_ops, gather_first(d)) for d in (1, 3, 2)]
    edge_in = move(ends, edge_target)
    strips = jnp.stack([firsts[0], firsts[1], firsts[3], firsts[2]])
    seconds = [move(strips, gather_second(d)) for d in (1, 3, 2)]
    t0, t1, t3, t2 = strips, *seconds
    edge_other = move(edge_in, other_core)
    edges = jnp.where(core == 0, jnp.concatenate([edge_in, edge_other]), jnp.concatenate([edge_other, edge_in]))

    smem = pl.BlockSpec(memory_space=pltpu.SMEM)
    vmem = pl.BlockSpec(memory_space=pltpu.VMEM)
    flops = 2 * OPS * SECS * B * B * B
    h = pl.pallas_call(
        first_product,
        out_shape=jax.ShapeDtypeStruct((SECS, OPS * B, B), BF),
        in_specs=[smem, smem, vmem, vmem],
        out_specs=vmem,
        scratch_shapes=[pltpu.VMEM((SECS, B, B), BF)],
        compiler_params=pltpu.CompilerParams(vmem_limit_bytes=40 << 20),
        cost_estimate=pl.CostEstimate(flops=flops, bytes_accessed=20 << 20, transcendentals=0),
        name="first_product",
    )(op_shift, sector_dims, psi, right_ops)

    def whole(*shape):
        return pl.BlockSpec(shape, lambda t: (0,) * len(shape))

    strip = whole(4, OPS, 16, B)
    mine, other = pl.pallas_call(
        second_product,
        grid=(SECS,),
        out_shape=[jax.ShapeDtypeStruct((NZ, SECS, 32, B), F32), jax.ShapeDtypeStruct((NZ, SECS, 32, B), BF)],
        in_specs=[smem, smem, strip, strip, strip, strip, whole(2 * QMAX, B, B), whole(OPS, B, B),
                  pl.BlockSpec((1, OPS * B, B), lambda t: (t, 0, 0))],
        out_specs=[pl.BlockSpec((NZ, 1, 32, B), lambda t: (0, t, 0, 0))] * 2,
        scratch_shapes=[pltpu.VMEM((B, OPS * B), BF), pltpu.VMEM((B, B), F32)],
        compiler_params=pltpu.CompilerParams(vmem_limit_bytes=40 << 20),
        cost_estimate=pl.CostEstimate(flops=flops, bytes_accessed=24 << 20, transcendentals=0),
        name="second_product",
    )(op_shift, place, t0, t1, t2, t3, edges, right_ops, h)

    total = mine + move(other, other_core).astype(F32)
    far = move(total[2].astype(BF), along_z(1))
    back = move(total[3].astype(BF), along_z(-1))
    near = move((total[1] + far.astype(F32)).astype(BF), along_z(1))
    summed = total[0] + back.astype(F32) + near.astype(F32)
    live = index[None, :] < sector_dims[:, None]
    mine_rows = p * 32 + jnp.arange(32, dtype=jnp.int32)
    live_rows = mine_rows[None, :] < sector_dims[:, None]
    return jnp.where(live_rows[:, :, None] & live[:, None, :], summed, 0.0).astype(BF)


def solution(mesh):
    placed = (P("sec", None, None), P("op", "sec", None), P("op", None, None), P("op"), P("sec"))
    return jax.shard_map(
        on_device, mesh=mesh, in_specs=placed, out_specs=P("sec", "op", None), check_vma=False
    )
```

time: 235 us -> 101 us (0.43)
  waiting for transfers between devices: 90.8 us -> 17.8 us
  other arithmetic: 75.4 us -> 4.61 us
  Pallas kernels: 0 us -> 53.8 us
  matrix products: 38.1 us -> 0 us
  starting transfers between devices: 4.56 us -> 19.9 us
  between operations: 13.5 us -> 0.12 us
  loops' own time: 5.28 us -> 0 us
  local copies, waits for them, and re-layouts: 7.2 us -> 4.17 us
    add x8 -> x1, other arithmetic: 65.1 us -> 0.01 us  [on_device(): mine_rows = p * 32 + jnp.arange(32, dtype=jnp.int32)]
    pallas_call x0 -> x2, Pallas kernels: none -> 53.8 us  [the longest x1 33.6 us: on_device(): pl.pallas_call(first_product, out_shape=jax.ShapeDtypeStruct((SECS, OPS *...]
    all_gather x1 -> x0, waiting for transfers between devices: 45.2 us -> none  [on_device(): slab_rows = lax.all_gather(left_ops, 'sec', axis=1, tiled=True)]
    reduce_scatter x1 -> x0, waiting for transfers between devices: 41 us -> none  [on_device(): lax.psum_scatter(core_blocks, 'op', scatter_dimension=1, tiled=True)]
    pad x8 -> x0, matrix products: 38.1 us -> none  [one_operator(): padded = jnp.pad(images, ((margin, margin), (0, 0), (0, 0)))]
    ppermute x2 -> x12, starting transfers between devices: 4.52 us -> 19.9 us  [move(): return lax.ppermute(block, ('op', 'sec'), route)]
    ppermute x2 -> x12, waiting for transfers between devices: 3.87 us -> 17.8 us  [move(): return lax.ppermute(block, ('op', 'sec'), route)]
    another operation x1 -> x0, loops' own time: 5.28 us -> none  [on_device(): lax.scan(one_operator, start_value, (slab_rows, right_ops, op_shift))]
  transfers between devices with their start and end apart: 4 -> 12, of which waited for: 4 -> 6; matrix products, arithmetic and copies ran while one was open for 2% -> 1% of each run, Pallas kernels for 0% -> 33%
where the time goes in v1:
time: 101 us
  Pallas kernels  53.8 us (53%)
  starting transfers between devices  19.9 us (20%)
  waiting for transfers between devices  17.8 us (18%)
  other arithmetic  4.61 us (5%)
  local copies, waits for them, and re-layouts  4.17 us (4%)
    pallas_call x1, Pallas kernels, on_device(): pl.pallas_call(first_product, out_shape=jax.ShapeDtypeStruct((SECS, OPS *...  33.6 us
    pallas_call x1, Pallas kernels, on_device(): pl.pallas_call(second_product, grid=(SECS,), out_shape=[jax.ShapeDtypeStr...  20.3 us
    ppermute x12, starting transfers between devices, move(): return lax.ppermute(block, ('op', 'sec'), route)  19.9 us
    ppermute x12, waiting for transfers between devices, move(): return lax.ppermute(block, ('op', 'sec'), route)  17.8 us
    unnamed x14, local copies, waits for them, and re-layouts  4.14 us
  transfers between devices with their start and end apart: 12, of which 6 were waited for; matrix products, arithmetic and copies ran while one was open for 1% of the time, Pallas kernels for 33%

profile of v1, /device:TPU:0, one launch (start us, length us, event | category | flops | bytes accessed | tf_op | source)
XLA Modules:
  0.0 100.5 jit_solution(4654083140386818940)
XLA Ops:
  0.0 0.8 broadcast_select_fusion
  0.8 0.1 iota_compare_fusion.1
  0.9 1.2 %and_select_fusion = bf16[2,256,256]{2,1,0:T(8,128)(2,1)S(1)} fusion(bf16[16,256,256]{2,1,0:T(8,128)(2,1)} %psi_ref.1, pred[]{:T(512)S(6)} %eq.8, pred[2,256]{1,0:T(4,128)(4,1)S(1)} %iota_compare_fusion.1), kind=kLoop, calls=%fused_computation.10 | loop fusion | flops 393216 | bytes 788481 | tf_op jit(solution)/shard_map/jit(_where)/select_n | solution.py:138
  2.1 3.5 %collective-permute-start.6 = (bf16[2,256,256]{2,1,0:T(8,128)(2,1)S(1)}, bf16[2,256,256]{2,1,0:T(8,128)(2,1)S(1)}, u32[]{:S(2)}, u32[]{:S(2)}) collective-permute-start(bf16[2,256,256]{2,1,0:T(8,128)(2,1)S(1)} %and_select_fusion), channel_id=1, source_target_pairs={{0,1},{1,2},{2,3},{3,4},{4,5},{5,6},{6,7},{7,8},{8,9},{9,10},{10,1... | collective-permute-start | bytes 786440 | tf_op jit(solution)/shard_map/ppermute | solution.py:33
  5.6 1.5 %collective-permute-start = (bf16[8,16,256]{2,1,0:T(8,128)(2,1)}, bf16[8,16,256]{2,1,0:T(8,128)(2,1)S(1)}, u32[]{:S(2)}, u32[]{:S(2)}) collective-permute-start(bf16[8,16,256]{2,1,0:T(8,128)(2,1)} %param.6), channel_id=1, source_target_pairs={{0,1},{1,2},{2,3},{3,0},{4,5},{5,6},{6,7},{7,4},{8,9},{9,10},{10,1... | collective-permute-start | bytes 196616 | tf_op jit(solution)/shard_map/ppermute | solution.py:33
  7.1 2.7 %collective-permute-start.1 = (bf16[8,16,256]{2,1,0:T(8,128)(2,1)}, bf16[8,16,256]{2,1,0:T(8,128)(2,1)S(1)}, u32[]{:S(2)}, u32[]{:S(2)}) collective-permute-start(bf16[8,16,256]{2,1,0:T(8,128)(2,1)} %param.6), channel_id=1, source_target_pairs={{0,2},{1,3},{2,0},{3,1},{4,6},{5,7},{6,4},{7,5},{8,10},{9,11},{10,... | collective-permute-start | bytes 196616 | tf_op jit(solution)/shard_map/ppermute | solution.py:33
  9.8 1.1 %collective-permute-start.2 = (bf16[8,16,256]{2,1,0:T(8,128)(2,1)}, bf16[8,16,256]{2,1,0:T(8,128)(2,1)S(1)}, u32[]{:S(2)}, u32[]{:S(2)}) collective-permute-start(bf16[8,16,256]{2,1,0:T(8,128)(2,1)} %param.6), channel_id=1, source_target_pairs={{0,3},{1,0},{2,1},{3,2},{4,7},{5,4},{6,5},{7,6},{8,11},{9,8},{10,9... | collective-permute-start | bytes 196616 | tf_op jit(solution)/shard_map/ppermute | solution.py:33
  11.0 2.4 %collective-permute-done = bf16[8,16,256]{2,1,0:T(8,128)(2,1)S(1)} collective-permute-done((bf16[8,16,256]{2,1,0:T(8,128)(2,1)}, bf16[8,16,256]{2,1,0:T(8,128)(2,1)S(1)}, u32[]{:S(2)}, u32[]{:S(2)}) %collective-permute-start) | collective-permute-done | bytes 65568 | tf_op jit(solution)/shard_map/ppermute | solution.py:33
  13.4 0.7 collective-permute-done.1
  14.1 0.2 collective-permute-done.2
  14.3 0.9 pad_maximum_fusion.t0
  15.2 1.6 %collective-permute-start.3 = (bf16[4,8,16,256]{3,2,1,0:T(8,128)(2,1)S(1)}, bf16[4,8,16,256]{3,2,1,0:T(8,128)(2,1)S(1)}, u32[]{:S(2)}, u32[]{:S(2)}) collective-permute-start(bf16[4,8,16,256]{3,2,1,0:T(8,128)(2,1)S(1)} %pad_maximum_fusion.t0), channel_id=1, source_target_pairs={{0,4},{1,5},{2,6},{3,7},{4,8},{5,9},{6,10},{7,11},{8,12},{9,13},{1... | collective-permute-start | bytes 786440 | tf_op jit(solution)/shard_map/ppermute | solution.py:33
  16.8 2.6 %collective-permute-start.4 = (bf16[4,8,16,256]{3,2,1,0:T(8,128)(2,1)S(1)}, bf16[4,8,16,256]{3,2,1,0:T(8,128)(2,1)S(1)}, u32[]{:S(2)}, u32[]{:S(2)}) collective-permute-start(bf16[4,8,16,256]{3,2,1,0:T(8,128)(2,1)S(1)} %pad_maximum_fusion.t0), channel_id=1, source_target_pairs={{0,8},{1,9},{2,10},{3,11},{4,12},{5,13},{6,14},{7,15},{8,0},{9,1},... | collective-permute-start | bytes 786440 | tf_op jit(solution)/shard_map/ppermute | solution.py:33
  19.4 1.4 %collective-permute-start.5 = (bf16[4,8,16,256]{3,2,1,0:T(8,128)(2,1)S(1)}, bf16[4,8,16,256]{3,2,1,0:T(8,128)(2,1)S(1)}, u32[]{:S(2)}, u32[]{:S(2)}) collective-permute-start(bf16[4,8,16,256]{3,2,1,0:T(8,128)(2,1)S(1)} %pad_maximum_fusion.t0), channel_id=1, source_target_pairs={{0,12},{1,13},{2,14},{3,15},{4,0},{5,1},{6,2},{7,3},{8,4},{9,5},{1... | collective-permute-start | bytes 786440 | tf_op jit(solution)/shard_map/ppermute | solution.py:33
  20.8 1.2 %copy-done = bf16[8,256,256]{2,1,0:T(8,128)(2,1)S(1)} copy-done((bf16[8,256,256]{2,1,0:T(8,128)(2,1)S(1)}, bf16[8,256,256]{2,1,0:T(8,128)(2,1)}, u32[]{:S(2)}) %copy-start) | copy-done | bytes 1048600
  22.0 1.6 %copy-done.2 = bf16[16,256,256]{2,1,0:T(8,128)(2,1)S(1)} copy-done((bf16[16,256,256]{2,1,0:T(8,128)(2,1)S(1)}, bf16[16,256,256]{2,1,0:T(8,128)(2,1)}, u32[]{:S(2)}) %copy-start.2) | copy-done | bytes 2097176
  23.6 0.7 copy-done.3
  24.3 0.7 copy-done.5
  24.9 33.6 %first_product.1.h_ref = bf16[16,2048,256]{2,1,0:T(8,128)(2,1)} custom-call(s32[8]{0:T(128)S(1)} %copy-done.5, s32[16]{0:T(128)S(1)} %copy-done.3, bf16[16,256,256]{2,1,0:T(8,128)(2,1)S(1)} %copy-done.2, bf16[8,256,256]{2,1,0:T(8,128)(2,1)S(1)} %copy-done), custom_call_target="tpu_custom_call" | custom-call | flops 4294967296 | bytes 20971520 | tf_op jit(solution)/shard_map/first_product/pallas_call | solution.py:151
  58.5 0.1 pad_add_fusion.place_ref
  58.6 0.1 maximum_select_fusion.edge_ref
  58.7 20.3 %second_product.1 = (f32[4,16,32,256]{3,2,1,0:T(8,128)S(1)}, bf16[4,16,32,256]{3,2,1,0:T(8,128)(2,1)S(1)}) custom-call(s32[8]{0:T(128)S(1)} %copy-done.6, s32[4]{0:T(128)S(1)} %pad_add_fusion.place_ref, bf16[4,8,16,256]{3,2,1,0:T(8,128)(2,1)S(1)} %pad_maximum_fusion.t0, bf16[4,8,16,256]{3,2,1,0:T(8,128)(2,1)S(1)} %collective-permute-done.3.t1, ...), custom_call_target="tpu_custom_call" | custom-call | flops 4294967296 | bytes 25165824 | tf_op jit(solution)/shard_map/second_product/pallas_call | solution.py:166
  79.0 0.2 collective-permute-start.8
  79.2 2.6 %collective-permute-done.8 = bf16[4,16,32,256]{3,2,1,0:T(8,128)(2,1)S(1)} collective-permute-done((bf16[4,16,32,256]{3,2,1,0:T(8,128)(2,1)S(1)}, bf16[4,16,32,256]{3,2,1,0:T(8,128)(2,1)S(1)}, u32[]{:S(2)}, u32[]{:S(2)}) %collective-permute-start.8) | collective-permute-done | bytes 1048608 | tf_op jit(solution)/shard_map/ppermute | solution.py:33
  81.8 0.4 fusion.6
  82.2 2.2 %collective-permute-start.10 = (bf16[16,32,256]{2,1,0:T(8,128)(2,1)S(1)}, bf16[16,32,256]{2,1,0:T(8,128)(2,1)S(1)}, u32[]{:S(2)}, u32[]{:S(2)}) collective-permute-start(bf16[16,32,256]{2,1,0:T(8,128)(2,1)S(1)} %get-tuple-element.12), channel_id=1, source_target_pairs={{0,32},{1,33},{2,34},{3,35},{4,36},{5,37},{6,38},{7,39},{8,40},{9,... | collective-permute-start | bytes 786440 | tf_op jit(solution)/shard_map/ppermute | solution.py:33
  84.5 2.3 %collective-permute-start.9 = (bf16[16,32,256]{2,1,0:T(8,128)(2,1)S(1)}, bf16[16,32,256]{2,1,0:T(8,128)(2,1)S(1)}, u32[]{:S(2)}, u32[]{:S(2)}) collective-permute-start(bf16[16,32,256]{2,1,0:T(8,128)(2,1)S(1)} %get-tuple-element.11), channel_id=1, source_target_pairs={{0,96},{1,97},{2,98},{3,99},{4,100},{5,101},{6,102},{7,103},{8,104... | collective-permute-start | bytes 786440 | tf_op jit(solution)/shard_map/ppermute | solution.py:33
  86.8 4.9 %collective-permute-done.10 = bf16[16,32,256]{2,1,0:T(8,128)(2,1)S(1)} collective-permute-done((bf16[16,32,256]{2,1,0:T(8,128)(2,1)S(1)}, bf16[16,32,256]{2,1,0:T(8,128)(2,1)S(1)}, u32[]{:S(2)}, u32[]{:S(2)}) %collective-permute-start.10) | collective-permute-done | bytes 262176 | tf_op jit(solution)/shard_map/ppermute | solution.py:33
  91.7 0.1 fusion.1
  91.8 0.7 collective-permute-start.11
  92.6 7.0 %collective-permute-done.11 = bf16[16,32,256]{2,1,0:T(8,128)(2,1)S(1)} collective-permute-done((bf16[16,32,256]{2,1,0:T(8,128)(2,1)S(1)}, bf16[16,32,256]{2,1,0:T(8,128)(2,1)S(1)}, u32[]{:S(2)}, u32[]{:S(2)}) %collective-permute-start.11) | collective-permute-done | bytes 262176 | tf_op jit(solution)/shard_map/ppermute | solution.py:33
  99.6 0.9 fusion.5
  (21 shorter events, 0.2 us)
Async XLA Ops:
  2.1 18.8 %collective-permute-start.6 = (bf16[2,256,256]{2,1,0:T(8,128)(2,1)S(1)}, bf16[2,256,256]{2,1,0:T(8,128)(2,1)S(1)}, u32[]{:S(2)}, u32[]{:S(2)}) collective-permute-start(bf16[2,256,256]{2,1,0:T(8,128)(2,1)S(1)} %and_select_fusion), channel_id=1, source_target_pairs={{0,1},{1,2},{2,3},{3,4},{4,5},{5,6},{6,7},{7,8},{8,9},{9,10},{10,1... | collective-permute-start | bytes 786440 | tf_op jit(solution)/shard_map/ppermute | solution.py:33
  5.6 7.8 %collective-permute-start = (bf16[8,16,256]{2,1,0:T(8,128)(2,1)}, bf16[8,16,256]{2,1,0:T(8,128)(2,1)S(1)}, u32[]{:S(2)}, u32[]{:S(2)}) collective-permute-start(bf16[8,16,256]{2,1,0:T(8,128)(2,1)} %param.6), channel_id=1, source_target_pairs={{0,1},{1,2},{2,3},{3,0},{4,5},{5,6},{6,7},{7,4},{8,9},{9,10},{10,1... | collective-permute-start | bytes 196616 | tf_op jit(solution)/shard_map/ppermute | solution.py:33
  7.1 7.0 %collective-permute-start.1 = (bf16[8,16,256]{2,1,0:T(8,128)(2,1)}, bf16[8,16,256]{2,1,0:T(8,128)(2,1)S(1)}, u32[]{:S(2)}, u32[]{:S(2)}) collective-permute-start(bf16[8,16,256]{2,1,0:T(8,128)(2,1)} %param.6), channel_id=1, source_target_pairs={{0,2},{1,3},{2,0},{3,1},{4,6},{5,7},{6,4},{7,5},{8,10},{9,11},{10,... | collective-permute-start | bytes 196616 | tf_op jit(solution)/shard_map/ppermute | solution.py:33
  9.8 4.5 %collective-permute-start.2 = (bf16[8,16,256]{2,1,0:T(8,128)(2,1)}, bf16[8,16,256]{2,1,0:T(8,128)(2,1)S(1)}, u32[]{:S(2)}, u32[]{:S(2)}) collective-permute-start(bf16[8,16,256]{2,1,0:T(8,128)(2,1)} %param.6), channel_id=1, source_target_pairs={{0,3},{1,0},{2,1},{3,2},{4,7},{5,4},{6,5},{7,6},{8,11},{9,8},{10,9... | collective-permute-start | bytes 196616 | tf_op jit(solution)/shard_map/ppermute | solution.py:33
  14.3 44.4 %copy-start.6 = (s32[8]{0:T(128)S(1)}, s32[8]{0:T(128)}, u32[]{:S(2)}) copy-start(s32[8]{0:T(128)} %shift_ref.3) | copy-start | bytes 100
  15.2 43.5 %collective-permute-start.3 = (bf16[4,8,16,256]{3,2,1,0:T(8,128)(2,1)S(1)}, bf16[4,8,16,256]{3,2,1,0:T(8,128)(2,1)S(1)}, u32[]{:S(2)}, u32[]{:S(2)}) collective-permute-start(bf16[4,8,16,256]{3,2,1,0:T(8,128)(2,1)S(1)} %pad_maximum_fusion.t0), channel_id=1, source_target_pairs={{0,4},{1,5},{2,6},{3,7},{4,8},{5,9},{6,10},{7,11},{8,12},{9,13},{1... | collective-permute-start | bytes 786440 | tf_op jit(solution)/shard_map/ppermute | solution.py:33
  16.8 41.8 %collective-permute-start.4 = (bf16[4,8,16,256]{3,2,1,0:T(8,128)(2,1)S(1)}, bf16[4,8,16,256]{3,2,1,0:T(8,128)(2,1)S(1)}, u32[]{:S(2)}, u32[]{:S(2)}) collective-permute-start(bf16[4,8,16,256]{3,2,1,0:T(8,128)(2,1)S(1)} %pad_maximum_fusion.t0), channel_id=1, source_target_pairs={{0,8},{1,9},{2,10},{3,11},{4,12},{5,13},{6,14},{7,15},{8,0},{9,1},... | collective-permute-start | bytes 786440 | tf_op jit(solution)/shard_map/ppermute | solution.py:33
  19.4 39.3 %collective-permute-start.5 = (bf16[4,8,16,256]{3,2,1,0:T(8,128)(2,1)S(1)}, bf16[4,8,16,256]{3,2,1,0:T(8,128)(2,1)S(1)}, u32[]{:S(2)}, u32[]{:S(2)}) collective-permute-start(bf16[4,8,16,256]{3,2,1,0:T(8,128)(2,1)S(1)} %pad_maximum_fusion.t0), channel_id=1, source_target_pairs={{0,12},{1,13},{2,14},{3,15},{4,0},{5,1},{6,2},{7,3},{8,4},{9,5},{1... | collective-permute-start | bytes 786440 | tf_op jit(solution)/shard_map/ppermute | solution.py:33
  20.8 37.8 %collective-permute-start.7 = (bf16[2,256,256]{2,1,0:T(8,128)(2,1)S(1)}, bf16[2,256,256]{2,1,0:T(8,128)(2,1)S(1)}, u32[]{:S(2)}, u32[]{:S(2)}) collective-permute-start(bf16[2,256,256]{2,1,0:T(8,128)(2,1)S(1)} %collective-permute-done.6), channel_id=1, source_target_pairs={{0,16},{1,17},{2,18},{3,19},{4,20},{5,21},{6,22},{7,23},{8,24},{9,... | collective-permute-start | bytes 786440 | tf_op jit(solution)/shard_map/ppermute | solution.py:33
  20.8 1.2 %copy-start = (bf16[8,256,256]{2,1,0:T(8,128)(2,1)S(1)}, bf16[8,256,256]{2,1,0:T(8,128)(2,1)}, u32[]{:S(2)}) copy-start(bf16[8,256,256]{2,1,0:T(8,128)(2,1)} %right_ref.3) | copy-start | bytes 3145732
  22.0 1.6 %copy-start.2 = (bf16[16,256,256]{2,1,0:T(8,128)(2,1)S(1)}, bf16[16,256,256]{2,1,0:T(8,128)(2,1)}, u32[]{:S(2)}) copy-start(bf16[16,256,256]{2,1,0:T(8,128)(2,1)} %psi_ref.1) | copy-start | bytes 6291460
  23.6 0.7 copy-start.3
  24.3 0.7 copy-start.5
  24.9 33.8 %copy-start.1 = (bf16[8,256,256]{2,1,0:T(8,128)(2,1)S(1)}, bf16[8,256,256]{2,1,0:T(8,128)(2,1)}, u32[]{:S(2)}) copy-start(bf16[8,256,256]{2,1,0:T(8,128)(2,1)} %right_ref.3) | copy-start | bytes 3145732
  79.0 2.7 %collective-permute-start.8 = (bf16[4,16,32,256]{3,2,1,0:T(8,128)(2,1)S(1)}, bf16[4,16,32,256]{3,2,1,0:T(8,128)(2,1)S(1)}, u32[]{:S(2)}, u32[]{:S(2)}) collective-permute-start(bf16[4,16,32,256]{3,2,1,0:T(8,128)(2,1)S(1)} %get-tuple-element.8), channel_id=1, source_target_pairs={{0,16},{1,17},{2,18},{3,19},{4,20},{5,21},{6,22},{7,23},{8,24},{9,... | collective-permute-start | bytes 3145736 | tf_op jit(solution)/shard_map/ppermute | solution.py:33
  82.2 10.3 %copy-start.4 = (s32[16]{0:T(128)S(1)}, s32[16]{0:T(128)}, u32[]{:S(2)}) copy-start(s32[16]{0:T(128)} %dims_ref.1) | copy-start | bytes 196
  82.2 9.4 %collective-permute-start.10 = (bf16[16,32,256]{2,1,0:T(8,128)(2,1)S(1)}, bf16[16,32,256]{2,1,0:T(8,128)(2,1)S(1)}, u32[]{:S(2)}, u32[]{:S(2)}) collective-permute-start(bf16[16,32,256]{2,1,0:T(8,128)(2,1)S(1)} %get-tuple-element.12), channel_id=1, source_target_pairs={{0,32},{1,33},{2,34},{3,35},{4,36},{5,37},{6,38},{7,39},{8,40},{9,... | collective-permute-start | bytes 786440 | tf_op jit(solution)/shard_map/ppermute | solution.py:33
  84.5 8.2 %collective-permute-start.9 = (bf16[16,32,256]{2,1,0:T(8,128)(2,1)S(1)}, bf16[16,32,256]{2,1,0:T(8,128)(2,1)S(1)}, u32[]{:S(2)}, u32[]{:S(2)}) collective-permute-start(bf16[16,32,256]{2,1,0:T(8,128)(2,1)S(1)} %get-tuple-element.11), channel_id=1, source_target_pairs={{0,96},{1,97},{2,98},{3,99},{4,100},{5,101},{6,102},{7,103},{8,104... | collective-permute-start | bytes 786440 | tf_op jit(solution)/shard_map/ppermute | solution.py:33
  91.8 7.9 %collective-permute-start.11 = (bf16[16,32,256]{2,1,0:T(8,128)(2,1)S(1)}, bf16[16,32,256]{2,1,0:T(8,128)(2,1)S(1)}, u32[]{:S(2)}, u32[]{:S(2)}) collective-permute-start(bf16[16,32,256]{2,1,0:T(8,128)(2,1)S(1)} %fusion.1), channel_id=1, source_target_pairs={{0,32},{1,33},{2,34},{3,35},{4,36},{5,37},{6,38},{7,39},{8,40},{9,... | collective-permute-start | bytes 786440 | tf_op jit(solution)/shard_map/ppermute | solution.py:33

commit v2 on v1

v2 whole, which is shorter than its diff:
```python
import jax
import jax.numpy as jnp
from jax import lax
from jax.experimental import pallas as pl
from jax.experimental.pallas import tpu as pltpu
from jax.sharding import PartitionSpec as P

NZ, NC, NY, NX = 4, 2, 4, 4
B = 256
OPS = 8
SECS = 16
QMAX = 2
HELD = SECS + 2 * QMAX
BF = jnp.bfloat16
F32 = jnp.float32


def flat(z, c, y, x):
    return ((z * NC + c) * NY + y) * NX + x


def move(block, target):
    route = []
    for z in range(NZ):
        for c in range(NC):
            for y in range(NY):
                for x in range(NX):
                    to = target(z, c, y, x)
                    if to is not None:
                        route.append((flat(z, c, y, x), flat(*to)))
    return lax.ppermute(block, ("op", "sec"), route)


def gather_first(d):
    return lambda z, c, y, x: (z, c, y, (x + d) % NX) if c == 0 else (z, c, (y + d) % NY, x)


def gather_second(d):
    return lambda z, c, y, x: (z, c, (y + d) % NY, x) if c == 0 else (z, c, y, (x + d) % NX)


def edge_target(z, c, y, x):
    q = y * NX + x + (1 if c == 0 else -1)
    return (z, c, q // NX, q % NX) if 0 <= q < NX * NY else None


def other_core(z, c, y, x):
    return (z, 1 - c, y, x)


def along_z(sign):
    return lambda z, c, y, x: ((z + (sign if c == 0 else -sign)) % NZ, c, y, x)


def mask_sectors(dims_ref, place_ref, psi_ref, masked_ref, ends_ref):
    rows = lax.broadcasted_iota(jnp.int32, (B, B), 0)
    cols = lax.broadcasted_iota(jnp.int32, (B, B), 1)

    def mask_one(s, _):
        d = dims_ref[s]
        keep = (rows < d) & (cols < d)
        masked_ref[s] = jnp.where(keep, psi_ref[s].astype(F32), 0.0).astype(BF)
        return 0

    lax.fori_loop(0, SECS, mask_one, 0)
    start = (1 - place_ref[1]) * (SECS - QMAX)
    for e in range(QMAX):
        ends_ref[e] = masked_ref[start + e]


def stack_strips(s0, s1, s2, s3, out_ref):
    for d, strip in enumerate((s0, s1, s2, s3)):
        out_ref[d] = strip[...]


def own_sectors(masked_ref, right_ref, h_ref):
    def one_operator(o, _):
        right_t = right_ref[o].T
        for s in range(0, SECS, 4):
            h = jnp.dot(masked_ref[s:s + 4].reshape(4 * B, B), right_t, preferred_element_type=F32)
            h_ref[o, (s + QMAX) * B:(s + QMAX + 4) * B, :] = h.astype(BF)
        return 0

    lax.fori_loop(0, OPS, one_operator, 0)


def edge_sectors(place_ref, edge_in, edge_other, right_ref, _, h_ref):
    below = place_ref[1] * (SECS + QMAX) * B

    def one_operator(o, _):
        right_t = right_ref[o].T
        for edge, start in ((edge_in, below), (edge_other, (SECS + QMAX) * B - below)):
            h = jnp.dot(edge[...].reshape(QMAX * B, B), right_t, preferred_element_type=F32)
            h_ref[o, pl.ds(pl.multiple_of(start, B), QMAX * B), :] = h.astype(BF)
        return 0

    lax.fori_loop(0, OPS, one_operator, 0)


def second_product(shift_ref, place_ref, t0, t1, t2, t3, h_ref, mine_ref, other_ref, left_ref):
    z, core, y, x = place_ref[0], place_ref[1], place_ref[2], place_ref[3]
    for e, block in enumerate((t0, t1, t2, t3)):
        for d in range(4):
            row_y = (y - jnp.where(core == 0, e, d) + NY) % NY
            row_x = (x - jnp.where(core == 0, d, e) + NX) % NX
            q = row_y * NX + row_x
            to_z, to_core = q // 4, (q // 2) % 2
            ahead = jnp.where(to_core == 0, to_z - z + NZ, z - to_z + NZ) % NZ
            start = jnp.where(to_core == core, 0, B // 2) + ahead * 32 + (q % 2) * 16
            start = pl.multiple_of(start, 16)
            for o in range(OPS):
                left_ref[pl.ds(start, 16), o * B:(o + 1) * B] = block[d, o]

    def four_targets(i, _):
        for u in range(4):
            t = i * 4 + u
            sources = [
                h_ref[o, pl.ds(pl.multiple_of((t + QMAX - shift_ref[o]) * B, B), B), :] for o in range(OPS)
            ]
            total = jnp.dot(left_ref[...], jnp.concatenate(sources, axis=0), preferred_element_type=F32)
            for k in range(NZ):
                mine_ref[k, t] = total[k * 32:(k + 1) * 32]
                other_ref[k, t] = total[B // 2 + k * 32:B // 2 + (k + 1) * 32].astype(BF)
        return 0

    lax.fori_loop(0, SECS // 4, four_targets, 0)


def on_device(psi, left_ops, right_ops, op_shift, sector_dims):
    p, q = lax.axis_index("op"), lax.axis_index("sec")
    core = p % NC
    place = jnp.stack([p // NC, core, q // NX, q % NX]).astype(jnp.int32)
    index = jnp.arange(B, dtype=jnp.int32)

    smem = pl.BlockSpec(memory_space=pltpu.SMEM)
    vmem = pl.BlockSpec(memory_space=pltpu.VMEM)

    def call(kernel, name, in_specs, out_shape, dots, scratch=(), aliases={}):
        return pl.pallas_call(
            kernel, in_specs=in_specs, out_shape=[jax.ShapeDtypeStruct(*o) for o in out_shape],
            out_specs=[vmem] * len(out_shape), name=name, scratch_shapes=scratch, input_output_aliases=aliases,
            compiler_params=pltpu.CompilerParams(vmem_limit_bytes=4 << 20),
            cost_estimate=pl.CostEstimate(flops=2 * dots * B ** 3, bytes_accessed=4 << 20, transcendentals=0))

    place, left_ops = lax.optimization_barrier((place, left_ops))
    firsts = [left_ops] + [move(left_ops, gather_first(d)) for d in (1, 3, 2)]
    masked, ends = call(
        mask_sectors, "mask_sectors", [smem, smem, vmem],
        [((SECS, B, B), BF), ((QMAX, B, B), BF)], 0,
    )(sector_dims, place, psi)
    ends, *_ = lax.optimization_barrier((ends, *firsts[1:]))
    edge_in = move(ends, edge_target)
    strips, = call(stack_strips, "stack_strips", [vmem] * 4, [((4, OPS, 16, B), BF)], 0)(
        firsts[0], firsts[1], firsts[3], firsts[2])
    seconds = [move(strips, gather_second(d)) for d in (1, 3, 2)]
    t0, t1, t3, t2 = strips, *seconds
    edge_in, _ = lax.optimization_barrier((edge_in, strips))
    edge_other = move(edge_in, other_core)

    masked, _ = lax.optimization_barrier((masked, edge_in))
    h, = call(
        own_sectors, "own_sectors", [vmem] * 2, [((OPS, HELD * B, B), BF)], OPS * SECS,
    )(masked, right_ops)
    h, = call(
        edge_sectors, "edge_sectors", [smem] + [vmem] * 4, [((OPS, HELD * B, B), BF)], 1, aliases={4: 0},
    )(place, edge_in, edge_other, right_ops, h)
    mine, other = call(
        second_product, "second_product", [smem, smem] + [vmem] * 5,
        [((NZ, SECS, 32, B), F32), ((NZ, SECS, 32, B), BF)], OPS * SECS, [pltpu.VMEM((B, OPS * B), BF)],
    )(op_shift, place, t0, t1, t2, t3, h)

    total = mine + move(other, other_core).astype(F32)
    far = move(total[2].astype(BF), along_z(1))
    back = move(total[3].astype(BF), along_z(-1))
    near = move((total[1] + far.astype(F32)).astype(BF), along_z(1))
    summed = total[0] + back.astype(F32) + near.astype(F32)
    live = index[None, :] < sector_dims[:, None]
    mine_rows = p * 32 + jnp.arange(32, dtype=jnp.int32)
    live_rows = mine_rows[None, :] < sector_dims[:, None]
    return jnp.where(live_rows[:, :, None] & live[:, None, :], summed, 0.0).astype(BF)


def solution(mesh):
    placed = (P("sec", None, None), P("op", "sec", None), P("op", None, None), P("op"), P("sec"))
    return jax.shard_map(
        on_device, mesh=mesh, in_specs=placed, out_specs=P("sec", "op", None), check_vma=False
    )
```

time: 101 us -> 62.3 us (0.62)
  the two profiles are of different devices: /device:TPU:0 before, /device:TPU:16 now
where the time goes in v2:
time: 62.3 us; the launch traced here: 62.1 us
  waiting for transfers between devices  24 us (39%)
  starting transfers between devices  17.3 us (28%)
  Pallas kernels  16.7 us (27%)
  local copies, waits for them, and re-layouts  2.3 us (4%)
  other arithmetic  1.6 us (3%)
    ppermute x12, waiting for transfers between devices, move(): return lax.ppermute(block, ('op', 'sec'), route)  24 us
    ppermute x12, starting transfers between devices, move(): return lax.ppermute(block, ('op', 'sec'), route)  17.3 us
    pallas_call x1, Pallas kernels, on_device(): call(second_product, 'second_product', [smem, smem] + [vmem] * 5, [((NZ,...  6.13 us
    pallas_call x1, Pallas kernels, on_device(): call(own_sectors, 'own_sectors', [vmem] * 2, [((OPS, HELD * B, B), BF)],...  5.99 us
    pallas_call x1, Pallas kernels, on_device(): call(edge_sectors, 'edge_sectors', [smem] + [vmem] * 4, [((OPS, HELD * B,...  3.37 us
    unnamed x12, local copies, waits for them, and re-layouts  2.27 us
  transfers between devices with their start and end apart: 12, of which 4 were waited for; matrix products, arithmetic and copies ran while one was open for 0% of the time, Pallas kernels for 17%

profile of v2, /device:TPU:16, one launch (start us, length us, event | category | flops | bytes accessed | tf_op | source)
XLA Modules:
  0.0 62.1 jit_solution(680981542601475996)
XLA Ops:
  0.0 0.1 pad_add_fusion.place_ref
  0.1 1.5 %collective-permute-start = (bf16[8,16,256]{2,1,0:T(8,128)(2,1)}, bf16[8,16,256]{2,1,0:T(8,128)(2,1)S(1)}, u32[]{:S(2)}, u32[]{:S(2)}) collective-permute-start(bf16[8,16,256]{2,1,0:T(8,128)(2,1)} %s0), channel_id=1, source_target_pairs={{0,1},{1,2},{2,3},{3,0},{4,5},{5,6},{6,7},{7,4},{8,9},{9,10},{10,1... | collective-permute-start | bytes 196616 | tf_op jit(solution)/shard_map/ppermute | solution.py:31
  1.6 2.7 %collective-permute-start.1 = (bf16[8,16,256]{2,1,0:T(8,128)(2,1)}, bf16[8,16,256]{2,1,0:T(8,128)(2,1)S(1)}, u32[]{:S(2)}, u32[]{:S(2)}) collective-permute-start(bf16[8,16,256]{2,1,0:T(8,128)(2,1)} %s0), channel_id=1, source_target_pairs={{0,2},{1,3},{2,0},{3,1},{4,6},{5,7},{6,4},{7,5},{8,10},{9,11},{10,... | collective-permute-start | bytes 196616 | tf_op jit(solution)/shard_map/ppermute | solution.py:31
  4.3 1.4 %collective-permute-start.2 = (bf16[8,16,256]{2,1,0:T(8,128)(2,1)}, bf16[8,16,256]{2,1,0:T(8,128)(2,1)S(1)}, u32[]{:S(2)}, u32[]{:S(2)}) collective-permute-start(bf16[8,16,256]{2,1,0:T(8,128)(2,1)} %s0), channel_id=1, source_target_pairs={{0,3},{1,0},{2,1},{3,2},{4,7},{5,4},{6,5},{7,6},{8,11},{9,8},{10,9... | collective-permute-start | bytes 196616 | tf_op jit(solution)/shard_map/ppermute | solution.py:31
  5.7 1.6 %copy-done.1 = bf16[16,256,256]{2,1,0:T(8,128)(2,1)S(1)} copy-done((bf16[16,256,256]{2,1,0:T(8,128)(2,1)S(1)}, bf16[16,256,256]{2,1,0:T(8,128)(2,1)}, u32[]{:S(2)}) %copy-start.1) | copy-done | bytes 2097176
  7.3 0.7 %copy-done.3 = s32[16]{0:T(128)S(1)} copy-done((s32[16]{0:T(128)S(1)}, s32[16]{0:T(128)}, u32[]{:S(2)}) %copy-start.3) | copy-done | bytes 88
  8.0 1.2 %mask_sectors.1 = (bf16[16,256,256]{2,1,0:T(8,128)(2,1)S(1)}, bf16[2,256,256]{2,1,0:T(8,128)(2,1)S(1)}) custom-call(s32[16]{0:T(128)S(1)} %copy-done.3, s32[4]{0:T(128)S(1)} %pad_add_fusion.place_ref, bf16[16,256,256]{2,1,0:T(8,128)(2,1)S(1)} %copy-done.1), custom_call_target="tpu_custom_call" | custom-call | bytes 4194304 | tf_op jit(solution)/shard_map/mask_sectors/pallas_call | solution.py:147
  9.2 0.0 collective-permute-done.1.s2
  9.2 0.0 collective-permute-done.2.s3
  9.2 2.5 %collective-permute-start.6 = (bf16[2,256,256]{2,1,0:T(8,128)(2,1)S(1)}, bf16[2,256,256]{2,1,0:T(8,128)(2,1)S(1)}, u32[]{:S(2)}, u32[]{:S(2)}) collective-permute-start(bf16[2,256,256]{2,1,0:T(8,128)(2,1)S(1)} %get-tuple-element.17), channel_id=1, source_target_pairs={{0,1},{1,2},{2,3},{3,4},{4,5},{5,6},{6,7},{7,8},{8,9},{9,10},{10,1... | collective-permute-start | bytes 786440 | tf_op jit(solution)/shard_map/ppermute | solution.py:31
  11.8 1.4 %collective-permute-start.3 = (bf16[4,8,16,256]{3,2,1,0:T(8,128)(2,1)S(1)}, bf16[4,8,16,256]{3,2,1,0:T(8,128)(2,1)S(1)}, u32[]{:S(2)}, u32[]{:S(2)}) collective-permute-start(bf16[4,8,16,256]{3,2,1,0:T(8,128)(2,1)S(1)} %stack_strips.1.t0), channel_id=1, source_target_pairs={{0,4},{1,5},{2,6},{3,7},{4,8},{5,9},{6,10},{7,11},{8,12},{9,13},{1... | collective-permute-start | bytes 786440 | tf_op jit(solution)/shard_map/ppermute | solution.py:31
  13.1 0.6 %collective-permute-start.4 = (bf16[4,8,16,256]{3,2,1,0:T(8,128)(2,1)S(1)}, bf16[4,8,16,256]{3,2,1,0:T(8,128)(2,1)S(1)}, u32[]{:S(2)}, u32[]{:S(2)}) collective-permute-start(bf16[4,8,16,256]{3,2,1,0:T(8,128)(2,1)S(1)} %stack_strips.1.t0), channel_id=1, source_target_pairs={{0,8},{1,9},{2,10},{3,11},{4,12},{5,13},{6,14},{7,15},{8,0},{9,1},... | collective-permute-start | bytes 786440 | tf_op jit(solution)/shard_map/ppermute | solution.py:31
  13.7 1.1 %collective-permute-start.5 = (bf16[4,8,16,256]{3,2,1,0:T(8,128)(2,1)S(1)}, bf16[4,8,16,256]{3,2,1,0:T(8,128)(2,1)S(1)}, u32[]{:S(2)}, u32[]{:S(2)}) collective-permute-start(bf16[4,8,16,256]{3,2,1,0:T(8,128)(2,1)S(1)} %stack_strips.1.t0), channel_id=1, source_target_pairs={{0,12},{1,13},{2,14},{3,15},{4,0},{5,1},{6,2},{7,3},{8,4},{9,5},{1... | collective-permute-start | bytes 786440 | tf_op jit(solution)/shard_map/ppermute | solution.py:31
  14.8 10.2 %collective-permute-done.6.edge_in = bf16[2,256,256]{2,1,0:T(8,128)(2,1)S(1)} collective-permute-done((bf16[2,256,256]{2,1,0:T(8,128)(2,1)S(1)}, bf16[2,256,256]{2,1,0:T(8,128)(2,1)S(1)}, u32[]{:S(2)}, u32[]{:S(2)}) %collective-permute-start.6) | collective-permute-done | bytes 262176 | tf_op jit(solution)/shard_map/ppermute | solution.py:31
  25.0 0.0 collective-permute-start.7
  25.0 6.0 %own_sectors.1._ = bf16[8,5120,256]{2,1,0:T(8,128)(2,1)S(1)} custom-call(bf16[16,256,256]{2,1,0:T(8,128)(2,1)S(1)} %get-tuple-element.20.masked_ref, bf16[8,256,256]{2,1,0:T(8,128)(2,1)S(1)} %copy-done), custom_call_target="tpu_custom_call" | custom-call | flops 4294967296 | bytes 4194304 | tf_op jit(solution)/shard_map/own_sectors/pallas_call | solution.py:161
  31.0 0.0 copy-start.5
  31.0 3.4 %edge_sectors.1.h_ref = bf16[8,5120,256]{2,1,0:T(8,128)(2,1)S(1)} custom-call(s32[4]{0:T(128)S(1)} %pad_add_fusion.place_ref, bf16[2,256,256]{2,1,0:T(8,128)(2,1)S(1)} %collective-permute-done.6.edge_in, bf16[2,256,256]{2,1,0:T(8,128)(2,1)S(1)} %collective-permute-done.7.edge_other, ...), custom_call_target="tpu_custom_call", output_to_operand_aliasing={{}: (4, {})} | custom-call | flops 33554432 | bytes 4194304 | tf_op jit(solution)/shard_map/edge_sectors/pallas_call | solution.py:164
  34.4 6.1 %second_product.1 = (f32[4,16,32,256]{3,2,1,0:T(8,128)S(1)}, bf16[4,16,32,256]{3,2,1,0:T(8,128)(2,1)S(1)}) custom-call(s32[8]{0:T(128)S(1)} %copy-done.5, s32[4]{0:T(128)S(1)} %pad_add_fusion.place_ref, bf16[4,8,16,256]{3,2,1,0:T(8,128)(2,1)S(1)} %stack_strips.1.t0, bf16[4,8,16,256]{3,2,1,0:T(8,128)(2,1)S(1)} %collective-permute-done.3.t1, ...), custom_call_target="tpu_custom_call" | custom-call | flops 4294967296 | bytes 4194304 | tf_op jit(solution)/shard_map/second_product/pallas_call | solution.py:167
  40.6 0.6 collective-permute-start.8
  41.1 2.3 %collective-permute-done.8 = bf16[4,16,32,256]{3,2,1,0:T(8,128)(2,1)S(1)} collective-permute-done((bf16[4,16,32,256]{3,2,1,0:T(8,128)(2,1)S(1)}, bf16[4,16,32,256]{3,2,1,0:T(8,128)(2,1)S(1)}, u32[]{:S(2)}, u32[]{:S(2)}) %collective-permute-start.8) | collective-permute-done | bytes 1048608 | tf_op jit(solution)/shard_map/ppermute | solution.py:31
  43.4 0.4 fusion.6
  43.9 0.0 copy-start.4
  43.9 1.9 %collective-permute-start.10 = (bf16[16,32,256]{2,1,0:T(8,128)(2,1)S(1)}, bf16[16,32,256]{2,1,0:T(8,128)(2,1)S(1)}, u32[]{:S(2)}, u32[]{:S(2)}) collective-permute-start(bf16[16,32,256]{2,1,0:T(8,128)(2,1)S(1)} %get-tuple-element.26), channel_id=1, source_target_pairs={{0,32},{1,33},{2,34},{3,35},{4,36},{5,37},{6,38},{7,39},{8,40},{9,... | collective-permute-start | bytes 786440 | tf_op jit(solution)/shard_map/ppermute | solution.py:31
  45.8 2.3 %collective-permute-start.9 = (bf16[16,32,256]{2,1,0:T(8,128)(2,1)S(1)}, bf16[16,32,256]{2,1,0:T(8,128)(2,1)S(1)}, u32[]{:S(2)}, u32[]{:S(2)}) collective-permute-start(bf16[16,32,256]{2,1,0:T(8,128)(2,1)S(1)} %get-tuple-element.25), channel_id=1, source_target_pairs={{0,96},{1,97},{2,98},{3,99},{4,100},{5,101},{6,102},{7,103},{8,104... | collective-permute-start | bytes 786440 | tf_op jit(solution)/shard_map/ppermute | solution.py:31
  48.1 4.6 %collective-permute-done.10 = bf16[16,32,256]{2,1,0:T(8,128)(2,1)S(1)} collective-permute-done((bf16[16,32,256]{2,1,0:T(8,128)(2,1)S(1)}, bf16[16,32,256]{2,1,0:T(8,128)(2,1)S(1)}, u32[]{:S(2)}, u32[]{:S(2)}) %collective-permute-start.10) | collective-permute-done | bytes 262176 | tf_op jit(solution)/shard_map/ppermute | solution.py:31
  52.8 0.1 fusion.1
  52.8 1.3 %collective-permute-start.11 = (bf16[16,32,256]{2,1,0:T(8,128)(2,1)S(1)}, bf16[16,32,256]{2,1,0:T(8,128)(2,1)S(1)}, u32[]{:S(2)}, u32[]{:S(2)}) collective-permute-start(bf16[16,32,256]{2,1,0:T(8,128)(2,1)S(1)} %fusion.1), channel_id=1, source_target_pairs={{0,32},{1,33},{2,34},{3,35},{4,36},{5,37},{6,38},{7,39},{8,40},{9,... | collective-permute-start | bytes 786440 | tf_op jit(solution)/shard_map/ppermute | solution.py:31
  54.2 0.1 broadcast_compare_fusion
  54.3 0.1 iota_compare_fusion
  54.3 6.9 %collective-permute-done.11 = bf16[16,32,256]{2,1,0:T(8,128)(2,1)S(1)} collective-permute-done((bf16[16,32,256]{2,1,0:T(8,128)(2,1)S(1)}, bf16[16,32,256]{2,1,0:T(8,128)(2,1)S(1)}, u32[]{:S(2)}, u32[]{:S(2)}) %collective-permute-start.11) | collective-permute-done | bytes 262176 | tf_op jit(solution)/shard_map/ppermute | solution.py:31
  61.3 0.9 %fusion.5 = bf16[16,32,256]{2,1,0:T(8,128)(2,1)} fusion(f32[4,16,32,256]{3,2,1,0:T(8,128)S(1)} %get-tuple-element.24, bf16[16,32,256]{2,1,0:T(8,128)(2,1)S(1)} %collective-permute-done.11, bf16[16,32,256]{2,1,0:T(8,128)(2,1)S(1)} %collective-permute-done.9, pred[16,256]{1,0:T(8,128)(4,1)S(1)} %iota_compare_fusion, pred[16,32]{1,0:T(8,128)(4,1)S(1)} %broadcast_compare_fusion), kind=kLoop, calls=%fused_computation.8 | loop fusion | flops 917504 | bytes 1315328 | tf_op jit(solution)/shard_map/convert_element_type | solution.py:180
  (17 shorter events, 0.1 us)
Async XLA Ops:
  0.0 25.0 %copy-start = (bf16[8,256,256]{2,1,0:T(8,128)(2,1)S(1)}, bf16[8,256,256]{2,1,0:T(8,128)(2,1)}, u32[]{:S(2)}) copy-start(bf16[8,256,256]{2,1,0:T(8,128)(2,1)} %right_ref.3) | copy-start | bytes 3145732
  0.1 9.1 %collective-permute-start = (bf16[8,16,256]{2,1,0:T(8,128)(2,1)}, bf16[8,16,256]{2,1,0:T(8,128)(2,1)S(1)}, u32[]{:S(2)}, u32[]{:S(2)}) collective-permute-start(bf16[8,16,256]{2,1,0:T(8,128)(2,1)} %s0), channel_id=1, source_target_pairs={{0,1},{1,2},{2,3},{3,0},{4,5},{5,6},{6,7},{7,4},{8,9},{9,10},{10,1... | collective-permute-start | bytes 196616 | tf_op jit(solution)/shard_map/ppermute | solution.py:31
  1.6 7.6 %collective-permute-start.1 = (bf16[8,16,256]{2,1,0:T(8,128)(2,1)}, bf16[8,16,256]{2,1,0:T(8,128)(2,1)S(1)}, u32[]{:S(2)}, u32[]{:S(2)}) collective-permute-start(bf16[8,16,256]{2,1,0:T(8,128)(2,1)} %s0), channel_id=1, source_target_pairs={{0,2},{1,3},{2,0},{3,1},{4,6},{5,7},{6,4},{7,5},{8,10},{9,11},{10,... | collective-permute-start | bytes 196616 | tf_op jit(solution)/shard_map/ppermute | solution.py:31
  4.3 4.9 %collective-permute-start.2 = (bf16[8,16,256]{2,1,0:T(8,128)(2,1)}, bf16[8,16,256]{2,1,0:T(8,128)(2,1)S(1)}, u32[]{:S(2)}, u32[]{:S(2)}) collective-permute-start(bf16[8,16,256]{2,1,0:T(8,128)(2,1)} %s0), channel_id=1, source_target_pairs={{0,3},{1,0},{2,1},{3,2},{4,7},{5,4},{6,5},{7,6},{8,11},{9,8},{10,9... | collective-permute-start | bytes 196616 | tf_op jit(solution)/shard_map/ppermute | solution.py:31
  5.7 1.6 %copy-start.1 = (bf16[16,256,256]{2,1,0:T(8,128)(2,1)S(1)}, bf16[16,256,256]{2,1,0:T(8,128)(2,1)}, u32[]{:S(2)}) copy-start(bf16[16,256,256]{2,1,0:T(8,128)(2,1)} %psi_ref.1) | copy-start | bytes 6291460
  7.3 0.7 %copy-start.3 = (s32[16]{0:T(128)S(1)}, s32[16]{0:T(128)}, u32[]{:S(2)}) copy-start(s32[16]{0:T(128)} %dims_ref.1) | copy-start | bytes 196
  8.0 3.7 %copy-start.2 = (bf16[8,16,256]{2,1,0:T(8,128)(2,1)S(1)}, bf16[8,16,256]{2,1,0:T(8,128)(2,1)}, u32[]{:S(2)}) copy-start(bf16[8,16,256]{2,1,0:T(8,128)(2,1)} %s0) | copy-start | bytes 196612
  9.2 15.8 %collective-permute-start.6 = (bf16[2,256,256]{2,1,0:T(8,128)(2,1)S(1)}, bf16[2,256,256]{2,1,0:T(8,128)(2,1)S(1)}, u32[]{:S(2)}, u32[]{:S(2)}) collective-permute-start(bf16[2,256,256]{2,1,0:T(8,128)(2,1)S(1)} %get-tuple-element.17), channel_id=1, source_target_pairs={{0,1},{1,2},{2,3},{3,4},{4,5},{5,6},{6,7},{7,8},{8,9},{9,10},{10,1... | collective-permute-start | bytes 786440 | tf_op jit(solution)/shard_map/ppermute | solution.py:31
  11.8 22.6 %collective-permute-start.3 = (bf16[4,8,16,256]{3,2,1,0:T(8,128)(2,1)S(1)}, bf16[4,8,16,256]{3,2,1,0:T(8,128)(2,1)S(1)}, u32[]{:S(2)}, u32[]{:S(2)}) collective-permute-start(bf16[4,8,16,256]{3,2,1,0:T(8,128)(2,1)S(1)} %stack_strips.1.t0), channel_id=1, source_target_pairs={{0,4},{1,5},{2,6},{3,7},{4,8},{5,9},{6,10},{7,11},{8,12},{9,13},{1... | collective-permute-start | bytes 786440 | tf_op jit(solution)/shard_map/ppermute | solution.py:31
  13.1 21.3 %collective-permute-start.4 = (bf16[4,8,16,256]{3,2,1,0:T(8,128)(2,1)S(1)}, bf16[4,8,16,256]{3,2,1,0:T(8,128)(2,1)S(1)}, u32[]{:S(2)}, u32[]{:S(2)}) collective-permute-start(bf16[4,8,16,256]{3,2,1,0:T(8,128)(2,1)S(1)} %stack_strips.1.t0), channel_id=1, source_target_pairs={{0,8},{1,9},{2,10},{3,11},{4,12},{5,13},{6,14},{7,15},{8,0},{9,1},... | collective-permute-start | bytes 786440 | tf_op jit(solution)/shard_map/ppermute | solution.py:31
  13.7 20.7 %collective-permute-start.5 = (bf16[4,8,16,256]{3,2,1,0:T(8,128)(2,1)S(1)}, bf16[4,8,16,256]{3,2,1,0:T(8,128)(2,1)S(1)}, u32[]{:S(2)}, u32[]{:S(2)}) collective-permute-start(bf16[4,8,16,256]{3,2,1,0:T(8,128)(2,1)S(1)} %stack_strips.1.t0), channel_id=1, source_target_pairs={{0,12},{1,13},{2,14},{3,15},{4,0},{5,1},{6,2},{7,3},{8,4},{9,5},{1... | collective-permute-start | bytes 786440 | tf_op jit(solution)/shard_map/ppermute | solution.py:31
  25.0 6.0 %collective-permute-start.7 = (bf16[2,256,256]{2,1,0:T(8,128)(2,1)S(1)}, bf16[2,256,256]{2,1,0:T(8,128)(2,1)S(1)}, u32[]{:S(2)}, u32[]{:S(2)}) collective-permute-start(bf16[2,256,256]{2,1,0:T(8,128)(2,1)S(1)} %collective-permute-done.6.edge_in), channel_id=1, source_target_pairs={{0,16},{1,17},{2,18},{3,19},{4,20},{5,21},{6,22},{7,23},{8,24},{9,... | collective-permute-start | bytes 786440 | tf_op jit(solution)/shard_map/ppermute | solution.py:31
  31.0 3.4 %copy-start.5 = (s32[8]{0:T(128)S(1)}, s32[8]{0:T(128)}, u32[]{:S(2)}) copy-start(s32[8]{0:T(128)} %shift_ref.1) | copy-start | bytes 100
  40.6 2.9 %collective-permute-start.8 = (bf16[4,16,32,256]{3,2,1,0:T(8,128)(2,1)S(1)}, bf16[4,16,32,256]{3,2,1,0:T(8,128)(2,1)S(1)}, u32[]{:S(2)}, u32[]{:S(2)}) collective-permute-start(bf16[4,16,32,256]{3,2,1,0:T(8,128)(2,1)S(1)} %get-tuple-element.22), channel_id=1, source_target_pairs={{0,16},{1,17},{2,18},{3,19},{4,20},{5,21},{6,22},{7,23},{8,24},{9,... | collective-permute-start | bytes 3145736 | tf_op jit(solution)/shard_map/ppermute | solution.py:31
  43.9 10.3 %copy-start.4 = (s32[16]{0:T(128)S(1)}, s32[16]{0:T(128)}, u32[]{:S(2)}) copy-start(s32[16]{0:T(128)} %dims_ref.1) | copy-start | bytes 196
  43.9 8.8 %collective-permute-start.10 = (bf16[16,32,256]{2,1,0:T(8,128)(2,1)S(1)}, bf16[16,32,256]{2,1,0:T(8,128)(2,1)S(1)}, u32[]{:S(2)}, u32[]{:S(2)}) collective-permute-start(bf16[16,32,256]{2,1,0:T(8,128)(2,1)S(1)} %get-tuple-element.26), channel_id=1, source_target_pairs={{0,32},{1,33},{2,34},{3,35},{4,36},{5,37},{6,38},{7,39},{8,40},{9,... | collective-permute-start | bytes 786440 | tf_op jit(solution)/shard_map/ppermute | solution.py:31
  45.8 8.5 %collective-permute-start.9 = (bf16[16,32,256]{2,1,0:T(8,128)(2,1)S(1)}, bf16[16,32,256]{2,1,0:T(8,128)(2,1)S(1)}, u32[]{:S(2)}, u32[]{:S(2)}) collective-permute-start(bf16[16,32,256]{2,1,0:T(8,128)(2,1)S(1)} %get-tuple-element.25), channel_id=1, source_target_pairs={{0,96},{1,97},{2,98},{3,99},{4,100},{5,101},{6,102},{7,103},{8,104... | collective-permute-start | bytes 786440 | tf_op jit(solution)/shard_map/ppermute | solution.py:31
  52.8 8.4 %collective-permute-start.11 = (bf16[16,32,256]{2,1,0:T(8,128)(2,1)S(1)}, bf16[16,32,256]{2,1,0:T(8,128)(2,1)S(1)}, u32[]{:S(2)}, u32[]{:S(2)}) collective-permute-start(bf16[16,32,256]{2,1,0:T(8,128)(2,1)S(1)} %fusion.1), channel_id=1, source_target_pairs={{0,32},{1,33},{2,34},{3,35},{4,36},{5,37},{6,38},{7,39},{8,40},{9,... | collective-permute-start | bytes 786440 | tf_op jit(solution)/shard_map/ppermute | solution.py:31

commit v3 on v2

--- a/solution.py
+++ b/solution.py
@@ -11,6 +11,7 @@
 SECS = 16
 QMAX = 2
 HELD = SECS + 2 * QMAX
+STRIP = OPS * 16
 BF = jnp.bfloat16
 F32 = jnp.float32
 
@@ -32,16 +33,21 @@
 
 
 def gather_first(d):
-    return lambda z, c, y, x: (z, c, y, (x + d) % NX) if c == 0 else (z, c, (y + d) % NY, x)
+    def target(z, c, y, x):
+        if c == 0:
+            q = (y * NX + x + d) % SECS
+            return (z, c, q // NX, q % NX)
+        return (z, c, (y + d) % NY, x)
+
+    return target
 
 
 def gather_second(d):
     return lambda z, c, y, x: (z, c, (y + d) % NY, x) if c == 0 else (z, c, y, (x + d) % NX)
 
 
-def edge_target(z, c, y, x):
-    q = y * NX + x + (1 if c == 0 else -1)
-    return (z, c, q // NX, q % NX) if 0 <= q < NX * NY else None
+def to_core_1(z, c, y, x):
+    return (z, 1, y, x) if c == 0 else None
 
 
 def other_core(z, c, y, x):
@@ -52,58 +58,87 @@
     return lambda z, c, y, x: ((z + (sign if c == 0 else -sign)) % NZ, c, y, x)
 
 
-def mask_sectors(dims_ref, place_ref, psi_ref, masked_ref, ends_ref):
+def masked(block, d):
     rows = lax.broadcasted_iota(jnp.int32, (B, B), 0)
     cols = lax.broadcasted_iota(jnp.int32, (B, B), 1)
-
+    return jnp.where((rows < d) & (cols < d), block.astype(F32), 0.0).astype(BF)
+
+
+def pack(dims_ref, first_psi, last_psi, left_ref, up_ref, down_ref):
+    strip = left_ref[...].reshape(STRIP, B)
+    up_ref[:STRIP, :] = strip
+    down_ref[:STRIP, :] = strip
+    for e in range(QMAX):
+        to = slice(STRIP + e * B, STRIP + (e + 1) * B)
+        up_ref[to, :] = masked(last_psi[e], dims_ref[SECS - QMAX + e])
+        down_ref[to, :] = masked(first_psi[e], dims_ref[e])
+
+
+def mask_sectors(dims_ref, psi_ref, masked_ref):
     def mask_one(s, _):
-        d = dims_ref[s]
-        keep = (rows < d) & (cols < d)
-        masked_ref[s] = jnp.where(keep, psi_ref[s].astype(F32), 0.0).astype(BF)
+        masked_ref[s] = masked(psi_ref[s], dims_ref[s])
         return 0
 
     lax.fori_loop(0, SECS, mask_one, 0)
-    start = (1 - place_ref[1]) * (SECS - QMAX)
-    for e in range(QMAX):
-        ends_ref[e] = masked_ref[start + e]
-
-
-def stack_strips(s0, s1, s2, s3, out_ref):
-    for d, strip in enumerate((s0, s1, s2, s3)):
-        out_ref[d] = strip[...]
+
+
+def unpack(place_ref, own, from_below, from_above, second_below, strips_ref, edges_ref):
+    strips_ref[0] = own[...]
+    strips_ref[1] = from_below[:STRIP, :].reshape(OPS, 16, B)
+    strips_ref[2] = from_above[:STRIP, :].reshape(OPS, 16, B)
+    strips_ref[3] = second_below[...]
+    q = place_ref[2] * NX + place_ref[3]
+    for k, (source, present) in enumerate(((from_below, q > 0), (from_above, q < SECS - 1))):
+        keep = jnp.broadcast_to(present.astype(jnp.int32), (QMAX * B, B)) > 0
+        edges_ref[k * QMAX * B:(k + 1) * QMAX * B, :] = jnp.where(keep, source[STRIP:, :].astype(F32), 0.0).astype(BF)
+
+
+def by_twos(one):
+    def two_operators(i, _):
+        one(2 * i)
+        one(2 * i + 1)
+        return 0
+
+    lax.fori_loop(0, OPS // 2, two_operators, 0)
 
 
 def own_sectors(masked_ref, right_ref, h_ref):
-    def one_operator(o, _):
+    def one_operator(o):
         right_t = right_ref[o].T
         for s in range(0, SECS, 4):
             h = jnp.dot(masked_ref[s:s + 4].reshape(4 * B, B), right_t, preferred_element_type=F32)
             h_ref[o, (s + QMAX) * B:(s + QMAX + 4) * B, :] = h.astype(BF)
-        return 0
-
-    lax.fori_loop(0, OPS, one_operator, 0)
-
-
-def edge_sectors(place_ref, edge_in, edge_other, right_ref, _, h_ref):
-    below = place_ref[1] * (SECS + QMAX) * B
-
-    def one_operator(o, _):
-        right_t = right_ref[o].T
-        for edge, start in ((edge_in, below), (edge_other, (SECS + QMAX) * B - below)):
-            h = jnp.dot(edge[...].reshape(QMAX * B, B), right_t, preferred_element_type=F32)
-            h_ref[o, pl.ds(pl.multiple_of(start, B), QMAX * B), :] = h.astype(BF)
-        return 0
-
-    lax.fori_loop(0, OPS, one_operator, 0)
+
+    by_twos(one_operator)
+
+
+def edge_sectors(place_ref, edge_own, edge_other, right_ref, _, h_ref, edge_ref):
+    core = place_ref[1]
+
+    @pl.when(core == 0)
+    def _():
+        edge_ref[...] = edge_own[...]
+
+    @pl.when(core == 1)
+    def _():
+        edge_ref[...] = edge_other[...]
+
+    def one_operator(o):
+        h = jnp.dot(edge_ref[...], right_ref[o].T, preferred_element_type=F32).astype(BF)
+        h_ref[o, :QMAX * B, :] = h[:QMAX * B]
+        h_ref[o, (SECS + QMAX) * B:, :] = h[QMAX * B:]
+
+    by_twos(one_operator)
 
 
 def second_product(shift_ref, place_ref, t0, t1, t2, t3, h_ref, mine_ref, other_ref, left_ref):
     z, core, y, x = place_ref[0], place_ref[1], place_ref[2], place_ref[3]
     for e, block in enumerate((t0, t1, t2, t3)):
         for d in range(4):
-            row_y = (y - jnp.where(core == 0, e, d) + NY) % NY
-            row_x = (x - jnp.where(core == 0, d, e) + NX) % NX
-            q = row_y * NX + row_x
+            step = (0, -1, 1, -2)[d]
+            along_ring = (y * NX + x + step - e * NX + 2 * SECS) % SECS
+            along_y = (y + step + NY) % NY * NX + (x - e + NX) % NX
+            q = jnp.where(core == 0, along_ring, along_y)
             to_z, to_core = q // 4, (q // 2) % 2
             ahead = jnp.where(to_core == 0, to_z - z + NZ, z - to_z + NZ) % NZ
             start = jnp.where(to_core == core, 0, B // 2) + ahead * 32 + (q % 2) * 16
@@ -142,28 +177,37 @@
             compiler_params=pltpu.CompilerParams(vmem_limit_bytes=4 << 20),
             cost_estimate=pl.CostEstimate(flops=2 * dots * B ** 3, bytes_accessed=4 << 20, transcendentals=0))
 
-    place, left_ops = lax.optimization_barrier((place, left_ops))
-    firsts = [left_ops] + [move(left_ops, gather_first(d)) for d in (1, 3, 2)]
-    masked, ends = call(
-        mask_sectors, "mask_sectors", [smem, smem, vmem],
-        [((SECS, B, B), BF), ((QMAX, B, B), BF)], 0,
-    )(sector_dims, place, psi)
-    ends, *_ = lax.optimization_barrier((ends, *firsts[1:]))
-    edge_in = move(ends, edge_target)
-    strips, = call(stack_strips, "stack_strips", [vmem] * 4, [((4, OPS, 16, B), BF)], 0)(
-        firsts[0], firsts[1], firsts[3], firsts[2])
+    ends = pl.BlockSpec((QMAX, B, B), lambda i: (0, 0, 0)), pl.BlockSpec((QMAX, B, B), lambda i: (SECS // QMAX - 1, 0, 0))
+    packed = jax.ShapeDtypeStruct((STRIP + QMAX * B, B), BF)
+    whole = pl.BlockSpec((STRIP + QMAX * B, B), lambda i: (0, 0))
+    psi_there = pltpu.with_memory_space_constraint(psi, pltpu.HBM)
+    up, down = pl.pallas_call(
+        pack, grid=(1,), in_specs=[smem, *ends, pl.BlockSpec((OPS, 16, B), lambda i: (0, 0, 0))],
+        out_shape=[packed, packed], out_specs=[whole, whole], name="pack",
+        compiler_params=pltpu.CompilerParams(vmem_limit_bytes=4 << 20),
+        cost_estimate=pl.CostEstimate(flops=0, bytes_accessed=1 << 20, transcendentals=0),
+    )(sector_dims, psi_there, psi_there, pltpu.with_memory_space_constraint(left_ops, pltpu.HBM))
+    place, left_ops, up = lax.optimization_barrier((place, left_ops, up))
+    up = move(up, gather_first(1))
+    down = move(down, gather_first(-1))
+    two = move(left_ops, gather_first(2))
+    live_psi, = call(mask_sectors, "mask_sectors", [smem, vmem], [((SECS, B, B), BF)], 0)(sector_dims, psi)
+    two, _ = lax.optimization_barrier((two, live_psi))
+    strips, edges = call(
+        unpack, "unpack", [smem] + [vmem] * 4, [((4, OPS, 16, B), BF), ((2 * QMAX * B, B), BF)], 0,
+    )(place, left_ops, up, down, two)
     seconds = [move(strips, gather_second(d)) for d in (1, 3, 2)]
     t0, t1, t3, t2 = strips, *seconds
-    edge_in, _ = lax.optimization_barrier((edge_in, strips))
-    edge_other = move(edge_in, other_core)
-
-    masked, _ = lax.optimization_barrier((masked, edge_in))
+    edges_other = move(edges, to_core_1)
+
+    live_psi, _ = lax.optimization_barrier((live_psi, edges))
     h, = call(
         own_sectors, "own_sectors", [vmem] * 2, [((OPS, HELD * B, B), BF)], OPS * SECS,
-    )(masked, right_ops)
+    )(live_psi, right_ops)
     h, = call(
-        edge_sectors, "edge_sectors", [smem] + [vmem] * 4, [((OPS, HELD * B, B), BF)], 1, aliases={4: 0},
-    )(place, edge_in, edge_other, right_ops, h)
+        edge_sectors, "edge_sectors", [smem] + [vmem] * 4, [((OPS, HELD * B, B), BF)], 1,
+        [pltpu.VMEM((2 * QMAX * B, B), BF)], {4: 0},
+    )(place, edges, edges_other, right_ops, h)
     mine, other = call(
         second_product, "second_product", [smem, smem] + [vmem] * 5,
         [((NZ, SECS, 32, B), F32), ((NZ, SECS, 32, B), BF)], OPS * SECS, [pltpu.VMEM((B, OPS * B), BF)],

time: 62.3 us -> 56.5 us (0.907)
  the two profiles are of different devices: /device:TPU:16 before, /device:TPU:0 now
where the time goes in v3:
time: 56.5 us; the launch traced here: 56.4 us
  waiting for transfers between devices  21.2 us (38%)
  Pallas kernels  17 us (30%)
  starting transfers between devices  15.7 us (28%)
  other arithmetic  1.61 us (3%)
  local copies, waits for them, and re-layouts  0.71 us (1%)
    ppermute x11, waiting for transfers between devices, move(): return lax.ppermute(block, ('op', 'sec'), route)  21.2 us
    ppermute x11, starting transfers between devices, move(): return lax.ppermute(block, ('op', 'sec'), route)  15.7 us
    pallas_call x1, Pallas kernels, on_device(): call(second_product, 'second_product', [smem, smem] + [vmem] * 5, [((NZ,...  6.16 us
    pallas_call x1, Pallas kernels, on_device(): call(own_sectors, 'own_sectors', [vmem] * 2, [((OPS, HELD * B, B), BF)],...  5.17 us
    pallas_call x1, Pallas kernels, on_device(): call(edge_sectors, 'edge_sectors', [smem] + [vmem] * 4, [((OPS, HELD * B,...  2.47 us
    pallas_call x1, Pallas kernels, on_device(): pl.pallas_call(pack, grid=(1,), in_specs=[smem, *ends, pl.BlockSpec((OPS,...  1.33 us
    pallas_call x1, Pallas kernels, on_device(): call(mask_sectors, 'mask_sectors', [smem, vmem], [((SECS, B, B), BF)], 0)  1.21 us
  transfers between devices with their start and end apart: 11, of which 4 were waited for; matrix products, arithmetic and copies ran while one was open for 0% of the time, Pallas kernels for 16%

profile of v3, /device:TPU:0, one launch (start us, length us, event | category | flops | bytes accessed | tf_op | source)
XLA Modules:
  0.0 56.4 jit_solution(7224474413076980032)
XLA Ops:
  0.0 0.7 %copy-done.3 = s32[16]{0:T(128)S(1)} copy-done((s32[16]{0:T(128)S(1)}, s32[16]{0:T(128)}, u32[]{:S(2)}) %copy-start.3) | copy-done | bytes 88
  0.7 1.3 %pack.1 = (bf16[640,256]{1,0:T(8,128)(2,1)S(1)}, bf16[640,256]{1,0:T(8,128)(2,1)S(1)}) custom-call(s32[16]{0:T(128)S(1)} %copy-done.3, bf16[16,256,256]{2,1,0:T(8,128)(2,1)} %psi_ref.1, bf16[16,256,256]{2,1,0:T(8,128)(2,1)} %psi_ref.1, bf16[8,16,256]{2,1,0:T(8,128)(2,1)} %own), custom_call_target="tpu_custom_call" | custom-call | bytes 1048576 | tf_op jit(solution)/shard_map/pack/pallas_call | solution.py:184
  2.0 0.1 pad_add_fusion.place_ref
  2.1 1.6 %collective-permute-start = (bf16[640,256]{1,0:T(8,128)(2,1)S(1)}, bf16[640,256]{1,0:T(8,128)(2,1)S(1)}, u32[]{:S(2)}, u32[]{:S(2)}) collective-permute-start(bf16[640,256]{1,0:T(8,128)(2,1)S(1)} %get-tuple-element.19), channel_id=1, source_target_pairs={{0,1},{1,2},{2,3},{3,4},{4,5},{5,6},{6,7},{7,8},{8,9},{9,10},{10,1... | collective-permute-start | bytes 983048 | tf_op jit(solution)/shard_map/ppermute | solution.py:32
  3.7 3.8 %collective-permute-start.1 = (bf16[640,256]{1,0:T(8,128)(2,1)S(1)}, bf16[640,256]{1,0:T(8,128)(2,1)S(1)}, u32[]{:S(2)}, u32[]{:S(2)}) collective-permute-start(bf16[640,256]{1,0:T(8,128)(2,1)S(1)} %get-tuple-element.20), channel_id=1, source_target_pairs={{0,15},{1,0},{2,1},{3,2},{4,3},{5,4},{6,5},{7,6},{8,7},{9,8},{10,9... | collective-permute-start | bytes 983048 | tf_op jit(solution)/shard_map/ppermute | solution.py:32
  7.5 1.2 %mask_sectors.1.masked_ref = bf16[16,256,256]{2,1,0:T(8,128)(2,1)S(1)} custom-call(s32[16]{0:T(128)S(1)} %copy-done.4, bf16[16,256,256]{2,1,0:T(8,128)(2,1)S(1)} %copy-done), custom_call_target="tpu_custom_call" | custom-call | bytes 4194304 | tf_op jit(solution)/shard_map/mask_sectors/pallas_call | solution.py:194
  8.7 6.8 %collective-permute-done.2.second_below = bf16[8,16,256]{2,1,0:T(8,128)(2,1)S(1)} collective-permute-done((bf16[8,16,256]{2,1,0:T(8,128)(2,1)S(1)}, bf16[8,16,256]{2,1,0:T(8,128)(2,1)S(1)}, u32[]{:S(2)}, u32[]{:S(2)}) %collective-permute-start.2) | collective-permute-done | bytes 65568 | tf_op jit(solution)/shard_map/ppermute | solution.py:32
  15.5 0.0 collective-permute-done.1.from_above
  15.5 0.6 %unpack.1 = (bf16[4,8,16,256]{3,2,1,0:T(8,128)(2,1)S(1)}, bf16[1024,256]{1,0:T(8,128)(2,1)S(1)}) custom-call(s32[4]{0:T(128)S(1)} %pad_add_fusion.place_ref, bf16[8,16,256]{2,1,0:T(8,128)(2,1)S(1)} %copy-done.2, bf16[640,256]{1,0:T(8,128)(2,1)S(1)} %collective-permute-done.from_below, bf16[640,256]{1,0:T(8,128)(2,1)S(1)} %collective-permute-done.1.from_above, ...), custom_call_target="tpu_custom_call" | custom-call | bytes 4194304 | tf_op jit(solution)/shard_map/unpack/pallas_call | solution.py:196
  16.1 1.4 %collective-permute-start.6 = (bf16[1024,256]{1,0:T(8,128)(2,1)S(1)}, bf16[1024,256]{1,0:T(8,128)(2,1)S(1)}, u32[]{:S(2)}, u32[]{:S(2)}) collective-permute-start(bf16[1024,256]{1,0:T(8,128)(2,1)S(1)} %get-tuple-element.23.edge_own), channel_id=1, source_target_pairs={{0,16},{1,17},{2,18},{3,19},{4,20},{5,21},{6,22},{7,23},{8,24},{9,... | collective-permute-start | bytes 1572872 | tf_op jit(solution)/shard_map/ppermute | solution.py:32
  17.5 0.1 collective-permute-start.3
  17.6 2.0 %collective-permute-start.4 = (bf16[4,8,16,256]{3,2,1,0:T(8,128)(2,1)S(1)}, bf16[4,8,16,256]{3,2,1,0:T(8,128)(2,1)S(1)}, u32[]{:S(2)}, u32[]{:S(2)}) collective-permute-start(bf16[4,8,16,256]{3,2,1,0:T(8,128)(2,1)S(1)} %get-tuple-element.22.t0), channel_id=1, source_target_pairs={{0,8},{1,9},{2,10},{3,11},{4,12},{5,13},{6,14},{7,15},{8,0},{9,1},... | collective-permute-start | bytes 786440 | tf_op jit(solution)/shard_map/ppermute | solution.py:32
  19.6 1.8 %collective-permute-start.5 = (bf16[4,8,16,256]{3,2,1,0:T(8,128)(2,1)S(1)}, bf16[4,8,16,256]{3,2,1,0:T(8,128)(2,1)S(1)}, u32[]{:S(2)}, u32[]{:S(2)}) collective-permute-start(bf16[4,8,16,256]{3,2,1,0:T(8,128)(2,1)S(1)} %get-tuple-element.22.t0), channel_id=1, source_target_pairs={{0,12},{1,13},{2,14},{3,15},{4,0},{5,1},{6,2},{7,3},{8,4},{9,5},{1... | collective-permute-start | bytes 786440 | tf_op jit(solution)/shard_map/ppermute | solution.py:32
  21.3 5.2 %own_sectors.1._ = bf16[8,5120,256]{2,1,0:T(8,128)(2,1)S(1)} custom-call(bf16[16,256,256]{2,1,0:T(8,128)(2,1)S(1)} %mask_sectors.1.masked_ref, bf16[8,256,256]{2,1,0:T(8,128)(2,1)S(1)} %copy-done.1), custom_call_target="tpu_custom_call" | custom-call | flops 4294967296 | bytes 4194304 | tf_op jit(solution)/shard_map/own_sectors/pallas_call | solution.py:204
  26.5 0.0 copy-start.5
  26.5 0.0 collective-permute-done.6.edge_other
  26.5 2.5 %edge_sectors.1.h_ref = bf16[8,5120,256]{2,1,0:T(8,128)(2,1)S(1)} custom-call(s32[4]{0:T(128)S(1)} %pad_add_fusion.place_ref, bf16[1024,256]{1,0:T(8,128)(2,1)S(1)} %get-tuple-element.23.edge_own, bf16[1024,256]{1,0:T(8,128)(2,1)S(1)} %collective-permute-done.6.edge_other, bf16[8,256,256]{2,1,0:T(8,128)(2,1)S(1)} %copy-done.1, ...), custom_call_target="tpu_custom_call", output_to_operand_aliasing={{}: (4, {})} | custom-call | flops 33554432 | bytes 4194304 | tf_op jit(solution)/shard_map/edge_sectors/pallas_call | solution.py:207
  29.0 0.0 collective-permute-done.4.t2
  29.0 0.0 collective-permute-done.5.t3
  29.1 6.2 %second_product.1 = (f32[4,16,32,256]{3,2,1,0:T(8,128)S(1)}, bf16[4,16,32,256]{3,2,1,0:T(8,128)(2,1)S(1)}) custom-call(s32[8]{0:T(128)S(1)} %copy-done.5, s32[4]{0:T(128)S(1)} %pad_add_fusion.place_ref, bf16[4,8,16,256]{3,2,1,0:T(8,128)(2,1)S(1)} %get-tuple-element.22.t0, bf16[4,8,16,256]{3,2,1,0:T(8,128)(2,1)S(1)} %collective-permute-done.3.t1, ...), custom_call_target="tpu_custom_call" | custom-call | flops 4294967296 | bytes 4194304 | tf_op jit(solution)/shard_map/second_product/pallas_call | solution.py:211
  35.2 0.1 collective-permute-start.7
  35.3 2.6 %collective-permute-done.7 = bf16[4,16,32,256]{3,2,1,0:T(8,128)(2,1)S(1)} collective-permute-done((bf16[4,16,32,256]{3,2,1,0:T(8,128)(2,1)S(1)}, bf16[4,16,32,256]{3,2,1,0:T(8,128)(2,1)S(1)}, u32[]{:S(2)}, u32[]{:S(2)}) %collective-permute-start.7) | collective-permute-done | bytes 1048608 | tf_op jit(solution)/shard_map/ppermute | solution.py:32
  38.0 0.4 fusion.6
  38.4 2.0 %collective-permute-start.9 = (bf16[16,32,256]{2,1,0:T(8,128)(2,1)S(1)}, bf16[16,32,256]{2,1,0:T(8,128)(2,1)S(1)}, u32[]{:S(2)}, u32[]{:S(2)}) collective-permute-start(bf16[16,32,256]{2,1,0:T(8,128)(2,1)S(1)} %get-tuple-element.30), channel_id=1, source_target_pairs={{0,32},{1,33},{2,34},{3,35},{4,36},{5,37},{6,38},{7,39},{8,40},{9,... | collective-permute-start | bytes 786440 | tf_op jit(solution)/shard_map/ppermute | solution.py:32
  40.4 2.2 %collective-permute-start.8 = (bf16[16,32,256]{2,1,0:T(8,128)(2,1)S(1)}, bf16[16,32,256]{2,1,0:T(8,128)(2,1)S(1)}, u32[]{:S(2)}, u32[]{:S(2)}) collective-permute-start(bf16[16,32,256]{2,1,0:T(8,128)(2,1)S(1)} %get-tuple-element.29), channel_id=1, source_target_pairs={{0,96},{1,97},{2,98},{3,99},{4,100},{5,101},{6,102},{7,103},{8,104... | collective-permute-start | bytes 786440 | tf_op jit(solution)/shard_map/ppermute | solution.py:32
  42.7 4.9 %collective-permute-done.9 = bf16[16,32,256]{2,1,0:T(8,128)(2,1)S(1)} collective-permute-done((bf16[16,32,256]{2,1,0:T(8,128)(2,1)S(1)}, bf16[16,32,256]{2,1,0:T(8,128)(2,1)S(1)}, u32[]{:S(2)}, u32[]{:S(2)}) %collective-permute-start.9) | collective-permute-done | bytes 262176 | tf_op jit(solution)/shard_map/ppermute | solution.py:32
  47.5 0.1 fusion.1
  47.6 0.8 %collective-permute-start.10 = (bf16[16,32,256]{2,1,0:T(8,128)(2,1)S(1)}, bf16[16,32,256]{2,1,0:T(8,128)(2,1)S(1)}, u32[]{:S(2)}, u32[]{:S(2)}) collective-permute-start(bf16[16,32,256]{2,1,0:T(8,128)(2,1)S(1)} %fusion.1), channel_id=1, source_target_pairs={{0,32},{1,33},{2,34},{3,35},{4,36},{5,37},{6,38},{7,39},{8,40},{9,... | collective-permute-start | bytes 786440 | tf_op jit(solution)/shard_map/ppermute | solution.py:32
  48.5 0.1 broadcast_compare_fusion
  48.5 0.1 iota_compare_fusion
  48.6 6.9 %collective-permute-done.10 = bf16[16,32,256]{2,1,0:T(8,128)(2,1)S(1)} collective-permute-done((bf16[16,32,256]{2,1,0:T(8,128)(2,1)S(1)}, bf16[16,32,256]{2,1,0:T(8,128)(2,1)S(1)}, u32[]{:S(2)}, u32[]{:S(2)}) %collective-permute-start.10) | collective-permute-done | bytes 262176 | tf_op jit(solution)/shard_map/ppermute | solution.py:32
  55.5 0.9 %fusion.5 = bf16[16,32,256]{2,1,0:T(8,128)(2,1)} fusion(f32[4,16,32,256]{3,2,1,0:T(8,128)S(1)} %get-tuple-element.28, bf16[16,32,256]{2,1,0:T(8,128)(2,1)S(1)} %collective-permute-done.10, bf16[16,32,256]{2,1,0:T(8,128)(2,1)S(1)} %collective-permute-done.8, pred[16,256]{1,0:T(8,128)(4,1)S(1)} %iota_compare_fusion, pred[16,32]{1,0:T(8,128)(4,1)S(1)} %broadcast_compare_fusion), kind=kLoop, calls=%fused_computation.8 | loop fusion | flops 917504 | bytes 1315328 | tf_op jit(solution)/shard_map/convert_element_type | solution.py:224
  (16 shorter events, 0.1 us)
Async XLA Ops:
  0.0 0.7 %copy-start.3 = (s32[16]{0:T(128)S(1)}, s32[16]{0:T(128)}, u32[]{:S(2)}) copy-start(s32[16]{0:T(128)} %dims_ref.3) | copy-start | bytes 196
  0.7 6.8 %copy-start.2 = (bf16[8,16,256]{2,1,0:T(8,128)(2,1)S(1)}, bf16[8,16,256]{2,1,0:T(8,128)(2,1)}, u32[]{:S(2)}) copy-start(bf16[8,16,256]{2,1,0:T(8,128)(2,1)} %own) | copy-start | bytes 196612
  0.7 6.8 %copy-start = (bf16[16,256,256]{2,1,0:T(8,128)(2,1)S(1)}, bf16[16,256,256]{2,1,0:T(8,128)(2,1)}, u32[]{:S(2)}) copy-start(bf16[16,256,256]{2,1,0:T(8,128)(2,1)} %psi_ref.1) | copy-start | bytes 6291460
  0.7 6.8 %copy-start.4 = (s32[16]{0:T(128)S(1)}, s32[16]{0:T(128)}, u32[]{:S(2)}) copy-start(s32[16]{0:T(128)} %dims_ref.3) | copy-start | bytes 196
  2.1 13.4 %collective-permute-start = (bf16[640,256]{1,0:T(8,128)(2,1)S(1)}, bf16[640,256]{1,0:T(8,128)(2,1)S(1)}, u32[]{:S(2)}, u32[]{:S(2)}) collective-permute-start(bf16[640,256]{1,0:T(8,128)(2,1)S(1)} %get-tuple-element.19), channel_id=1, source_target_pairs={{0,1},{1,2},{2,3},{3,4},{4,5},{5,6},{6,7},{7,8},{8,9},{9,10},{10,1... | collective-permute-start | bytes 983048 | tf_op jit(solution)/shard_map/ppermute | solution.py:32
  3.7 17.7 %copy-start.1 = (bf16[8,256,256]{2,1,0:T(8,128)(2,1)S(1)}, bf16[8,256,256]{2,1,0:T(8,128)(2,1)}, u32[]{:S(2)}) copy-start(bf16[8,256,256]{2,1,0:T(8,128)(2,1)} %right_ref.3) | copy-start | bytes 3145732
  3.7 11.8 %collective-permute-start.1 = (bf16[640,256]{1,0:T(8,128)(2,1)S(1)}, bf16[640,256]{1,0:T(8,128)(2,1)S(1)}, u32[]{:S(2)}, u32[]{:S(2)}) collective-permute-start(bf16[640,256]{1,0:T(8,128)(2,1)S(1)} %get-tuple-element.20), channel_id=1, source_target_pairs={{0,15},{1,0},{2,1},{3,2},{4,3},{5,4},{6,5},{7,6},{8,7},{9,8},{10,9... | collective-permute-start | bytes 983048 | tf_op jit(solution)/shard_map/ppermute | solution.py:32
  7.5 8.0 %collective-permute-start.2 = (bf16[8,16,256]{2,1,0:T(8,128)(2,1)S(1)}, bf16[8,16,256]{2,1,0:T(8,128)(2,1)S(1)}, u32[]{:S(2)}, u32[]{:S(2)}) collective-permute-start(bf16[8,16,256]{2,1,0:T(8,128)(2,1)S(1)} %copy-done.2), channel_id=1, source_target_pairs={{0,2},{1,3},{2,4},{3,5},{4,6},{5,7},{6,8},{7,9},{8,10},{9,11},{10,... | collective-permute-start | bytes 196616 | tf_op jit(solution)/shard_map/ppermute | solution.py:32
  16.1 10.4 %collective-permute-start.6 = (bf16[1024,256]{1,0:T(8,128)(2,1)S(1)}, bf16[1024,256]{1,0:T(8,128)(2,1)S(1)}, u32[]{:S(2)}, u32[]{:S(2)}) collective-permute-start(bf16[1024,256]{1,0:T(8,128)(2,1)S(1)} %get-tuple-element.23.edge_own), channel_id=1, source_target_pairs={{0,16},{1,17},{2,18},{3,19},{4,20},{5,21},{6,22},{7,23},{8,24},{9,... | collective-permute-start | bytes 1572872 | tf_op jit(solution)/shard_map/ppermute | solution.py:32
  17.5 11.5 %collective-permute-start.3 = (bf16[4,8,16,256]{3,2,1,0:T(8,128)(2,1)S(1)}, bf16[4,8,16,256]{3,2,1,0:T(8,128)(2,1)S(1)}, u32[]{:S(2)}, u32[]{:S(2)}) collective-permute-start(bf16[4,8,16,256]{3,2,1,0:T(8,128)(2,1)S(1)} %get-tuple-element.22.t0), channel_id=1, source_target_pairs={{0,4},{1,5},{2,6},{3,7},{4,8},{5,9},{6,10},{7,11},{8,12},{9,13},{1... | collective-permute-start | bytes 786440 | tf_op jit(solution)/shard_map/ppermute | solution.py:32
  17.6 11.4 %collective-permute-start.4 = (bf16[4,8,16,256]{3,2,1,0:T(8,128)(2,1)S(1)}, bf16[4,8,16,256]{3,2,1,0:T(8,128)(2,1)S(1)}, u32[]{:S(2)}, u32[]{:S(2)}) collective-permute-start(bf16[4,8,16,256]{3,2,1,0:T(8,128)(2,1)S(1)} %get-tuple-element.22.t0), channel_id=1, source_target_pairs={{0,8},{1,9},{2,10},{3,11},{4,12},{5,13},{6,14},{7,15},{8,0},{9,1},... | collective-permute-start | bytes 786440 | tf_op jit(solution)/shard_map/ppermute | solution.py:32
  19.6 9.5 %collective-permute-start.5 = (bf16[4,8,16,256]{3,2,1,0:T(8,128)(2,1)S(1)}, bf16[4,8,16,256]{3,2,1,0:T(8,128)(2,1)S(1)}, u32[]{:S(2)}, u32[]{:S(2)}) collective-permute-start(bf16[4,8,16,256]{3,2,1,0:T(8,128)(2,1)S(1)} %get-tuple-element.22.t0), channel_id=1, source_target_pairs={{0,12},{1,13},{2,14},{3,15},{4,0},{5,1},{6,2},{7,3},{8,4},{9,5},{1... | collective-permute-start | bytes 786440 | tf_op jit(solution)/shard_map/ppermute | solution.py:32
  26.5 2.5 %copy-start.5 = (s32[8]{0:T(128)S(1)}, s32[8]{0:T(128)}, u32[]{:S(2)}) copy-start(s32[8]{0:T(128)} %shift_ref.1) | copy-start | bytes 100
  35.2 2.7 %collective-permute-start.7 = (bf16[4,16,32,256]{3,2,1,0:T(8,128)(2,1)S(1)}, bf16[4,16,32,256]{3,2,1,0:T(8,128)(2,1)S(1)}, u32[]{:S(2)}, u32[]{:S(2)}) collective-permute-start(bf16[4,16,32,256]{3,2,1,0:T(8,128)(2,1)S(1)} %get-tuple-element.26), channel_id=1, source_target_pairs={{0,16},{1,17},{2,18},{3,19},{4,20},{5,21},{6,22},{7,23},{8,24},{9,... | collective-permute-start | bytes 3145736 | tf_op jit(solution)/shard_map/ppermute | solution.py:32
  38.4 9.1 %collective-permute-start.9 = (bf16[16,32,256]{2,1,0:T(8,128)(2,1)S(1)}, bf16[16,32,256]{2,1,0:T(8,128)(2,1)S(1)}, u32[]{:S(2)}, u32[]{:S(2)}) collective-permute-start(bf16[16,32,256]{2,1,0:T(8,128)(2,1)S(1)} %get-tuple-element.30), channel_id=1, source_target_pairs={{0,32},{1,33},{2,34},{3,35},{4,36},{5,37},{6,38},{7,39},{8,40},{9,... | collective-permute-start | bytes 786440 | tf_op jit(solution)/shard_map/ppermute | solution.py:32
  40.4 8.2 %collective-permute-start.8 = (bf16[16,32,256]{2,1,0:T(8,128)(2,1)S(1)}, bf16[16,32,256]{2,1,0:T(8,128)(2,1)S(1)}, u32[]{:S(2)}, u32[]{:S(2)}) collective-permute-start(bf16[16,32,256]{2,1,0:T(8,128)(2,1)S(1)} %get-tuple-element.29), channel_id=1, source_target_pairs={{0,96},{1,97},{2,98},{3,99},{4,100},{5,101},{6,102},{7,103},{8,104... | collective-permute-start | bytes 786440 | tf_op jit(solution)/shard_map/ppermute | solution.py:32
  47.6 7.9 %collective-permute-start.10 = (bf16[16,32,256]{2,1,0:T(8,128)(2,1)S(1)}, bf16[16,32,256]{2,1,0:T(8,128)(2,1)S(1)}, u32[]{:S(2)}, u32[]{:S(2)}) collective-permute-start(bf16[16,32,256]{2,1,0:T(8,128)(2,1)S(1)} %fusion.1), channel_id=1, source_target_pairs={{0,32},{1,33},{2,34},{3,35},{4,36},{5,37},{6,38},{7,39},{8,40},{9,... | collective-permute-start | bytes 786440 | tf_op jit(solution)/shard_map/ppermute | solution.py:32

commit v4 on v3

--- a/solution.py
+++ b/solution.py
@@ -1,3 +1,5 @@
+import functools
+
 import jax
 import jax.numpy as jnp
 from jax import lax
@@ -12,6 +14,8 @@
 QMAX = 2
 HELD = SECS + 2 * QMAX
 STRIP = OPS * 16
+EARLY = 4
+SPLIT = 12
 BF = jnp.bfloat16
 F32 = jnp.float32
 
@@ -46,10 +50,6 @@
     return lambda z, c, y, x: (z, c, (y + d) % NY, x) if c == 0 else (z, c, y, (x + d) % NX)
 
 
-def to_core_1(z, c, y, x):
-    return (z, 1, y, x) if c == 0 else None
-
-
 def other_core(z, c, y, x):
     return (z, 1 - c, y, x)
 
@@ -74,16 +74,8 @@
         down_ref[to, :] = masked(first_psi[e], dims_ref[e])
 
 
-def mask_sectors(dims_ref, psi_ref, masked_ref):
-    def mask_one(s, _):
-        masked_ref[s] = masked(psi_ref[s], dims_ref[s])
-        return 0
-
-    lax.fori_loop(0, SECS, mask_one, 0)
-
-
-def unpack(place_ref, own, from_below, from_above, second_below, strips_ref, edges_ref):
-    strips_ref[0] = own[...]
+def unpack(place_ref, own, from_below, from_above, second_below, after, strips_ref, edges_ref):
+    strips_ref[0] = own[:STRIP, :].reshape(OPS, 16, B)
     strips_ref[1] = from_below[:STRIP, :].reshape(OPS, 16, B)
     strips_ref[2] = from_above[:STRIP, :].reshape(OPS, 16, B)
     strips_ref[3] = second_below[...]
@@ -93,23 +85,46 @@
         edges_ref[k * QMAX * B:(k + 1) * QMAX * B, :] = jnp.where(keep, source[STRIP:, :].astype(F32), 0.0).astype(BF)
 
 
-def by_twos(one):
+def by_twos(one, ops=(0, OPS)):
     def two_operators(i, _):
         one(2 * i)
         one(2 * i + 1)
         return 0
 
-    lax.fori_loop(0, OPS // 2, two_operators, 0)
-
-
-def own_sectors(masked_ref, right_ref, h_ref):
+    lax.fori_loop(ops[0] // 2, ops[1] // 2, two_operators, 0)
+
+
+def own_sectors(ops, masked_ref, right_ref, *refs):
+    h_ref = refs[-1]
+
     def one_operator(o):
         right_t = right_ref[o].T
         for s in range(0, SECS, 4):
             h = jnp.dot(masked_ref[s:s + 4].reshape(4 * B, B), right_t, preferred_element_type=F32)
             h_ref[o, (s + QMAX) * B:(s + QMAX + 4) * B, :] = h.astype(BF)
 
-    by_twos(one_operator)
+    by_twos(one_operator, ops)
+
+
+def first_operators(dims_ref, psi_hbm, right_hbm, masked_ref, right_ref, h_ref, done_ref, psi_sem, right_sem):
+    right_in = pltpu.make_async_copy(right_hbm, right_ref, right_sem)
+
+    def psi_in(s):
+        return pltpu.make_async_copy(psi_hbm.at[s], masked_ref.at[s], psi_sem.at[s])
+
+    for s in range(SECS):
+        psi_in(s).start()
+    right_in.start()
+
+    def mask_one(s, _):
+        psi_in(s).wait()
+        masked_ref[s] = masked(masked_ref[s], dims_ref[s])
+        return 0
+
+    lax.fori_loop(0, SECS, mask_one, 0)
+    right_in.wait()
+    own_sectors((0, EARLY), masked_ref, right_ref, h_ref)
+    done_ref[...] = jnp.zeros_like(done_ref)
 
 
 def edge_sectors(place_ref, edge_own, edge_other, right_ref, _, h_ref, edge_ref):
@@ -131,7 +146,7 @@
     by_twos(one_operator)
 
 
-def second_product(shift_ref, place_ref, t0, t1, t2, t3, h_ref, mine_ref, other_ref, left_ref):
+def order_left(place_ref, t0, t1, t2, t3, left_ref):
     z, core, y, x = place_ref[0], place_ref[1], place_ref[2], place_ref[3]
     for e, block in enumerate((t0, t1, t2, t3)):
         for d in range(4):
@@ -146,11 +161,13 @@
             for o in range(OPS):
                 left_ref[pl.ds(start, 16), o * B:(o + 1) * B] = block[d, o]
 
+
+def some_targets(first, shift_ref, left_ref, h_ref, mine_ref, other_ref):
     def four_targets(i, _):
         for u in range(4):
             t = i * 4 + u
             sources = [
-                h_ref[o, pl.ds(pl.multiple_of((t + QMAX - shift_ref[o]) * B, B), B), :] for o in range(OPS)
+                h_ref[o, pl.ds(pl.multiple_of((first + t + QMAX - shift_ref[o]) * B, B), B), :] for o in range(OPS)
             ]
             total = jnp.dot(left_ref[...], jnp.concatenate(sources, axis=0), preferred_element_type=F32)
             for k in range(NZ):
@@ -158,66 +175,92 @@
                 other_ref[k, t] = total[B // 2 + k * 32:B // 2 + (k + 1) * 32].astype(BF)
         return 0
 
-    lax.fori_loop(0, SECS // 4, four_targets, 0)
+    lax.fori_loop(0, mine_ref.shape[1] // 4, four_targets, 0)
+
+
+def first_targets(shift_ref, place_ref, t0, t1, t2, t3, h_ref, mine_ref, other_ref, left_ref):
+    order_left(place_ref, t0, t1, t2, t3, left_ref)
+    some_targets(0, shift_ref, left_ref, h_ref, mine_ref, other_ref)
+
+
+def add_cores(mine_a, mine_b, got_a, got_b, own_ref, near_ref, far_ref, back_ref):
+    for mine, got, to in ((mine_a, got_a, slice(0, SPLIT)), (mine_b, got_b, slice(SPLIT, SECS))):
+        own_ref[to] = mine[0] + got[0].astype(F32)
+        near_ref[to] = mine[1] + got[1].astype(F32)
+        far_ref[to] = (mine[2] + got[2].astype(F32)).astype(BF)
+        back_ref[to] = (mine[3] + got[3].astype(F32)).astype(BF)
 
 
 def on_device(psi, left_ops, right_ops, op_shift, sector_dims):
     p, q = lax.axis_index("op"), lax.axis_index("sec")
     core = p % NC
     place = jnp.stack([p // NC, core, q // NX, q % NX]).astype(jnp.int32)
-    index = jnp.arange(B, dtype=jnp.int32)
 
     smem = pl.BlockSpec(memory_space=pltpu.SMEM)
     vmem = pl.BlockSpec(memory_space=pltpu.VMEM)
+    hbm = pl.BlockSpec(memory_space=pltpu.HBM)
 
     def call(kernel, name, in_specs, out_shape, dots, scratch=(), aliases={}):
         return pl.pallas_call(
             kernel, in_specs=in_specs, out_shape=[jax.ShapeDtypeStruct(*o) for o in out_shape],
             out_specs=[vmem] * len(out_shape), name=name, scratch_shapes=scratch, input_output_aliases=aliases,
             compiler_params=pltpu.CompilerParams(vmem_limit_bytes=4 << 20),
-            cost_estimate=pl.CostEstimate(flops=2 * dots * B ** 3, bytes_accessed=4 << 20, transcendentals=0))
+            cost_estimate=pl.CostEstimate(flops=2 * dots * B ** 3, bytes_accessed=(4 << 20) * (dots > 0), transcendentals=0))
 
     ends = pl.BlockSpec((QMAX, B, B), lambda i: (0, 0, 0)), pl.BlockSpec((QMAX, B, B), lambda i: (SECS // QMAX - 1, 0, 0))
     packed = jax.ShapeDtypeStruct((STRIP + QMAX * B, B), BF)
     whole = pl.BlockSpec((STRIP + QMAX * B, B), lambda i: (0, 0))
+    dims_there = pltpu.with_memory_space_constraint(sector_dims, pltpu.HBM)
+    right_there = pltpu.with_memory_space_constraint(right_ops, pltpu.HBM)
     psi_there = pltpu.with_memory_space_constraint(psi, pltpu.HBM)
     up, down = pl.pallas_call(
         pack, grid=(1,), in_specs=[smem, *ends, pl.BlockSpec((OPS, 16, B), lambda i: (0, 0, 0))],
         out_shape=[packed, packed], out_specs=[whole, whole], name="pack",
         compiler_params=pltpu.CompilerParams(vmem_limit_bytes=4 << 20),
         cost_estimate=pl.CostEstimate(flops=0, bytes_accessed=1 << 20, transcendentals=0),
-    )(sector_dims, psi_there, psi_there, pltpu.with_memory_space_constraint(left_ops, pltpu.HBM))
+    )(dims_there, psi_there, psi_there, pltpu.with_memory_space_constraint(left_ops, pltpu.HBM))
     place, left_ops, up = lax.optimization_barrier((place, left_ops, up))
-    up = move(up, gather_first(1))
+    sent = up
+    up = move(sent, gather_first(1))
     down = move(down, gather_first(-1))
     two = move(left_ops, gather_first(2))
-    live_psi, = call(mask_sectors, "mask_sectors", [smem, vmem], [((SECS, B, B), BF)], 0)(sector_dims, psi)
-    two, _ = lax.optimization_barrier((two, live_psi))
+    live_psi, right, h, done = call(
+        first_operators, "first_operators", [smem, hbm, hbm],
+        [((SECS, B, B), BF), ((OPS, B, B), BF), ((OPS, HELD * B, B), BF), ((8, 128), F32)], EARLY * SECS,
+        [pltpu.SemaphoreType.DMA((SECS,)), pltpu.SemaphoreType.DMA],
+    )(dims_there, psi_there, right_there)
     strips, edges = call(
-        unpack, "unpack", [smem] + [vmem] * 4, [((4, OPS, 16, B), BF), ((2 * QMAX * B, B), BF)], 0,
-    )(place, left_ops, up, down, two)
+        unpack, "unpack", [smem] + [vmem] * 5, [((4, OPS, 16, B), BF), ((2 * QMAX * B, B), BF)], 0,
+    )(place, sent, up, down, two, done)
     seconds = [move(strips, gather_second(d)) for d in (1, 3, 2)]
     t0, t1, t3, t2 = strips, *seconds
-    edges_other = move(edges, to_core_1)
-
-    live_psi, _ = lax.optimization_barrier((live_psi, edges))
+    edges_other = move(edges, other_core)
+
     h, = call(
-        own_sectors, "own_sectors", [vmem] * 2, [((OPS, HELD * B, B), BF)], OPS * SECS,
-    )(live_psi, right_ops)
+        functools.partial(own_sectors, (EARLY, OPS)), "own_sectors", [vmem] * 4, [((OPS, HELD * B, B), BF)],
+        0, (), {3: 0},
+    )(live_psi, right, strips, h)
     h, = call(
-        edge_sectors, "edge_sectors", [smem] + [vmem] * 4, [((OPS, HELD * B, B), BF)], 1,
+        edge_sectors, "edge_sectors", [smem] + [vmem] * 4, [((OPS, HELD * B, B), BF)], 0,
         [pltpu.VMEM((2 * QMAX * B, B), BF)], {4: 0},
-    )(place, edges, edges_other, right_ops, h)
-    mine, other = call(
-        second_product, "second_product", [smem, smem] + [vmem] * 5,
-        [((NZ, SECS, 32, B), F32), ((NZ, SECS, 32, B), BF)], OPS * SECS, [pltpu.VMEM((B, OPS * B), BF)],
-    )(op_shift, place, t0, t1, t2, t3, h)
-
-    total = mine + move(other, other_core).astype(F32)
-    far = move(total[2].astype(BF), along_z(1))
-    back = move(total[3].astype(BF), along_z(-1))
-    near = move((total[1] + far.astype(F32)).astype(BF), along_z(1))
-    summed = total[0] + back.astype(F32) + near.astype(F32)
+    )(place, edges, edges_other, right, h)
+    first_a = [((NZ, SPLIT, 32, B), F32), ((NZ, SPLIT, 32, B), BF), ((B, OPS * B), BF)]
+    mine_a, away_a, left = call(first_targets, "first_targets", [smem, smem] + [vmem] * 5, first_a, OPS * SPLIT)(
+        op_shift, place, t0, t1, t2, t3, h)
+    rest = [((NZ, SECS - SPLIT, 32, B), F32), ((NZ, SECS - SPLIT, 32, B), BF)]
+    mine_b, away_b = call(
+        functools.partial(some_targets, SPLIT), "last_targets", [smem, vmem, vmem], rest, OPS * (SECS - SPLIT),
+    )(op_shift, left, h)
+
+    slot = (SECS, 32, B)
+    own, near, far, back = call(
+        add_cores, "add_cores", [vmem] * 4, [(slot, F32), (slot, F32), (slot, BF), (slot, BF)], 0,
+    )(mine_a, mine_b, move(away_a, other_core), move(away_b, other_core))
+    far = move(far, along_z(1))
+    back = move(back, along_z(-1))
+    near = move((near + far.astype(F32)).astype(BF), along_z(1))
+    summed = own + back.astype(F32) + near.astype(F32)
+    index = jnp.arange(B, dtype=jnp.int32)
     live = index[None, :] < sector_dims[:, None]
     mine_rows = p * 32 + jnp.arange(32, dtype=jnp.int32)
     live_rows = mine_rows[None, :] < sector_dims[:, None]

time: 56.5 us -> 54 us (0.956)
  waiting for transfers between devices: 21.2 us -> 18.2 us
  Pallas kernels: 17 us -> 19 us
  local copies, waits for them, and re-layouts: 0.71 us -> 0.01 us
    ppermute x11 -> x12, waiting for transfers between devices: 21.2 us -> 18.2 us  [move(): return lax.ppermute(block, ('op', 'sec'), route)]
    pallas_call x4 -> x6, Pallas kernels: 13.2 us -> 15.3 us  [the longest x1 5.37 us: on_device(): call(first_operators, 'first_operators', [smem, hbm, hbm], [((SECS, B, B)...]
    unnamed x12 -> x4, local copies, waits for them, and re-layouts: 0.68 us -> 0.01 us
    ppermute x11 -> x12, starting transfers between devices: 15.7 us -> 15.2 us  [move(): return lax.ppermute(block, ('op', 'sec'), route)]
  transfers between devices with their start and end apart: 11 -> 12, of which waited for: 4 -> 6; matrix products, arithmetic and copies ran while one was open for 0% -> 0% of each run, Pallas kernels for 16% -> 23%
where the time goes in v4:
time: 54 us; the launch traced here: 53.7 us
  Pallas kernels  19 us (35%)
  waiting for transfers between devices  18.2 us (34%)
  starting transfers between devices  15.2 us (28%)
  other arithmetic  1.16 us (2%)
    ppermute x12, waiting for transfers between devices, move(): return lax.ppermute(block, ('op', 'sec'), route)  18.2 us
    ppermute x12, starting transfers between devices, move(): return lax.ppermute(block, ('op', 'sec'), route)  15.2 us
    pallas_call x1, Pallas kernels, on_device(): call(first_operators, 'first_operators', [smem, hbm, hbm], [((SECS, B, B)...  5.37 us
    pallas_call x1, Pallas kernels, on_device(): call(first_targets, 'first_targets', [smem, smem] + [vmem] * 5, first_a,...  4.73 us
    pallas_call x1, Pallas kernels, on_device(): call(functools.partial(own_sectors, (EARLY, OPS)), 'own_sectors', [vmem]...  2.59 us
    pallas_call x1, Pallas kernels, on_device(): call(edge_sectors, 'edge_sectors', [smem] + [vmem] * 4, [((OPS, HELD * B,...  2.47 us
    pallas_call x1, Pallas kernels, on_device(): call(functools.partial(some_targets, SPLIT), 'last_targets', [smem, vmem,...  1.79 us
    pallas_call x1, Pallas kernels, on_device(): pl.pallas_call(pack, grid=(1,), in_specs=[smem, *ends, pl.BlockSpec((OPS,...  1.18 us
  transfers between devices with their start and end apart: 12, of which 6 were waited for; matrix products, arithmetic and copies ran while one was open for 0% of the time, Pallas kernels for 23%

profile of v4, /device:TPU:0, one launch (start us, length us, event | category | flops | bytes accessed | tf_op | source)
XLA Modules:
  0.0 53.7 jit_solution(12306250968654660863)
XLA Ops:
  0.0 1.2 %pack.1 = (bf16[640,256]{1,0:T(8,128)(2,1)S(1)}, bf16[640,256]{1,0:T(8,128)(2,1)S(1)}) custom-call(s32[16]{0:T(128)} %dims_ref.3, bf16[16,256,256]{2,1,0:T(8,128)(2,1)} %psi_hbm.1, bf16[16,256,256]{2,1,0:T(8,128)(2,1)} %psi_hbm.1, bf16[8,16,256]{2,1,0:T(8,128)(2,1)} %left_ref.1), custom_call_target="tpu_custom_call" | custom-call | bytes 1048576 | tf_op jit(solution)/shard_map/pack/pallas_call | solution.py:216
  1.2 0.1 pad_add_fusion.place_ref
  1.3 1.6 %collective-permute-start = (bf16[640,256]{1,0:T(8,128)(2,1)S(1)}, bf16[640,256]{1,0:T(8,128)(2,1)S(1)}, u32[]{:S(2)}, u32[]{:S(2)}) collective-permute-start(bf16[640,256]{1,0:T(8,128)(2,1)S(1)} %get-tuple-element.27.own), channel_id=1, source_target_pairs={{0,1},{1,2},{2,3},{3,4},{4,5},{5,6},{6,7},{7,8},{8,9},{9,10},{10,1... | collective-permute-start | bytes 983048 | tf_op jit(solution)/shard_map/ppermute | solution.py:36
  2.9 3.8 %collective-permute-start.1 = (bf16[640,256]{1,0:T(8,128)(2,1)S(1)}, bf16[640,256]{1,0:T(8,128)(2,1)S(1)}, u32[]{:S(2)}, u32[]{:S(2)}) collective-permute-start(bf16[640,256]{1,0:T(8,128)(2,1)S(1)} %get-tuple-element.28), channel_id=1, source_target_pairs={{0,15},{1,0},{2,1},{3,2},{4,3},{5,4},{6,5},{7,6},{8,7},{9,8},{10,9... | collective-permute-start | bytes 983048 | tf_op jit(solution)/shard_map/ppermute | solution.py:36
  6.7 5.4 %first_operators.1 = (bf16[16,256,256]{2,1,0:T(8,128)(2,1)S(1)}, bf16[8,256,256]{2,1,0:T(8,128)(2,1)S(1)}, bf16[8,5120,256]{2,1,0:T(8,128)(2,1)S(1)}, f32[8,128]{1,0:T(8,128)S(1)}) custom-call(s32[16]{0:T(128)} %dims_ref.3, bf16[16,256,256]{2,1,0:T(8,128)(2,1)} %psi_hbm.1, bf16[8,256,256]{2,1,0:T(8,128)(2,1)} %right_hbm.1), custom_call_target="tpu_custom_call" | custom-call | flops 2147483648 | bytes 4194304 | tf_op jit(solution)/shard_map/first_operators/pallas_call | solution.py:227
  12.0 2.7 %collective-permute-done.2.second_below = bf16[8,16,256]{2,1,0:T(8,128)(2,1)S(1)} collective-permute-done((bf16[8,16,256]{2,1,0:T(8,128)(2,1)}, bf16[8,16,256]{2,1,0:T(8,128)(2,1)S(1)}, u32[]{:S(2)}, u32[]{:S(2)}) %collective-permute-start.2) | collective-permute-done | bytes 65568 | tf_op jit(solution)/shard_map/ppermute | solution.py:36
  14.8 0.6 %unpack.1 = (bf16[4,8,16,256]{3,2,1,0:T(8,128)(2,1)S(1)}, bf16[1024,256]{1,0:T(8,128)(2,1)S(1)}) custom-call(s32[4]{0:T(128)S(1)} %pad_add_fusion.place_ref, bf16[640,256]{1,0:T(8,128)(2,1)S(1)} %get-tuple-element.27.own, bf16[640,256]{1,0:T(8,128)(2,1)S(1)} %collective-permute-done.from_below, bf16[640,256]{1,0:T(8,128)(2,1)S(1)} %collective-permute-done.1.from_above, ...), custom_call_target="tpu_custom_call" | custom-call | tf_op jit(solution)/shard_map/unpack/pallas_call | solution.py:232
  15.4 0.1 collective-permute-start.6
  15.5 0.1 collective-permute-start.3
  15.6 2.1 %collective-permute-start.4 = (bf16[4,8,16,256]{3,2,1,0:T(8,128)(2,1)S(1)}, bf16[4,8,16,256]{3,2,1,0:T(8,128)(2,1)S(1)}, u32[]{:S(2)}, u32[]{:S(2)}) collective-permute-start(bf16[4,8,16,256]{3,2,1,0:T(8,128)(2,1)S(1)} %get-tuple-element.31.refs_0_.t0), channel_id=1, source_target_pairs={{0,8},{1,9},{2,10},{3,11},{4,12},{5,13},{6,14},{7,15},{8,0},{9,1},... | collective-permute-start | bytes 786440 | tf_op jit(solution)/shard_map/ppermute | solution.py:36
  17.7 1.3 %collective-permute-start.5 = (bf16[4,8,16,256]{3,2,1,0:T(8,128)(2,1)S(1)}, bf16[4,8,16,256]{3,2,1,0:T(8,128)(2,1)S(1)}, u32[]{:S(2)}, u32[]{:S(2)}) collective-permute-start(bf16[4,8,16,256]{3,2,1,0:T(8,128)(2,1)S(1)} %get-tuple-element.31.refs_0_.t0), channel_id=1, source_target_pairs={{0,12},{1,13},{2,14},{3,15},{4,0},{5,1},{6,2},{7,3},{8,4},{9,5},{1... | collective-permute-start | bytes 786440 | tf_op jit(solution)/shard_map/ppermute | solution.py:36
  19.0 2.6 %own_sectors.1._ = bf16[8,5120,256]{2,1,0:T(8,128)(2,1)S(1)} custom-call(bf16[16,256,256]{2,1,0:T(8,128)(2,1)S(1)} %get-tuple-element.34.masked_ref, bf16[8,256,256]{2,1,0:T(8,128)(2,1)S(1)} %get-tuple-element.33.right_ref, bf16[4,8,16,256]{3,2,1,0:T(8,128)(2,1)S(1)} %get-tuple-element.31.refs_0_.t0, ...), custom_call_target="tpu_custom_call", output_to_operand_aliasing={{}: (3, {})} | custom-call | tf_op jit(solution)/shard_map/own_sectors/pallas_call | solution.py:239
  21.6 0.0 copy-start
  21.6 2.5 %edge_sectors.1.h_ref = bf16[8,5120,256]{2,1,0:T(8,128)(2,1)S(1)} custom-call(s32[4]{0:T(128)S(1)} %pad_add_fusion.place_ref, bf16[1024,256]{1,0:T(8,128)(2,1)S(1)} %get-tuple-element.32.edge_own, bf16[1024,256]{1,0:T(8,128)(2,1)S(1)} %collective-permute-done.6.edge_other, ...), custom_call_target="tpu_custom_call", output_to_operand_aliasing={{}: (4, {})} | custom-call | tf_op jit(solution)/shard_map/edge_sectors/pallas_call | solution.py:243
  24.1 0.0 copy-start.1
  24.1 1.8 %collective-permute-done.3.t1 = bf16[4,8,16,256]{3,2,1,0:T(8,128)(2,1)S(1)} collective-permute-done((bf16[4,8,16,256]{3,2,1,0:T(8,128)(2,1)S(1)}, bf16[4,8,16,256]{3,2,1,0:T(8,128)(2,1)S(1)}, u32[]{:S(2)}, u32[]{:S(2)}) %collective-permute-start.3) | collective-permute-done | bytes 262176 | tf_op jit(solution)/shard_map/ppermute | solution.py:36
  26.0 0.9 %collective-permute-done.5.t3 = bf16[4,8,16,256]{3,2,1,0:T(8,128)(2,1)S(1)} collective-permute-done((bf16[4,8,16,256]{3,2,1,0:T(8,128)(2,1)S(1)}, bf16[4,8,16,256]{3,2,1,0:T(8,128)(2,1)S(1)}, u32[]{:S(2)}, u32[]{:S(2)}) %collective-permute-start.5) | collective-permute-done | bytes 262176 | tf_op jit(solution)/shard_map/ppermute | solution.py:36
  26.9 4.7 %first_targets.1 = (f32[4,12,32,256]{3,2,1,0:T(8,128)S(1)}, bf16[4,12,32,256]{3,2,1,0:T(8,128)(2,1)S(1)}, bf16[256,2048]{1,0:T(8,128)(2,1)S(1)}) custom-call(s32[8]{0:T(128)S(1)} %copy-done, s32[4]{0:T(128)S(1)} %pad_add_fusion.place_ref, bf16[4,8,16,256]{3,2,1,0:T(8,128)(2,1)S(1)} %get-tuple-element.31.refs_0_.t0, ...), custom_call_target="tpu_custom_call" | custom-call | flops 3221225472 | bytes 4194304 | tf_op jit(solution)/shard_map/first_targets/pallas_call | solution.py:248
  31.6 0.1 collective-permute-start.7
  31.7 1.8 %last_targets.1 = (f32[4,4,32,256]{3,2,1,0:T(8,128)S(1)}, bf16[4,4,32,256]{3,2,1,0:T(8,128)(2,1)S(1)}) custom-call(s32[8]{0:T(128)S(1)} %copy-done, bf16[256,2048]{1,0:T(8,128)(2,1)S(1)} %get-tuple-element.37.left_ref, bf16[8,5120,256]{2,1,0:T(8,128)(2,1)S(1)} %edge_sectors.1.h_ref), custom_call_target="tpu_custom_call" | custom-call | flops 1073741824 | bytes 4194304 | tf_op jit(solution)/shard_map/last_targets/pallas_call | solution.py:251
  33.5 0.6 %collective-permute-start.8 = (bf16[4,4,32,256]{3,2,1,0:T(8,128)(2,1)S(1)}, bf16[4,4,32,256]{3,2,1,0:T(8,128)(2,1)S(1)}, u32[]{:S(2)}, u32[]{:S(2)}) collective-permute-start(bf16[4,4,32,256]{3,2,1,0:T(8,128)(2,1)S(1)} %get-tuple-element.40), channel_id=1, source_target_pairs={{0,16},{1,17},{2,18},{3,19},{4,20},{5,21},{6,22},{7,23},{8,24},{9,... | collective-permute-start | bytes 786440 | tf_op jit(solution)/shard_map/ppermute | solution.py:36
  34.1 1.2 %collective-permute-done.8.got_b = bf16[4,4,32,256]{3,2,1,0:T(8,128)(2,1)S(1)} collective-permute-done((bf16[4,4,32,256]{3,2,1,0:T(8,128)(2,1)S(1)}, bf16[4,4,32,256]{3,2,1,0:T(8,128)(2,1)S(1)}, u32[]{:S(2)}, u32[]{:S(2)}) %collective-permute-start.8) | collective-permute-done | bytes 262176 | tf_op jit(solution)/shard_map/ppermute | solution.py:36
  35.2 0.2 add_cores.1
  35.5 2.0 %collective-permute-start.10 = (bf16[16,32,256]{2,1,0:T(8,128)(2,1)S(1)}, bf16[16,32,256]{2,1,0:T(8,128)(2,1)S(1)}, u32[]{:S(2)}, u32[]{:S(2)}) collective-permute-start(bf16[16,32,256]{2,1,0:T(8,128)(2,1)S(1)} %get-tuple-element.44), channel_id=1, source_target_pairs={{0,32},{1,33},{2,34},{3,35},{4,36},{5,37},{6,38},{7,39},{8,40},{9,... | collective-permute-start | bytes 786440 | tf_op jit(solution)/shard_map/ppermute | solution.py:36
  37.5 2.2 %collective-permute-start.9 = (bf16[16,32,256]{2,1,0:T(8,128)(2,1)S(1)}, bf16[16,32,256]{2,1,0:T(8,128)(2,1)S(1)}, u32[]{:S(2)}, u32[]{:S(2)}) collective-permute-start(bf16[16,32,256]{2,1,0:T(8,128)(2,1)S(1)} %get-tuple-element.42), channel_id=1, source_target_pairs={{0,96},{1,97},{2,98},{3,99},{4,100},{5,101},{6,102},{7,103},{8,104... | collective-permute-start | bytes 786440 | tf_op jit(solution)/shard_map/ppermute | solution.py:36
  39.7 4.6 %collective-permute-done.10 = bf16[16,32,256]{2,1,0:T(8,128)(2,1)S(1)} collective-permute-done((bf16[16,32,256]{2,1,0:T(8,128)(2,1)S(1)}, bf16[16,32,256]{2,1,0:T(8,128)(2,1)S(1)}, u32[]{:S(2)}, u32[]{:S(2)}) %collective-permute-start.10) | collective-permute-done | bytes 262176 | tf_op jit(solution)/shard_map/ppermute | solution.py:36
  44.4 0.1 add_convert_fusion
  44.4 1.3 %collective-permute-start.11 = (bf16[16,32,256]{2,1,0:T(8,128)(2,1)S(1)}, bf16[16,32,256]{2,1,0:T(8,128)(2,1)S(1)}, u32[]{:S(2)}, u32[]{:S(2)}) collective-permute-start(bf16[16,32,256]{2,1,0:T(8,128)(2,1)S(1)} %add_convert_fusion), channel_id=1, source_target_pairs={{0,32},{1,33},{2,34},{3,35},{4,36},{5,37},{6,38},{7,39},{8,40},{9,... | collective-permute-start | bytes 786440 | tf_op jit(solution)/shard_map/ppermute | solution.py:36
  45.8 0.1 broadcast_compare_fusion
  45.9 0.1 iota_compare_fusion
  45.9 6.9 %collective-permute-done.11 = bf16[16,32,256]{2,1,0:T(8,128)(2,1)S(1)} collective-permute-done((bf16[16,32,256]{2,1,0:T(8,128)(2,1)S(1)}, bf16[16,32,256]{2,1,0:T(8,128)(2,1)S(1)}, u32[]{:S(2)}, u32[]{:S(2)}) %collective-permute-start.11) | collective-permute-done | bytes 262176 | tf_op jit(solution)/shard_map/ppermute | solution.py:36
  52.8 0.9 %select_convert_fusion = bf16[16,32,256]{2,1,0:T(8,128)(2,1)} fusion(bf16[16,32,256]{2,1,0:T(8,128)(2,1)S(1)} %collective-permute-done.11, f32[16,32,256]{2,1,0:T(8,128)S(1)} %get-tuple-element.41, bf16[16,32,256]{2,1,0:T(8,128)(2,1)S(1)} %collective-permute-done.9, pred[16,256]{1,0:T(8,128)(4,1)S(1)} %iota_compare_fusion, ...), kind=kLoop, calls=%fused_computation | loop fusion | flops 917504 | bytes 1315328 | tf_op jit(solution)/shard_map/convert_element_type | solution.py:267
  (10 shorter events, 0.0 us)
Async XLA Ops:
  1.3 13.5 %collective-permute-start = (bf16[640,256]{1,0:T(8,128)(2,1)S(1)}, bf16[640,256]{1,0:T(8,128)(2,1)S(1)}, u32[]{:S(2)}, u32[]{:S(2)}) collective-permute-start(bf16[640,256]{1,0:T(8,128)(2,1)S(1)} %get-tuple-element.27.own), channel_id=1, source_target_pairs={{0,1},{1,2},{2,3},{3,4},{4,5},{5,6},{6,7},{7,8},{8,9},{9,10},{10,1... | collective-permute-start | bytes 983048 | tf_op jit(solution)/shard_map/ppermute | solution.py:36
  2.9 11.9 %collective-permute-start.1 = (bf16[640,256]{1,0:T(8,128)(2,1)S(1)}, bf16[640,256]{1,0:T(8,128)(2,1)S(1)}, u32[]{:S(2)}, u32[]{:S(2)}) collective-permute-start(bf16[640,256]{1,0:T(8,128)(2,1)S(1)} %get-tuple-element.28), channel_id=1, source_target_pairs={{0,15},{1,0},{2,1},{3,2},{4,3},{5,4},{6,5},{7,6},{8,7},{9,8},{10,9... | collective-permute-start | bytes 983048 | tf_op jit(solution)/shard_map/ppermute | solution.py:36
  6.7 8.1 %collective-permute-start.2 = (bf16[8,16,256]{2,1,0:T(8,128)(2,1)}, bf16[8,16,256]{2,1,0:T(8,128)(2,1)S(1)}, u32[]{:S(2)}, u32[]{:S(2)}) collective-permute-start(bf16[8,16,256]{2,1,0:T(8,128)(2,1)} %left_ref.1), channel_id=1, source_target_pairs={{0,2},{1,3},{2,4},{3,5},{4,6},{5,7},{6,8},{7,9},{8,10},{9,11},{10,... | collective-permute-start | bytes 196616 | tf_op jit(solution)/shard_map/ppermute | solution.py:36
  15.4 6.2 %collective-permute-start.6 = (bf16[1024,256]{1,0:T(8,128)(2,1)S(1)}, bf16[1024,256]{1,0:T(8,128)(2,1)S(1)}, u32[]{:S(2)}, u32[]{:S(2)}) collective-permute-start(bf16[1024,256]{1,0:T(8,128)(2,1)S(1)} %get-tuple-element.32.edge_own), channel_id=1, source_target_pairs={{0,16},{1,17},{2,18},{3,19},{4,20},{5,21},{6,22},{7,23},{8,24},{9,... | collective-permute-start | bytes 1572872 | tf_op jit(solution)/shard_map/ppermute | solution.py:36
  15.5 10.5 %collective-permute-start.3 = (bf16[4,8,16,256]{3,2,1,0:T(8,128)(2,1)S(1)}, bf16[4,8,16,256]{3,2,1,0:T(8,128)(2,1)S(1)}, u32[]{:S(2)}, u32[]{:S(2)}) collective-permute-start(bf16[4,8,16,256]{3,2,1,0:T(8,128)(2,1)S(1)} %get-tuple-element.31.refs_0_.t0), channel_id=1, source_target_pairs={{0,4},{1,5},{2,6},{3,7},{4,8},{5,9},{6,10},{7,11},{8,12},{9,13},{1... | collective-permute-start | bytes 786440 | tf_op jit(solution)/shard_map/ppermute | solution.py:36
  15.6 10.4 %collective-permute-start.4 = (bf16[4,8,16,256]{3,2,1,0:T(8,128)(2,1)S(1)}, bf16[4,8,16,256]{3,2,1,0:T(8,128)(2,1)S(1)}, u32[]{:S(2)}, u32[]{:S(2)}) collective-permute-start(bf16[4,8,16,256]{3,2,1,0:T(8,128)(2,1)S(1)} %get-tuple-element.31.refs_0_.t0), channel_id=1, source_target_pairs={{0,8},{1,9},{2,10},{3,11},{4,12},{5,13},{6,14},{7,15},{8,0},{9,1},... | collective-permute-start | bytes 786440 | tf_op jit(solution)/shard_map/ppermute | solution.py:36
  17.7 9.2 %collective-permute-start.5 = (bf16[4,8,16,256]{3,2,1,0:T(8,128)(2,1)S(1)}, bf16[4,8,16,256]{3,2,1,0:T(8,128)(2,1)S(1)}, u32[]{:S(2)}, u32[]{:S(2)}) collective-permute-start(bf16[4,8,16,256]{3,2,1,0:T(8,128)(2,1)S(1)} %get-tuple-element.31.refs_0_.t0), channel_id=1, source_target_pairs={{0,12},{1,13},{2,14},{3,15},{4,0},{5,1},{6,2},{7,3},{8,4},{9,5},{1... | collective-permute-start | bytes 786440 | tf_op jit(solution)/shard_map/ppermute | solution.py:36
  21.6 5.2 %copy-start = (s32[8]{0:T(128)S(1)}, s32[8]{0:T(128)}, u32[]{:S(2)}) copy-start(s32[8]{0:T(128)} %shift_ref.3) | copy-start | bytes 100
  24.1 21.7 %copy-start.1 = (s32[16]{0:T(128)S(1)}, s32[16]{0:T(128)}, u32[]{:S(2)}) copy-start(s32[16]{0:T(128)} %dims_ref.3) | copy-start | bytes 196
  31.6 3.6 %collective-permute-start.7 = (bf16[4,12,32,256]{3,2,1,0:T(8,128)(2,1)S(1)}, bf16[4,12,32,256]{3,2,1,0:T(8,128)(2,1)S(1)}, u32[]{:S(2)}, u32[]{:S(2)}) collective-permute-start(bf16[4,12,32,256]{3,2,1,0:T(8,128)(2,1)S(1)} %get-tuple-element.39), channel_id=1, source_target_pairs={{0,16},{1,17},{2,18},{3,19},{4,20},{5,21},{6,22},{7,23},{8,24},{9,... | collective-permute-start | bytes 2359304 | tf_op jit(solution)/shard_map/ppermute | solution.py:36
  33.5 1.7 %collective-permute-start.8 = (bf16[4,4,32,256]{3,2,1,0:T(8,128)(2,1)S(1)}, bf16[4,4,32,256]{3,2,1,0:T(8,128)(2,1)S(1)}, u32[]{:S(2)}, u32[]{:S(2)}) collective-permute-start(bf16[4,4,32,256]{3,2,1,0:T(8,128)(2,1)S(1)} %get-tuple-element.40), channel_id=1, source_target_pairs={{0,16},{1,17},{2,18},{3,19},{4,20},{5,21},{6,22},{7,23},{8,24},{9,... | collective-permute-start | bytes 786440 | tf_op jit(solution)/shard_map/ppermute | solution.py:36
  35.5 8.9 %collective-permute-start.10 = (bf16[16,32,256]{2,1,0:T(8,128)(2,1)S(1)}, bf16[16,32,256]{2,1,0:T(8,128)(2,1)S(1)}, u32[]{:S(2)}, u32[]{:S(2)}) collective-permute-start(bf16[16,32,256]{2,1,0:T(8,128)(2,1)S(1)} %get-tuple-element.44), channel_id=1, source_target_pairs={{0,32},{1,33},{2,34},{3,35},{4,36},{5,37},{6,38},{7,39},{8,40},{9,... | collective-permute-start | bytes 786440 | tf_op jit(solution)/shard_map/ppermute | solution.py:36
  37.5 8.4 %collective-permute-start.9 = (bf16[16,32,256]{2,1,0:T(8,128)(2,1)S(1)}, bf16[16,32,256]{2,1,0:T(8,128)(2,1)S(1)}, u32[]{:S(2)}, u32[]{:S(2)}) collective-permute-start(bf16[16,32,256]{2,1,0:T(8,128)(2,1)S(1)} %get-tuple-element.42), channel_id=1, source_target_pairs={{0,96},{1,97},{2,98},{3,99},{4,100},{5,101},{6,102},{7,103},{8,104... | collective-permute-start | bytes 786440 | tf_op jit(solution)/shard_map/ppermute | solution.py:36
  44.4 8.4 %collective-permute-start.11 = (bf16[16,32,256]{2,1,0:T(8,128)(2,1)S(1)}, bf16[16,32,256]{2,1,0:T(8,128)(2,1)S(1)}, u32[]{:S(2)}, u32[]{:S(2)}) collective-permute-start(bf16[16,32,256]{2,1,0:T(8,128)(2,1)S(1)} %add_convert_fusion), channel_id=1, source_target_pairs={{0,32},{1,33},{2,34},{3,35},{4,36},{5,37},{6,38},{7,39},{8,40},{9,... | collective-permute-start | bytes 786440 | tf_op jit(solution)/shard_map/ppermute | solution.py:36

commit v5 on v4

--- a/solution.py
+++ b/solution.py
@@ -127,7 +127,7 @@
     done_ref[...] = jnp.zeros_like(done_ref)
 
 
-def edge_sectors(place_ref, edge_own, edge_other, right_ref, _, h_ref, edge_ref):
+def other_sectors(shift_ref, place_ref, edge_own, edge_other, masked_ref, right_ref, _, h_ref, edge_ref):
     core = place_ref[1]
 
     @pl.when(core == 0)
@@ -138,12 +138,16 @@
     def _():
         edge_ref[...] = edge_other[...]
 
-    def one_operator(o):
-        h = jnp.dot(edge_ref[...], right_ref[o].T, preferred_element_type=F32).astype(BF)
-        h_ref[o, :QMAX * B, :] = h[:QMAX * B]
-        h_ref[o, (SECS + QMAX) * B:, :] = h[QMAX * B:]
-
-    by_twos(one_operator)
+    def edge_side(o):
+        above = (shift_ref[o] < 0).astype(jnp.int32)
+        source = pl.multiple_of(above * (QMAX * B), QMAX * B)
+        to = pl.multiple_of(above * ((QMAX + SECS) * B), QMAX * B)
+        h = jnp.dot(edge_ref[pl.ds(source, QMAX * B), :], right_ref[o].T, preferred_element_type=F32)
+        h_ref[o, pl.ds(to, QMAX * B), :] = h.astype(BF)
+
+    own_sectors((EARLY, OPS), masked_ref, right_ref, h_ref)
+    for o in range(OPS):
+        edge_side(o)
 
 
 def order_left(place_ref, t0, t1, t2, t3, left_ref):
@@ -237,13 +241,10 @@
     edges_other = move(edges, other_core)
 
     h, = call(
-        functools.partial(own_sectors, (EARLY, OPS)), "own_sectors", [vmem] * 4, [((OPS, HELD * B, B), BF)],
-        0, (), {3: 0},
-    )(live_psi, right, strips, h)
-    h, = call(
-        edge_sectors, "edge_sectors", [smem] + [vmem] * 4, [((OPS, HELD * B, B), BF)], 0,
-        [pltpu.VMEM((2 * QMAX * B, B), BF)], {4: 0},
-    )(place, edges, edges_other, right, h)
+        other_sectors, "other_sectors", [smem, smem] + [vmem] * 5, [((OPS, HELD * B, B), BF)], 0,
+        [pltpu.VMEM((2 * QMAX * B, B), BF)], {6: 0},
+    )(op_shift, place, edges, edges_other, live_psi, right, h)
+
     first_a = [((NZ, SPLIT, 32, B), F32), ((NZ, SPLIT, 32, B), BF), ((B, OPS * B), BF)]
     mine_a, away_a, left = call(first_targets, "first_targets", [smem, smem] + [vmem] * 5, first_a, OPS * SPLIT)(
         op_shift, place, t0, t1, t2, t3, h)

time: 54 us -> 53.9 us (level)
  waiting for transfers between devices: 18.2 us -> 19.4 us
  Pallas kernels: 19 us -> 17.9 us
    ppermute x12, waiting for transfers between devices: 18.2 us -> 19.4 us  [move(): return lax.ppermute(block, ('op', 'sec'), route)]
    pallas_call x2 -> x1, Pallas kernels: 5.06 us -> 3.89 us  [on_device(): call(other_sectors, 'other_sectors', [smem, smem] + [vmem] * 5, [((OPS, H...]
  transfers between devices with their start and end apart: 12 -> 12, of which waited for: 6 -> 6; matrix products, arithmetic and copies ran while one was open for 0% -> 0% of each run, Pallas kernels for 23% -> 21%
where the time goes in v5:
time: 53.9 us; the launch traced here: 53.6 us
  waiting for transfers between devices  19.4 us (36%)
  Pallas kernels  17.9 us (33%)
  starting transfers between devices  15.1 us (28%)
  other arithmetic  1.16 us (2%)
    ppermute x12, waiting for transfers between devices, move(): return lax.ppermute(block, ('op', 'sec'), route)  19.4 us
    ppermute x12, starting transfers between devices, move(): return lax.ppermute(block, ('op', 'sec'), route)  15.1 us
    pallas_call x1, Pallas kernels, on_device(): call(first_operators, 'first_operators', [smem, hbm, hbm], [((SECS, B, B)...  5.36 us
    pallas_call x1, Pallas kernels, on_device(): call(first_targets, 'first_targets', [smem, smem] + [vmem] * 5, first_a,...  4.73 us
    pallas_call x1, Pallas kernels, on_device(): call(other_sectors, 'other_sectors', [smem, smem] + [vmem] * 5, [((OPS, H...  3.89 us
    pallas_call x1, Pallas kernels, on_device(): call(functools.partial(some_targets, SPLIT), 'last_targets', [smem, vmem,...  1.79 us
    pallas_call x1, Pallas kernels, on_device(): pl.pallas_call(pack, grid=(1,), in_specs=[smem, *ends, pl.BlockSpec((OPS,...  1.22 us
  transfers between devices with their start and end apart: 12, of which 6 were waited for; matrix products, arithmetic and copies ran while one was open for 0% of the time, Pallas kernels for 21%

profile of v5, /device:TPU:0, one launch (start us, length us, event | category | flops | bytes accessed | tf_op | source)
XLA Modules:
  0.0 53.6 jit_solution(6531318968913594248)
XLA Ops:
  0.0 1.2 %pack.1 = (bf16[640,256]{1,0:T(8,128)(2,1)S(1)}, bf16[640,256]{1,0:T(8,128)(2,1)S(1)}) custom-call(s32[16]{0:T(128)} %dims_ref.3, bf16[16,256,256]{2,1,0:T(8,128)(2,1)} %psi_hbm.1, bf16[16,256,256]{2,1,0:T(8,128)(2,1)} %psi_hbm.1, bf16[8,16,256]{2,1,0:T(8,128)(2,1)} %left_ref.1), custom_call_target="tpu_custom_call" | custom-call | bytes 1048576 | tf_op jit(solution)/shard_map/pack/pallas_call | solution.py:220
  1.2 0.1 pad_add_fusion.place_ref
  1.3 1.6 %collective-permute-start = (bf16[640,256]{1,0:T(8,128)(2,1)S(1)}, bf16[640,256]{1,0:T(8,128)(2,1)S(1)}, u32[]{:S(2)}, u32[]{:S(2)}) collective-permute-start(bf16[640,256]{1,0:T(8,128)(2,1)S(1)} %get-tuple-element.27.own), channel_id=1, source_target_pairs={{0,1},{1,2},{2,3},{3,4},{4,5},{5,6},{6,7},{7,8},{8,9},{9,10},{10,1... | collective-permute-start | bytes 983048 | tf_op jit(solution)/shard_map/ppermute | solution.py:36
  2.9 3.8 %collective-permute-start.1 = (bf16[640,256]{1,0:T(8,128)(2,1)S(1)}, bf16[640,256]{1,0:T(8,128)(2,1)S(1)}, u32[]{:S(2)}, u32[]{:S(2)}) collective-permute-start(bf16[640,256]{1,0:T(8,128)(2,1)S(1)} %get-tuple-element.28), channel_id=1, source_target_pairs={{0,15},{1,0},{2,1},{3,2},{4,3},{5,4},{6,5},{7,6},{8,7},{9,8},{10,9... | collective-permute-start | bytes 983048 | tf_op jit(solution)/shard_map/ppermute | solution.py:36
  6.7 0.0 collective-permute-start.2
  6.7 5.4 %first_operators.1 = (bf16[16,256,256]{2,1,0:T(8,128)(2,1)S(1)}, bf16[8,256,256]{2,1,0:T(8,128)(2,1)S(1)}, bf16[8,5120,256]{2,1,0:T(8,128)(2,1)S(1)}, f32[8,128]{1,0:T(8,128)S(1)}) custom-call(s32[16]{0:T(128)} %dims_ref.3, bf16[16,256,256]{2,1,0:T(8,128)(2,1)} %psi_hbm.1, bf16[8,256,256]{2,1,0:T(8,128)(2,1)} %right_hbm.1), custom_call_target="tpu_custom_call" | custom-call | flops 2147483648 | bytes 4194304 | tf_op jit(solution)/shard_map/first_operators/pallas_call | solution.py:231
  12.1 2.6 %collective-permute-done.2.second_below = bf16[8,16,256]{2,1,0:T(8,128)(2,1)S(1)} collective-permute-done((bf16[8,16,256]{2,1,0:T(8,128)(2,1)S(1)}, bf16[8,16,256]{2,1,0:T(8,128)(2,1)S(1)}, u32[]{:S(2)}, u32[]{:S(2)}) %collective-permute-start.2) | collective-permute-done | bytes 65568 | tf_op jit(solution)/shard_map/ppermute | solution.py:36
  14.7 0.6 %unpack.1 = (bf16[4,8,16,256]{3,2,1,0:T(8,128)(2,1)S(1)}, bf16[1024,256]{1,0:T(8,128)(2,1)S(1)}) custom-call(s32[4]{0:T(128)S(1)} %pad_add_fusion.place_ref, bf16[640,256]{1,0:T(8,128)(2,1)S(1)} %get-tuple-element.27.own, bf16[640,256]{1,0:T(8,128)(2,1)S(1)} %collective-permute-done.from_below, bf16[640,256]{1,0:T(8,128)(2,1)S(1)} %collective-permute-done.1.from_above, ...), custom_call_target="tpu_custom_call" | custom-call | tf_op jit(solution)/shard_map/unpack/pallas_call | solution.py:236
  15.4 0.1 collective-permute-start.6
  15.5 0.1 collective-permute-start.3
  15.5 2.0 %collective-permute-start.4 = (bf16[4,8,16,256]{3,2,1,0:T(8,128)(2,1)S(1)}, bf16[4,8,16,256]{3,2,1,0:T(8,128)(2,1)S(1)}, u32[]{:S(2)}, u32[]{:S(2)}) collective-permute-start(bf16[4,8,16,256]{3,2,1,0:T(8,128)(2,1)S(1)} %get-tuple-element.31.t0), channel_id=1, source_target_pairs={{0,8},{1,9},{2,10},{3,11},{4,12},{5,13},{6,14},{7,15},{8,0},{9,1},... | collective-permute-start | bytes 786440 | tf_op jit(solution)/shard_map/ppermute | solution.py:36
  17.6 1.3 %collective-permute-start.5 = (bf16[4,8,16,256]{3,2,1,0:T(8,128)(2,1)S(1)}, bf16[4,8,16,256]{3,2,1,0:T(8,128)(2,1)S(1)}, u32[]{:S(2)}, u32[]{:S(2)}) collective-permute-start(bf16[4,8,16,256]{3,2,1,0:T(8,128)(2,1)S(1)} %get-tuple-element.31.t0), channel_id=1, source_target_pairs={{0,12},{1,13},{2,14},{3,15},{4,0},{5,1},{6,2},{7,3},{8,4},{9,5},{1... | collective-permute-start | bytes 786440 | tf_op jit(solution)/shard_map/ppermute | solution.py:36
  18.9 0.0 collective-permute-done.6.edge_other
  18.9 3.9 %other_sectors.1.h_ref = bf16[8,5120,256]{2,1,0:T(8,128)(2,1)S(1)} custom-call(s32[8]{0:T(128)S(1)} %copy-done, s32[4]{0:T(128)S(1)} %pad_add_fusion.place_ref, bf16[1024,256]{1,0:T(8,128)(2,1)S(1)} %get-tuple-element.32.edge_own, bf16[1024,256]{1,0:T(8,128)(2,1)S(1)} %collective-permute-done.6.edge_other, ...), custom_call_target="tpu_custom_call", output_to_operand_aliasing={{}: (6, {})} | custom-call | tf_op jit(solution)/shard_map/other_sectors/pallas_call | solution.py:243
  22.8 3.1 %collective-permute-done.3.t1 = bf16[4,8,16,256]{3,2,1,0:T(8,128)(2,1)S(1)} collective-permute-done((bf16[4,8,16,256]{3,2,1,0:T(8,128)(2,1)S(1)}, bf16[4,8,16,256]{3,2,1,0:T(8,128)(2,1)S(1)}, u32[]{:S(2)}, u32[]{:S(2)}) %collective-permute-start.3) | collective-permute-done | bytes 262176 | tf_op jit(solution)/shard_map/ppermute | solution.py:36
  25.9 0.0 collective-permute-done.4.t2
  25.9 0.9 %collective-permute-done.5.t3 = bf16[4,8,16,256]{3,2,1,0:T(8,128)(2,1)S(1)} collective-permute-done((bf16[4,8,16,256]{3,2,1,0:T(8,128)(2,1)S(1)}, bf16[4,8,16,256]{3,2,1,0:T(8,128)(2,1)S(1)}, u32[]{:S(2)}, u32[]{:S(2)}) %collective-permute-start.5) | collective-permute-done | bytes 262176 | tf_op jit(solution)/shard_map/ppermute | solution.py:36
  26.8 4.7 %first_targets.1 = (f32[4,12,32,256]{3,2,1,0:T(8,128)S(1)}, bf16[4,12,32,256]{3,2,1,0:T(8,128)(2,1)S(1)}, bf16[256,2048]{1,0:T(8,128)(2,1)S(1)}) custom-call(s32[8]{0:T(128)S(1)} %copy-done, s32[4]{0:T(128)S(1)} %pad_add_fusion.place_ref, bf16[4,8,16,256]{3,2,1,0:T(8,128)(2,1)S(1)} %get-tuple-element.31.t0, ...), custom_call_target="tpu_custom_call" | custom-call | flops 3221225472 | bytes 4194304 | tf_op jit(solution)/shard_map/first_targets/pallas_call | solution.py:249
  31.6 0.1 collective-permute-start.7
  31.7 1.8 %last_targets.1 = (f32[4,4,32,256]{3,2,1,0:T(8,128)S(1)}, bf16[4,4,32,256]{3,2,1,0:T(8,128)(2,1)S(1)}) custom-call(s32[8]{0:T(128)S(1)} %copy-done, bf16[256,2048]{1,0:T(8,128)(2,1)S(1)} %get-tuple-element.37.left_ref, bf16[8,5120,256]{2,1,0:T(8,128)(2,1)S(1)} %other_sectors.1.h_ref), custom_call_target="tpu_custom_call" | custom-call | flops 1073741824 | bytes 4194304 | tf_op jit(solution)/shard_map/last_targets/pallas_call | solution.py:252
  33.5 0.6 %collective-permute-start.8 = (bf16[4,4,32,256]{3,2,1,0:T(8,128)(2,1)S(1)}, bf16[4,4,32,256]{3,2,1,0:T(8,128)(2,1)S(1)}, u32[]{:S(2)}, u32[]{:S(2)}) collective-permute-start(bf16[4,4,32,256]{3,2,1,0:T(8,128)(2,1)S(1)} %get-tuple-element.40), channel_id=1, source_target_pairs={{0,16},{1,17},{2,18},{3,19},{4,20},{5,21},{6,22},{7,23},{8,24},{9,... | collective-permute-start | bytes 786440 | tf_op jit(solution)/shard_map/ppermute | solution.py:36
  34.0 1.2 %collective-permute-done.8.got_b = bf16[4,4,32,256]{3,2,1,0:T(8,128)(2,1)S(1)} collective-permute-done((bf16[4,4,32,256]{3,2,1,0:T(8,128)(2,1)S(1)}, bf16[4,4,32,256]{3,2,1,0:T(8,128)(2,1)S(1)}, u32[]{:S(2)}, u32[]{:S(2)}) %collective-permute-start.8) | collective-permute-done | bytes 262176 | tf_op jit(solution)/shard_map/ppermute | solution.py:36
  35.2 0.2 add_cores.1
  35.4 2.0 %collective-permute-start.10 = (bf16[16,32,256]{2,1,0:T(8,128)(2,1)S(1)}, bf16[16,32,256]{2,1,0:T(8,128)(2,1)S(1)}, u32[]{:S(2)}, u32[]{:S(2)}) collective-permute-start(bf16[16,32,256]{2,1,0:T(8,128)(2,1)S(1)} %get-tuple-element.44), channel_id=1, source_target_pairs={{0,32},{1,33},{2,34},{3,35},{4,36},{5,37},{6,38},{7,39},{8,40},{9,... | collective-permute-start | bytes 786440 | tf_op jit(solution)/shard_map/ppermute | solution.py:36
  37.4 2.2 %collective-permute-start.9 = (bf16[16,32,256]{2,1,0:T(8,128)(2,1)S(1)}, bf16[16,32,256]{2,1,0:T(8,128)(2,1)S(1)}, u32[]{:S(2)}, u32[]{:S(2)}) collective-permute-start(bf16[16,32,256]{2,1,0:T(8,128)(2,1)S(1)} %get-tuple-element.42), channel_id=1, source_target_pairs={{0,96},{1,97},{2,98},{3,99},{4,100},{5,101},{6,102},{7,103},{8,104... | collective-permute-start | bytes 786440 | tf_op jit(solution)/shard_map/ppermute | solution.py:36
  39.6 4.6 %collective-permute-done.10 = bf16[16,32,256]{2,1,0:T(8,128)(2,1)S(1)} collective-permute-done((bf16[16,32,256]{2,1,0:T(8,128)(2,1)S(1)}, bf16[16,32,256]{2,1,0:T(8,128)(2,1)S(1)}, u32[]{:S(2)}, u32[]{:S(2)}) %collective-permute-start.10) | collective-permute-done | bytes 262176 | tf_op jit(solution)/shard_map/ppermute | solution.py:36
  44.3 0.1 add_convert_fusion
  44.3 1.3 %collective-permute-start.11 = (bf16[16,32,256]{2,1,0:T(8,128)(2,1)S(1)}, bf16[16,32,256]{2,1,0:T(8,128)(2,1)S(1)}, u32[]{:S(2)}, u32[]{:S(2)}) collective-permute-start(bf16[16,32,256]{2,1,0:T(8,128)(2,1)S(1)} %add_convert_fusion), channel_id=1, source_target_pairs={{0,32},{1,33},{2,34},{3,35},{4,36},{5,37},{6,38},{7,39},{8,40},{9,... | collective-permute-start | bytes 786440 | tf_op jit(solution)/shard_map/ppermute | solution.py:36
  45.7 0.1 broadcast_compare_fusion
  45.8 0.1 iota_compare_fusion
  45.8 6.9 %collective-permute-done.11 = bf16[16,32,256]{2,1,0:T(8,128)(2,1)S(1)} collective-permute-done((bf16[16,32,256]{2,1,0:T(8,128)(2,1)S(1)}, bf16[16,32,256]{2,1,0:T(8,128)(2,1)S(1)}, u32[]{:S(2)}, u32[]{:S(2)}) %collective-permute-start.11) | collective-permute-done | bytes 262176 | tf_op jit(solution)/shard_map/ppermute | solution.py:36
  52.7 0.9 %select_convert_fusion = bf16[16,32,256]{2,1,0:T(8,128)(2,1)} fusion(bf16[16,32,256]{2,1,0:T(8,128)(2,1)S(1)} %collective-permute-done.11, f32[16,32,256]{2,1,0:T(8,128)S(1)} %get-tuple-element.41, bf16[16,32,256]{2,1,0:T(8,128)(2,1)S(1)} %collective-permute-done.9, pred[16,256]{1,0:T(8,128)(4,1)S(1)} %iota_compare_fusion, ...), kind=kLoop, calls=%fused_computation | loop fusion | flops 917504 | bytes 1315328 | tf_op jit(solution)/shard_map/convert_element_type | solution.py:268
  (11 shorter events, 0.0 us)
Async XLA Ops:
  0.0 6.7 %copy-start.1 = (bf16[8,16,256]{2,1,0:T(8,128)(2,1)S(1)}, bf16[8,16,256]{2,1,0:T(8,128)(2,1)}, u32[]{:S(2)}) copy-start(bf16[8,16,256]{2,1,0:T(8,128)(2,1)} %left_ref.1) | copy-start | bytes 196612
  1.3 13.4 %collective-permute-start = (bf16[640,256]{1,0:T(8,128)(2,1)S(1)}, bf16[640,256]{1,0:T(8,128)(2,1)S(1)}, u32[]{:S(2)}, u32[]{:S(2)}) collective-permute-start(bf16[640,256]{1,0:T(8,128)(2,1)S(1)} %get-tuple-element.27.own), channel_id=1, source_target_pairs={{0,1},{1,2},{2,3},{3,4},{4,5},{5,6},{6,7},{7,8},{8,9},{9,10},{10,1... | collective-permute-start | bytes 983048 | tf_op jit(solution)/shard_map/ppermute | solution.py:36
  2.9 16.0 %copy-start = (s32[8]{0:T(128)S(1)}, s32[8]{0:T(128)}, u32[]{:S(2)}) copy-start(s32[8]{0:T(128)} %shift_ref.5) | copy-start | bytes 100
  2.9 11.8 %collective-permute-start.1 = (bf16[640,256]{1,0:T(8,128)(2,1)S(1)}, bf16[640,256]{1,0:T(8,128)(2,1)S(1)}, u32[]{:S(2)}, u32[]{:S(2)}) collective-permute-start(bf16[640,256]{1,0:T(8,128)(2,1)S(1)} %get-tuple-element.28), channel_id=1, source_target_pairs={{0,15},{1,0},{2,1},{3,2},{4,3},{5,4},{6,5},{7,6},{8,7},{9,8},{10,9... | collective-permute-start | bytes 983048 | tf_op jit(solution)/shard_map/ppermute | solution.py:36
  6.7 8.0 %collective-permute-start.2 = (bf16[8,16,256]{2,1,0:T(8,128)(2,1)S(1)}, bf16[8,16,256]{2,1,0:T(8,128)(2,1)S(1)}, u32[]{:S(2)}, u32[]{:S(2)}) collective-permute-start(bf16[8,16,256]{2,1,0:T(8,128)(2,1)S(1)} %copy-done.1), channel_id=1, source_target_pairs={{0,2},{1,3},{2,4},{3,5},{4,6},{5,7},{6,8},{7,9},{8,10},{9,11},{10,... | collective-permute-start | bytes 196616 | tf_op jit(solution)/shard_map/ppermute | solution.py:36
  15.4 3.5 %collective-permute-start.6 = (bf16[1024,256]{1,0:T(8,128)(2,1)S(1)}, bf16[1024,256]{1,0:T(8,128)(2,1)S(1)}, u32[]{:S(2)}, u32[]{:S(2)}) collective-permute-start(bf16[1024,256]{1,0:T(8,128)(2,1)S(1)} %get-tuple-element.32.edge_own), channel_id=1, source_target_pairs={{0,16},{1,17},{2,18},{3,19},{4,20},{5,21},{6,22},{7,23},{8,24},{9,... | collective-permute-start | bytes 1572872 | tf_op jit(solution)/shard_map/ppermute | solution.py:36
  15.5 10.5 %collective-permute-start.3 = (bf16[4,8,16,256]{3,2,1,0:T(8,128)(2,1)S(1)}, bf16[4,8,16,256]{3,2,1,0:T(8,128)(2,1)S(1)}, u32[]{:S(2)}, u32[]{:S(2)}) collective-permute-start(bf16[4,8,16,256]{3,2,1,0:T(8,128)(2,1)S(1)} %get-tuple-element.31.t0), channel_id=1, source_target_pairs={{0,4},{1,5},{2,6},{3,7},{4,8},{5,9},{6,10},{7,11},{8,12},{9,13},{1... | collective-permute-start | bytes 786440 | tf_op jit(solution)/shard_map/ppermute | solution.py:36
  15.5 10.4 %collective-permute-start.4 = (bf16[4,8,16,256]{3,2,1,0:T(8,128)(2,1)S(1)}, bf16[4,8,16,256]{3,2,1,0:T(8,128)(2,1)S(1)}, u32[]{:S(2)}, u32[]{:S(2)}) collective-permute-start(bf16[4,8,16,256]{3,2,1,0:T(8,128)(2,1)S(1)} %get-tuple-element.31.t0), channel_id=1, source_target_pairs={{0,8},{1,9},{2,10},{3,11},{4,12},{5,13},{6,14},{7,15},{8,0},{9,1},... | collective-permute-start | bytes 786440 | tf_op jit(solution)/shard_map/ppermute | solution.py:36
  17.6 9.3 %collective-permute-start.5 = (bf16[4,8,16,256]{3,2,1,0:T(8,128)(2,1)S(1)}, bf16[4,8,16,256]{3,2,1,0:T(8,128)(2,1)S(1)}, u32[]{:S(2)}, u32[]{:S(2)}) collective-permute-start(bf16[4,8,16,256]{3,2,1,0:T(8,128)(2,1)S(1)} %get-tuple-element.31.t0), channel_id=1, source_target_pairs={{0,12},{1,13},{2,14},{3,15},{4,0},{5,1},{6,2},{7,3},{8,4},{9,5},{1... | collective-permute-start | bytes 786440 | tf_op jit(solution)/shard_map/ppermute | solution.py:36
  31.6 3.6 %collective-permute-start.7 = (bf16[4,12,32,256]{3,2,1,0:T(8,128)(2,1)S(1)}, bf16[4,12,32,256]{3,2,1,0:T(8,128)(2,1)S(1)}, u32[]{:S(2)}, u32[]{:S(2)}) collective-permute-start(bf16[4,12,32,256]{3,2,1,0:T(8,128)(2,1)S(1)} %get-tuple-element.39), channel_id=1, source_target_pairs={{0,16},{1,17},{2,18},{3,19},{4,20},{5,21},{6,22},{7,23},{8,24},{9,... | collective-permute-start | bytes 2359304 | tf_op jit(solution)/shard_map/ppermute | solution.py:36
  33.5 1.7 %collective-permute-start.8 = (bf16[4,4,32,256]{3,2,1,0:T(8,128)(2,1)S(1)}, bf16[4,4,32,256]{3,2,1,0:T(8,128)(2,1)S(1)}, u32[]{:S(2)}, u32[]{:S(2)}) collective-permute-start(bf16[4,4,32,256]{3,2,1,0:T(8,128)(2,1)S(1)} %get-tuple-element.40), channel_id=1, source_target_pairs={{0,16},{1,17},{2,18},{3,19},{4,20},{5,21},{6,22},{7,23},{8,24},{9,... | collective-permute-start | bytes 786440 | tf_op jit(solution)/shard_map/ppermute | solution.py:36
  35.2 10.5 %copy-start.2 = (s32[16]{0:T(128)S(1)}, s32[16]{0:T(128)}, u32[]{:S(2)}) copy-start(s32[16]{0:T(128)} %dims_ref.3) | copy-start | bytes 196
  35.4 8.8 %collective-permute-start.10 = (bf16[16,32,256]{2,1,0:T(8,128)(2,1)S(1)}, bf16[16,32,256]{2,1,0:T(8,128)(2,1)S(1)}, u32[]{:S(2)}, u32[]{:S(2)}) collective-permute-start(bf16[16,32,256]{2,1,0:T(8,128)(2,1)S(1)} %get-tuple-element.44), channel_id=1, source_target_pairs={{0,32},{1,33},{2,34},{3,35},{4,36},{5,37},{6,38},{7,39},{8,40},{9,... | collective-permute-start | bytes 786440 | tf_op jit(solution)/shard_map/ppermute | solution.py:36
  37.4 8.4 %collective-permute-start.9 = (bf16[16,32,256]{2,1,0:T(8,128)(2,1)S(1)}, bf16[16,32,256]{2,1,0:T(8,128)(2,1)S(1)}, u32[]{:S(2)}, u32[]{:S(2)}) collective-permute-start(bf16[16,32,256]{2,1,0:T(8,128)(2,1)S(1)} %get-tuple-element.42), channel_id=1, source_target_pairs={{0,96},{1,97},{2,98},{3,99},{4,100},{5,101},{6,102},{7,103},{8,104... | collective-permute-start | bytes 786440 | tf_op jit(solution)/shard_map/ppermute | solution.py:36
  44.3 8.4 %collective-permute-start.11 = (bf16[16,32,256]{2,1,0:T(8,128)(2,1)S(1)}, bf16[16,32,256]{2,1,0:T(8,128)(2,1)S(1)}, u32[]{:S(2)}, u32[]{:S(2)}) collective-permute-start(bf16[16,32,256]{2,1,0:T(8,128)(2,1)S(1)} %add_convert_fusion), channel_id=1, source_target_pairs={{0,32},{1,33},{2,34},{3,35},{4,36},{5,37},{6,38},{7,39},{8,40},{9,... | collective-permute-start | bytes 786440 | tf_op jit(solution)/shard_map/ppermute | solution.py:36

commit v6 on v5

--- a/solution.py
+++ b/solution.py
@@ -74,15 +74,11 @@
         down_ref[to, :] = masked(first_psi[e], dims_ref[e])
 
 
-def unpack(place_ref, own, from_below, from_above, second_below, after, strips_ref, edges_ref):
+def unpack(own, from_below, from_above, second_below, after, strips_ref):
     strips_ref[0] = own[:STRIP, :].reshape(OPS, 16, B)
     strips_ref[1] = from_below[:STRIP, :].reshape(OPS, 16, B)
     strips_ref[2] = from_above[:STRIP, :].reshape(OPS, 16, B)
     strips_ref[3] = second_below[...]
-    q = place_ref[2] * NX + place_ref[3]
-    for k, (source, present) in enumerate(((from_below, q > 0), (from_above, q < SECS - 1))):
-        keep = jnp.broadcast_to(present.astype(jnp.int32), (QMAX * B, B)) > 0
-        edges_ref[k * QMAX * B:(k + 1) * QMAX * B, :] = jnp.where(keep, source[STRIP:, :].astype(F32), 0.0).astype(BF)
 
 
 def by_twos(one, ops=(0, OPS)):
@@ -127,16 +123,20 @@
     done_ref[...] = jnp.zeros_like(done_ref)
 
 
-def other_sectors(shift_ref, place_ref, edge_own, edge_other, masked_ref, right_ref, _, h_ref, edge_ref):
+def other_sectors(shift_ref, place_ref, below_0, above_0, below_1, above_1, masked_ref, right_ref, _, h_ref, edge_ref):
     core = place_ref[1]
-
-    @pl.when(core == 0)
-    def _():
-        edge_ref[...] = edge_own[...]
-
-    @pl.when(core == 1)
-    def _():
-        edge_ref[...] = edge_other[...]
+    q = place_ref[2] * NX + place_ref[3]
+    for k, (sources, present) in enumerate((((below_0, below_1), q > 0), ((above_0, above_1), q < SECS - 1))):
+        to = slice(k * QMAX * B, (k + 1) * QMAX * B)
+        for c, source in enumerate(sources):
+
+            @pl.when(present & (core == c))
+            def _():
+                edge_ref[to, :] = source[STRIP:, :]
+
+        @pl.when(jnp.logical_not(present))
+        def _():
+            edge_ref[to, :] = jnp.zeros((QMAX * B, B), BF)
 
     def edge_side(o):
         above = (shift_ref[o] < 0).astype(jnp.int32)
@@ -167,9 +167,12 @@
 
 
 def some_targets(first, shift_ref, left_ref, h_ref, mine_ref, other_ref):
-    def four_targets(i, _):
-        for u in range(4):
-            t = i * 4 + u
+    count = mine_ref.shape[1]
+    at_once = min(count, 6)
+
+    def several_targets(i, _):
+        for u in range(at_once):
+            t = i * at_once + u
             sources = [
                 h_ref[o, pl.ds(pl.multiple_of((first + t + QMAX - shift_ref[o]) * B, B), B), :] for o in range(OPS)
             ]
@@ -179,7 +182,7 @@
                 other_ref[k, t] = total[B // 2 + k * 32:B // 2 + (k + 1) * 32].astype(BF)
         return 0
 
-    lax.fori_loop(0, mine_ref.shape[1] // 4, four_targets, 0)
+    lax.fori_loop(0, count // at_once, several_targets, 0)
 
 
 def first_targets(shift_ref, place_ref, t0, t1, t2, t3, h_ref, mine_ref, other_ref, left_ref):
@@ -233,17 +236,16 @@
         [((SECS, B, B), BF), ((OPS, B, B), BF), ((OPS, HELD * B, B), BF), ((8, 128), F32)], EARLY * SECS,
         [pltpu.SemaphoreType.DMA((SECS,)), pltpu.SemaphoreType.DMA],
     )(dims_there, psi_there, right_there)
-    strips, edges = call(
-        unpack, "unpack", [smem] + [vmem] * 5, [((4, OPS, 16, B), BF), ((2 * QMAX * B, B), BF)], 0,
-    )(place, sent, up, down, two, done)
-    seconds = [move(strips, gather_second(d)) for d in (1, 3, 2)]
-    t0, t1, t3, t2 = strips, *seconds
-    edges_other = move(edges, other_core)
+    strips, = call(unpack, "unpack", [vmem] * 5, [((4, OPS, 16, B), BF)], 0)(sent, up, down, two, done)
+    up_late, down_late, _ = lax.optimization_barrier((up, down, strips))
+    up_other, down_other = move(up_late, other_core), move(down_late, other_core)
+    seconds = [move(strips, gather_second(d)) for d in (2, 1, 3)]
+    t0, t2, t1, t3 = strips, *seconds
 
     h, = call(
-        other_sectors, "other_sectors", [smem, smem] + [vmem] * 5, [((OPS, HELD * B, B), BF)], 0,
-        [pltpu.VMEM((2 * QMAX * B, B), BF)], {6: 0},
-    )(op_shift, place, edges, edges_other, live_psi, right, h)
+        other_sectors, "other_sectors", [smem, smem] + [vmem] * 7, [((OPS, HELD * B, B), BF)], 0,
+        [pltpu.VMEM((2 * QMAX * B, B), BF)], {8: 0},
+    )(op_shift, place, up, down, up_other, down_other, live_psi, right, h)
 
     first_a = [((NZ, SPLIT, 32, B), F32), ((NZ, SPLIT, 32, B), BF), ((B, OPS * B), BF)]
     mine_a, away_a, left = call(first_targets, "first_targets", [smem, smem] + [vmem] * 5, first_a, OPS * SPLIT)(

time: 53.9 us -> 53.5 us (level)
  Pallas kernels: 17.9 us -> 17.1 us
    pallas_call x2, Pallas kernels: 4.53 us -> 3.93 us  [the longest x1 3.91 us: on_device(): call(other_sectors, 'other_sectors', [smem, smem] + [vmem] * 7, [((OPS, H...]
    ppermute x12 -> x13, starting transfers between devices: 15.1 us -> 15.5 us  [move(): return lax.ppermute(block, ('op', 'sec'), route)]
    ppermute x12 -> x13, waiting for transfers between devices: 19.4 us -> 19.3 us  [move(): return lax.ppermute(block, ('op', 'sec'), route)]
  transfers between devices with their start and end apart: 12 -> 13, of which waited for: 6 -> 6; matrix products, arithmetic and copies ran while one was open for 0% -> 0% of each run, Pallas kernels for 21% -> 21%
where the time goes in v6:
time: 53.5 us; the launch traced here: 53.2 us
  waiting for transfers between devices  19.3 us (36%)
  Pallas kernels  17.1 us (32%)
  starting transfers between devices  15.5 us (29%)
  other arithmetic  1.16 us (2%)
    ppermute x13, waiting for transfers between devices, move(): return lax.ppermute(block, ('op', 'sec'), route)  19.3 us
    ppermute x13, starting transfers between devices, move(): return lax.ppermute(block, ('op', 'sec'), route)  15.5 us
    pallas_call x1, Pallas kernels, on_device(): call(first_operators, 'first_operators', [smem, hbm, hbm], [((SECS, B, B)...  5.36 us
    pallas_call x1, Pallas kernels, on_device(): call(first_targets, 'first_targets', [smem, smem] + [vmem] * 5, first_a,...  4.56 us
    pallas_call x1, Pallas kernels, on_device(): call(other_sectors, 'other_sectors', [smem, smem] + [vmem] * 7, [((OPS, H...  3.91 us
    pallas_call x1, Pallas kernels, on_device(): call(functools.partial(some_targets, SPLIT), 'last_targets', [smem, vmem,...  1.79 us
    pallas_call x1, Pallas kernels, on_device(): pl.pallas_call(pack, grid=(1,), in_specs=[smem, *ends, pl.BlockSpec((OPS,...  1.22 us
  transfers between devices with their start and end apart: 13, of which 6 were waited for; matrix products, arithmetic and copies ran while one was open for 0% of the time, Pallas kernels for 21%

profile of v6, /device:TPU:0, one launch (start us, length us, event | category | flops | bytes accessed | tf_op | source)
XLA Modules:
  0.0 53.2 jit_solution(1826262704636533087)
XLA Ops:
  0.0 1.2 %pack.1 = (bf16[640,256]{1,0:T(8,128)(2,1)S(1)}, bf16[640,256]{1,0:T(8,128)(2,1)S(1)}) custom-call(s32[16]{0:T(128)} %dims_ref.3, bf16[16,256,256]{2,1,0:T(8,128)(2,1)} %psi_hbm.1, bf16[16,256,256]{2,1,0:T(8,128)(2,1)} %psi_hbm.1, bf16[8,16,256]{2,1,0:T(8,128)(2,1)} %left_ref.1), custom_call_target="tpu_custom_call" | custom-call | bytes 1048576 | tf_op jit(solution)/shard_map/pack/pallas_call | solution.py:223
  1.2 0.1 pad_add_fusion.place_ref
  1.3 1.6 %collective-permute-start = (bf16[640,256]{1,0:T(8,128)(2,1)S(1)}, bf16[640,256]{1,0:T(8,128)(2,1)S(1)}, u32[]{:S(2)}, u32[]{:S(2)}) collective-permute-start(bf16[640,256]{1,0:T(8,128)(2,1)S(1)} %get-tuple-element.27.own), channel_id=1, source_target_pairs={{0,1},{1,2},{2,3},{3,4},{4,5},{5,6},{6,7},{7,8},{8,9},{9,10},{10,1... | collective-permute-start | bytes 983048 | tf_op jit(solution)/shard_map/ppermute | solution.py:36
  2.9 3.8 %collective-permute-start.1 = (bf16[640,256]{1,0:T(8,128)(2,1)S(1)}, bf16[640,256]{1,0:T(8,128)(2,1)S(1)}, u32[]{:S(2)}, u32[]{:S(2)}) collective-permute-start(bf16[640,256]{1,0:T(8,128)(2,1)S(1)} %get-tuple-element.28), channel_id=1, source_target_pairs={{0,15},{1,0},{2,1},{3,2},{4,3},{5,4},{6,5},{7,6},{8,7},{9,8},{10,9... | collective-permute-start | bytes 983048 | tf_op jit(solution)/shard_map/ppermute | solution.py:36
  6.7 5.4 %first_operators.1 = (bf16[16,256,256]{2,1,0:T(8,128)(2,1)S(1)}, bf16[8,256,256]{2,1,0:T(8,128)(2,1)S(1)}, bf16[8,5120,256]{2,1,0:T(8,128)(2,1)S(1)}, f32[8,128]{1,0:T(8,128)S(1)}) custom-call(s32[16]{0:T(128)} %dims_ref.3, bf16[16,256,256]{2,1,0:T(8,128)(2,1)} %psi_hbm.1, bf16[8,256,256]{2,1,0:T(8,128)(2,1)} %right_hbm.1), custom_call_target="tpu_custom_call" | custom-call | flops 2147483648 | bytes 4194304 | tf_op jit(solution)/shard_map/first_operators/pallas_call | solution.py:234
  12.1 2.6 %collective-permute-done.2.second_below = bf16[8,16,256]{2,1,0:T(8,128)(2,1)S(1)} collective-permute-done((bf16[8,16,256]{2,1,0:T(8,128)(2,1)S(1)}, bf16[8,16,256]{2,1,0:T(8,128)(2,1)S(1)}, u32[]{:S(2)}, u32[]{:S(2)}) %collective-permute-start.2) | collective-permute-done | bytes 65568 | tf_op jit(solution)/shard_map/ppermute | solution.py:36
  14.7 0.0 collective-permute-done.from_below.below_0
  14.7 0.0 collective-permute-done.1.from_above.above_0
  14.7 0.1 collective-permute-start.6
  14.8 0.5 collective-permute-start.7
  15.3 2.0 %collective-permute-start.4 = (bf16[4,8,16,256]{3,2,1,0:T(8,128)(2,1)S(1)}, bf16[4,8,16,256]{3,2,1,0:T(8,128)(2,1)S(1)}, u32[]{:S(2)}, u32[]{:S(2)}) collective-permute-start(bf16[4,8,16,256]{3,2,1,0:T(8,128)(2,1)S(1)} %unpack.1.t0), channel_id=1, source_target_pairs={{0,8},{1,9},{2,10},{3,11},{4,12},{5,13},{6,14},{7,15},{8,0},{9,1},... | collective-permute-start | bytes 786440 | tf_op jit(solution)/shard_map/ppermute | solution.py:36
  17.4 1.3 %collective-permute-start.5 = (bf16[4,8,16,256]{3,2,1,0:T(8,128)(2,1)S(1)}, bf16[4,8,16,256]{3,2,1,0:T(8,128)(2,1)S(1)}, u32[]{:S(2)}, u32[]{:S(2)}) collective-permute-start(bf16[4,8,16,256]{3,2,1,0:T(8,128)(2,1)S(1)} %unpack.1.t0), channel_id=1, source_target_pairs={{0,12},{1,13},{2,14},{3,15},{4,0},{5,1},{6,2},{7,3},{8,4},{9,5},{1... | collective-permute-start | bytes 786440 | tf_op jit(solution)/shard_map/ppermute | solution.py:36
  18.7 0.0 collective-permute-done.6.below_1
  18.7 0.0 collective-permute-done.7.above_1
  18.7 3.9 %other_sectors.1.h_ref = bf16[8,5120,256]{2,1,0:T(8,128)(2,1)S(1)} custom-call(s32[8]{0:T(128)S(1)} %copy-done, s32[4]{0:T(128)S(1)} %pad_add_fusion.place_ref, bf16[640,256]{1,0:T(8,128)(2,1)S(1)} %collective-permute-done.from_below.below_0, bf16[640,256]{1,0:T(8,128)(2,1)S(1)} %collective-permute-done.1.from_above.above_0, ...), custom_call_target="tpu_custom_call", output_to_operand_aliasing={{}: (8, {})} | custom-call | tf_op jit(solution)/shard_map/other_sectors/pallas_call | solution.py:245
  22.6 3.1 %collective-permute-done.3.t1 = bf16[4,8,16,256]{3,2,1,0:T(8,128)(2,1)S(1)} collective-permute-done((bf16[4,8,16,256]{3,2,1,0:T(8,128)(2,1)S(1)}, bf16[4,8,16,256]{3,2,1,0:T(8,128)(2,1)S(1)}, u32[]{:S(2)}, u32[]{:S(2)}) %collective-permute-start.3) | collective-permute-done | bytes 262176 | tf_op jit(solution)/shard_map/ppermute | solution.py:36
  25.7 0.9 %collective-permute-done.5.t3 = bf16[4,8,16,256]{3,2,1,0:T(8,128)(2,1)S(1)} collective-permute-done((bf16[4,8,16,256]{3,2,1,0:T(8,128)(2,1)S(1)}, bf16[4,8,16,256]{3,2,1,0:T(8,128)(2,1)S(1)}, u32[]{:S(2)}, u32[]{:S(2)}) %collective-permute-start.5) | collective-permute-done | bytes 262176 | tf_op jit(solution)/shard_map/ppermute | solution.py:36
  26.6 4.6 %first_targets.1 = (f32[4,12,32,256]{3,2,1,0:T(8,128)S(1)}, bf16[4,12,32,256]{3,2,1,0:T(8,128)(2,1)S(1)}, bf16[256,2048]{1,0:T(8,128)(2,1)S(1)}) custom-call(s32[8]{0:T(128)S(1)} %copy-done, s32[4]{0:T(128)S(1)} %pad_add_fusion.place_ref, bf16[4,8,16,256]{3,2,1,0:T(8,128)(2,1)S(1)} %unpack.1.t0, bf16[4,8,16,256]{3,2,1,0:T(8,128)(2,1)S(1)} %collective-permute-done.3.t1, ...), custom_call_target="tpu_custom_call" | custom-call | flops 3221225472 | bytes 4194304 | tf_op jit(solution)/shard_map/first_targets/pallas_call | solution.py:251
  31.2 0.1 collective-permute-start.8
  31.3 1.8 %last_targets.1 = (f32[4,4,32,256]{3,2,1,0:T(8,128)S(1)}, bf16[4,4,32,256]{3,2,1,0:T(8,128)(2,1)S(1)}) custom-call(s32[8]{0:T(128)S(1)} %copy-done, bf16[256,2048]{1,0:T(8,128)(2,1)S(1)} %get-tuple-element.37.left_ref, bf16[8,5120,256]{2,1,0:T(8,128)(2,1)S(1)} %other_sectors.1.h_ref), custom_call_target="tpu_custom_call" | custom-call | flops 1073741824 | bytes 4194304 | tf_op jit(solution)/shard_map/last_targets/pallas_call | solution.py:254
  33.1 0.6 %collective-permute-start.9 = (bf16[4,4,32,256]{3,2,1,0:T(8,128)(2,1)S(1)}, bf16[4,4,32,256]{3,2,1,0:T(8,128)(2,1)S(1)}, u32[]{:S(2)}, u32[]{:S(2)}) collective-permute-start(bf16[4,4,32,256]{3,2,1,0:T(8,128)(2,1)S(1)} %get-tuple-element.40), channel_id=1, source_target_pairs={{0,16},{1,17},{2,18},{3,19},{4,20},{5,21},{6,22},{7,23},{8,24},{9,... | collective-permute-start | bytes 786440 | tf_op jit(solution)/shard_map/ppermute | solution.py:36
  33.7 1.2 %collective-permute-done.9.got_b = bf16[4,4,32,256]{3,2,1,0:T(8,128)(2,1)S(1)} collective-permute-done((bf16[4,4,32,256]{3,2,1,0:T(8,128)(2,1)S(1)}, bf16[4,4,32,256]{3,2,1,0:T(8,128)(2,1)S(1)}, u32[]{:S(2)}, u32[]{:S(2)}) %collective-permute-start.9) | collective-permute-done | bytes 262176 | tf_op jit(solution)/shard_map/ppermute | solution.py:36
  34.8 0.2 add_cores.1
  35.1 2.0 %collective-permute-start.11 = (bf16[16,32,256]{2,1,0:T(8,128)(2,1)S(1)}, bf16[16,32,256]{2,1,0:T(8,128)(2,1)S(1)}, u32[]{:S(2)}, u32[]{:S(2)}) collective-permute-start(bf16[16,32,256]{2,1,0:T(8,128)(2,1)S(1)} %get-tuple-element.44), channel_id=1, source_target_pairs={{0,32},{1,33},{2,34},{3,35},{4,36},{5,37},{6,38},{7,39},{8,40},{9,... | collective-permute-start | bytes 786440 | tf_op jit(solution)/shard_map/ppermute | solution.py:36
  37.0 2.2 %collective-permute-start.10 = (bf16[16,32,256]{2,1,0:T(8,128)(2,1)S(1)}, bf16[16,32,256]{2,1,0:T(8,128)(2,1)S(1)}, u32[]{:S(2)}, u32[]{:S(2)}) collective-permute-start(bf16[16,32,256]{2,1,0:T(8,128)(2,1)S(1)} %get-tuple-element.42), channel_id=1, source_target_pairs={{0,96},{1,97},{2,98},{3,99},{4,100},{5,101},{6,102},{7,103},{8,104... | collective-permute-start | bytes 786440 | tf_op jit(solution)/shard_map/ppermute | solution.py:36
  39.3 4.6 %collective-permute-done.11 = bf16[16,32,256]{2,1,0:T(8,128)(2,1)S(1)} collective-permute-done((bf16[16,32,256]{2,1,0:T(8,128)(2,1)S(1)}, bf16[16,32,256]{2,1,0:T(8,128)(2,1)S(1)}, u32[]{:S(2)}, u32[]{:S(2)}) %collective-permute-start.11) | collective-permute-done | bytes 262176 | tf_op jit(solution)/shard_map/ppermute | solution.py:36
  43.9 0.1 add_convert_fusion
  44.0 1.3 %collective-permute-start.12 = (bf16[16,32,256]{2,1,0:T(8,128)(2,1)S(1)}, bf16[16,32,256]{2,1,0:T(8,128)(2,1)S(1)}, u32[]{:S(2)}, u32[]{:S(2)}) collective-permute-start(bf16[16,32,256]{2,1,0:T(8,128)(2,1)S(1)} %add_convert_fusion), channel_id=1, source_target_pairs={{0,32},{1,33},{2,34},{3,35},{4,36},{5,37},{6,38},{7,39},{8,40},{9,... | collective-permute-start | bytes 786440 | tf_op jit(solution)/shard_map/ppermute | solution.py:36
  45.3 0.1 broadcast_compare_fusion
  45.4 0.1 iota_compare_fusion
  45.5 6.9 %collective-permute-done.12 = bf16[16,32,256]{2,1,0:T(8,128)(2,1)S(1)} collective-permute-done((bf16[16,32,256]{2,1,0:T(8,128)(2,1)S(1)}, bf16[16,32,256]{2,1,0:T(8,128)(2,1)S(1)}, u32[]{:S(2)}, u32[]{:S(2)}) %collective-permute-start.12) | collective-permute-done | bytes 262176 | tf_op jit(solution)/shard_map/ppermute | solution.py:36
  52.4 0.9 %select_convert_fusion = bf16[16,32,256]{2,1,0:T(8,128)(2,1)} fusion(bf16[16,32,256]{2,1,0:T(8,128)(2,1)S(1)} %collective-permute-done.12, f32[16,32,256]{2,1,0:T(8,128)S(1)} %get-tuple-element.41, bf16[16,32,256]{2,1,0:T(8,128)(2,1)S(1)} %collective-permute-done.10, pred[16,256]{1,0:T(8,128)(4,1)S(1)} %iota_compare_fusion, ...), kind=kLoop, calls=%fused_computation | loop fusion | flops 917504 | bytes 1315328 | tf_op jit(solution)/shard_map/convert_element_type | solution.py:270
  (13 shorter events, 0.0 us)
Async XLA Ops:
  0.0 6.7 %copy-start.1 = (bf16[8,16,256]{2,1,0:T(8,128)(2,1)S(1)}, bf16[8,16,256]{2,1,0:T(8,128)(2,1)}, u32[]{:S(2)}) copy-start(bf16[8,16,256]{2,1,0:T(8,128)(2,1)} %left_ref.1) | copy-start | bytes 196612
  1.3 13.4 %collective-permute-start = (bf16[640,256]{1,0:T(8,128)(2,1)S(1)}, bf16[640,256]{1,0:T(8,128)(2,1)S(1)}, u32[]{:S(2)}, u32[]{:S(2)}) collective-permute-start(bf16[640,256]{1,0:T(8,128)(2,1)S(1)} %get-tuple-element.27.own), channel_id=1, source_target_pairs={{0,1},{1,2},{2,3},{3,4},{4,5},{5,6},{6,7},{7,8},{8,9},{9,10},{10,1... | collective-permute-start | bytes 983048 | tf_op jit(solution)/shard_map/ppermute | solution.py:36
  2.9 15.8 %copy-start = (s32[8]{0:T(128)S(1)}, s32[8]{0:T(128)}, u32[]{:S(2)}) copy-start(s32[8]{0:T(128)} %shift_ref.5) | copy-start | bytes 100
  2.9 11.8 %collective-permute-start.1 = (bf16[640,256]{1,0:T(8,128)(2,1)S(1)}, bf16[640,256]{1,0:T(8,128)(2,1)S(1)}, u32[]{:S(2)}, u32[]{:S(2)}) collective-permute-start(bf16[640,256]{1,0:T(8,128)(2,1)S(1)} %get-tuple-element.28), channel_id=1, source_target_pairs={{0,15},{1,0},{2,1},{3,2},{4,3},{5,4},{6,5},{7,6},{8,7},{9,8},{10,9... | collective-permute-start | bytes 983048 | tf_op jit(solution)/shard_map/ppermute | solution.py:36
  6.7 8.0 %collective-permute-start.2 = (bf16[8,16,256]{2,1,0:T(8,128)(2,1)S(1)}, bf16[8,16,256]{2,1,0:T(8,128)(2,1)S(1)}, u32[]{:S(2)}, u32[]{:S(2)}) collective-permute-start(bf16[8,16,256]{2,1,0:T(8,128)(2,1)S(1)} %copy-done.1), channel_id=1, source_target_pairs={{0,2},{1,3},{2,4},{3,5},{4,6},{5,7},{6,8},{7,9},{8,10},{9,11},{10,... | collective-permute-start | bytes 196616 | tf_op jit(solution)/shard_map/ppermute | solution.py:36
  14.7 4.0 %collective-permute-start.6 = (bf16[640,256]{1,0:T(8,128)(2,1)S(1)}, bf16[640,256]{1,0:T(8,128)(2,1)S(1)}, u32[]{:S(2)}, u32[]{:S(2)}) collective-permute-start(bf16[640,256]{1,0:T(8,128)(2,1)S(1)} %collective-permute-done.from_below.below_0), channel_id=1, source_target_pairs={{0,16},{1,17},{2,18},{3,19},{4,20},{5,21},{6,22},{7,23},{8,24},{9,... | collective-permute-start | bytes 983048 | tf_op jit(solution)/shard_map/ppermute | solution.py:36
  14.8 3.9 %collective-permute-start.7 = (bf16[640,256]{1,0:T(8,128)(2,1)S(1)}, bf16[640,256]{1,0:T(8,128)(2,1)S(1)}, u32[]{:S(2)}, u32[]{:S(2)}) collective-permute-start(bf16[640,256]{1,0:T(8,128)(2,1)S(1)} %collective-permute-done.1.from_above.above_0), channel_id=1, source_target_pairs={{0,16},{1,17},{2,18},{3,19},{4,20},{5,21},{6,22},{7,23},{8,24},{9,... | collective-permute-start | bytes 983048 | tf_op jit(solution)/shard_map/ppermute | solution.py:36
  15.3 10.4 %collective-permute-start.3 = (bf16[4,8,16,256]{3,2,1,0:T(8,128)(2,1)S(1)}, bf16[4,8,16,256]{3,2,1,0:T(8,128)(2,1)S(1)}, u32[]{:S(2)}, u32[]{:S(2)}) collective-permute-start(bf16[4,8,16,256]{3,2,1,0:T(8,128)(2,1)S(1)} %unpack.1.t0), channel_id=1, source_target_pairs={{0,4},{1,5},{2,6},{3,7},{4,8},{5,9},{6,10},{7,11},{8,12},{9,13},{1... | collective-permute-start | bytes 786440 | tf_op jit(solution)/shard_map/ppermute | solution.py:36
  15.3 10.4 %collective-permute-start.4 = (bf16[4,8,16,256]{3,2,1,0:T(8,128)(2,1)S(1)}, bf16[4,8,16,256]{3,2,1,0:T(8,128)(2,1)S(1)}, u32[]{:S(2)}, u32[]{:S(2)}) collective-permute-start(bf16[4,8,16,256]{3,2,1,0:T(8,128)(2,1)S(1)} %unpack.1.t0), channel_id=1, source_target_pairs={{0,8},{1,9},{2,10},{3,11},{4,12},{5,13},{6,14},{7,15},{8,0},{9,1},... | collective-permute-start | bytes 786440 | tf_op jit(solution)/shard_map/ppermute | solution.py:36
  17.4 9.3 %collective-permute-start.5 = (bf16[4,8,16,256]{3,2,1,0:T(8,128)(2,1)S(1)}, bf16[4,8,16,256]{3,2,1,0:T(8,128)(2,1)S(1)}, u32[]{:S(2)}, u32[]{:S(2)}) collective-permute-start(bf16[4,8,16,256]{3,2,1,0:T(8,128)(2,1)S(1)} %unpack.1.t0), channel_id=1, source_target_pairs={{0,12},{1,13},{2,14},{3,15},{4,0},{5,1},{6,2},{7,3},{8,4},{9,5},{1... | collective-permute-start | bytes 786440 | tf_op jit(solution)/shard_map/ppermute | solution.py:36
  31.2 3.6 %collective-permute-start.8 = (bf16[4,12,32,256]{3,2,1,0:T(8,128)(2,1)S(1)}, bf16[4,12,32,256]{3,2,1,0:T(8,128)(2,1)S(1)}, u32[]{:S(2)}, u32[]{:S(2)}) collective-permute-start(bf16[4,12,32,256]{3,2,1,0:T(8,128)(2,1)S(1)} %get-tuple-element.39), channel_id=1, source_target_pairs={{0,16},{1,17},{2,18},{3,19},{4,20},{5,21},{6,22},{7,23},{8,24},{9,... | collective-permute-start | bytes 2359304 | tf_op jit(solution)/shard_map/ppermute | solution.py:36
  33.1 1.7 %collective-permute-start.9 = (bf16[4,4,32,256]{3,2,1,0:T(8,128)(2,1)S(1)}, bf16[4,4,32,256]{3,2,1,0:T(8,128)(2,1)S(1)}, u32[]{:S(2)}, u32[]{:S(2)}) collective-permute-start(bf16[4,4,32,256]{3,2,1,0:T(8,128)(2,1)S(1)} %get-tuple-element.40), channel_id=1, source_target_pairs={{0,16},{1,17},{2,18},{3,19},{4,20},{5,21},{6,22},{7,23},{8,24},{9,... | collective-permute-start | bytes 786440 | tf_op jit(solution)/shard_map/ppermute | solution.py:36
  34.8 10.5 %copy-start.2 = (s32[16]{0:T(128)S(1)}, s32[16]{0:T(128)}, u32[]{:S(2)}) copy-start(s32[16]{0:T(128)} %dims_ref.3) | copy-start | bytes 196
  35.1 8.8 %collective-permute-start.11 = (bf16[16,32,256]{2,1,0:T(8,128)(2,1)S(1)}, bf16[16,32,256]{2,1,0:T(8,128)(2,1)S(1)}, u32[]{:S(2)}, u32[]{:S(2)}) collective-permute-start(bf16[16,32,256]{2,1,0:T(8,128)(2,1)S(1)} %get-tuple-element.44), channel_id=1, source_target_pairs={{0,32},{1,33},{2,34},{3,35},{4,36},{5,37},{6,38},{7,39},{8,40},{9,... | collective-permute-start | bytes 786440 | tf_op jit(solution)/shard_map/ppermute | solution.py:36
  37.0 8.4 %collective-permute-start.10 = (bf16[16,32,256]{2,1,0:T(8,128)(2,1)S(1)}, bf16[16,32,256]{2,1,0:T(8,128)(2,1)S(1)}, u32[]{:S(2)}, u32[]{:S(2)}) collective-permute-start(bf16[16,32,256]{2,1,0:T(8,128)(2,1)S(1)} %get-tuple-element.42), channel_id=1, source_target_pairs={{0,96},{1,97},{2,98},{3,99},{4,100},{5,101},{6,102},{7,103},{8,104... | collective-permute-start | bytes 786440 | tf_op jit(solution)/shard_map/ppermute | solution.py:36
  44.0 8.4 %collective-permute-start.12 = (bf16[16,32,256]{2,1,0:T(8,128)(2,1)S(1)}, bf16[16,32,256]{2,1,0:T(8,128)(2,1)S(1)}, u32[]{:S(2)}, u32[]{:S(2)}) collective-permute-start(bf16[16,32,256]{2,1,0:T(8,128)(2,1)S(1)} %add_convert_fusion), channel_id=1, source_target_pairs={{0,32},{1,33},{2,34},{3,35},{4,36},{5,37},{6,38},{7,39},{8,40},{9,... | collective-permute-start | bytes 786440 | tf_op jit(solution)/shard_map/ppermute | solution.py:36

commit v7 on v6

--- a/solution.py
+++ b/solution.py
@@ -14,7 +14,7 @@
 QMAX = 2
 HELD = SECS + 2 * QMAX
 STRIP = OPS * 16
-EARLY = 4
+EARLY = 6
 SPLIT = 12
 BF = jnp.bfloat16
 F32 = jnp.float32
@@ -102,23 +102,12 @@
     by_twos(one_operator, ops)
 
 
-def first_operators(dims_ref, psi_hbm, right_hbm, masked_ref, right_ref, h_ref, done_ref, psi_sem, right_sem):
-    right_in = pltpu.make_async_copy(right_hbm, right_ref, right_sem)
-
-    def psi_in(s):
-        return pltpu.make_async_copy(psi_hbm.at[s], masked_ref.at[s], psi_sem.at[s])
-
-    for s in range(SECS):
-        psi_in(s).start()
-    right_in.start()
-
+def first_operators(dims_ref, psi_ref, right_ref, masked_ref, h_ref, done_ref):
     def mask_one(s, _):
-        psi_in(s).wait()
-        masked_ref[s] = masked(masked_ref[s], dims_ref[s])
+        masked_ref[s] = masked(psi_ref[s], dims_ref[s])
         return 0
 
     lax.fori_loop(0, SECS, mask_one, 0)
-    right_in.wait()
     own_sectors((0, EARLY), masked_ref, right_ref, h_ref)
     done_ref[...] = jnp.zeros_like(done_ref)
 
@@ -205,7 +194,7 @@
 
     smem = pl.BlockSpec(memory_space=pltpu.SMEM)
     vmem = pl.BlockSpec(memory_space=pltpu.VMEM)
-    hbm = pl.BlockSpec(memory_space=pltpu.HBM)
+
 
     def call(kernel, name, in_specs, out_shape, dots, scratch=(), aliases={}):
         return pl.pallas_call(
@@ -231,11 +220,10 @@
     up = move(sent, gather_first(1))
     down = move(down, gather_first(-1))
     two = move(left_ops, gather_first(2))
-    live_psi, right, h, done = call(
-        first_operators, "first_operators", [smem, hbm, hbm],
-        [((SECS, B, B), BF), ((OPS, B, B), BF), ((OPS, HELD * B, B), BF), ((8, 128), F32)], EARLY * SECS,
-        [pltpu.SemaphoreType.DMA((SECS,)), pltpu.SemaphoreType.DMA],
-    )(dims_there, psi_there, right_there)
+    live_psi, h, done = call(
+        first_operators, "first_operators", [smem, vmem, vmem],
+        [((SECS, B, B), BF), ((OPS, HELD * B, B), BF), ((8, 128), F32)], EARLY * SECS,
+    )(dims_there, psi, right_ops)
     strips, = call(unpack, "unpack", [vmem] * 5, [((4, OPS, 16, B), BF)], 0)(sent, up, down, two, done)
     up_late, down_late, _ = lax.optimization_barrier((up, down, strips))
     up_other, down_other = move(up_late, other_core), move(down_late, other_core)
@@ -245,7 +233,7 @@
     h, = call(
         other_sectors, "other_sectors", [smem, smem] + [vmem] * 7, [((OPS, HELD * B, B), BF)], 0,
         [pltpu.VMEM((2 * QMAX * B, B), BF)], {8: 0},
-    )(op_shift, place, up, down, up_other, down_other, live_psi, right, h)
+    )(op_shift, place, up, down, up_other, down_other, live_psi, right_ops, h)
 
     first_a = [((NZ, SPLIT, 32, B), F32), ((NZ, SPLIT, 32, B), BF), ((B, OPS * B), BF)]
     mine_a, away_a, left = call(first_targets, "first_targets", [smem, smem] + [vmem] * 5, first_a, OPS * SPLIT)(

time: 53.5 us -> 53.7 us (level)
  waiting for transfers between devices: 19.3 us -> 21 us
  Pallas kernels: 17.1 us -> 15.7 us
    ppermute x13, waiting for transfers between devices: 19.3 us -> 21 us  [move(): return lax.ppermute(block, ('op', 'sec'), route)]
    pallas_call x1, Pallas kernels: 3.91 us -> 2.43 us  [on_device(): call(other_sectors, 'other_sectors', [smem, smem] + [vmem] * 7, [((OPS, H...]
  transfers between devices with their start and end apart: 13 -> 13, of which waited for: 6 -> 6; matrix products, arithmetic and copies ran while one was open for 0% -> 0% of each run, Pallas kernels for 21% -> 18%
where the time goes in v7:
time: 53.7 us; the launch traced here: 53.5 us
  waiting for transfers between devices  21 us (39%)
  Pallas kernels  15.7 us (29%)
  starting transfers between devices  15.5 us (29%)
  other arithmetic  1.16 us (2%)
    ppermute x13, waiting for transfers between devices, move(): return lax.ppermute(block, ('op', 'sec'), route)  21 us
    ppermute x13, starting transfers between devices, move(): return lax.ppermute(block, ('op', 'sec'), route)  15.5 us
    pallas_call x1, Pallas kernels, on_device(): call(first_operators, 'first_operators', [smem, vmem, vmem], [((SECS, B,...  5.21 us
    pallas_call x1, Pallas kernels, on_device(): call(first_targets, 'first_targets', [smem, smem] + [vmem] * 5, first_a,...  4.64 us
    pallas_call x1, Pallas kernels, on_device(): call(other_sectors, 'other_sectors', [smem, smem] + [vmem] * 7, [((OPS, H...  2.43 us
    pallas_call x1, Pallas kernels, on_device(): call(functools.partial(some_targets, SPLIT), 'last_targets', [smem, vmem,...  1.82 us
    pallas_call x1, Pallas kernels, on_device(): pl.pallas_call(pack, grid=(1,), in_specs=[smem, *ends, pl.BlockSpec((OPS,...  1.33 us
  transfers between devices with their start and end apart: 13, of which 6 were waited for; matrix products, arithmetic and copies ran while one was open for 0% of the time, Pallas kernels for 18%

profile of v7, /device:TPU:0, one launch (start us, length us, event | category | flops | bytes accessed | tf_op | source)
XLA Modules:
  0.0 53.5 jit_solution(17059482271252229566)
XLA Ops:
  0.0 1.3 %pack.1 = (bf16[640,256]{1,0:T(8,128)(2,1)S(1)}, bf16[640,256]{1,0:T(8,128)(2,1)S(1)}) custom-call(s32[16]{0:T(128)} %dims_ref.3, bf16[16,256,256]{2,1,0:T(8,128)(2,1)} %psi_ref.1, bf16[16,256,256]{2,1,0:T(8,128)(2,1)} %psi_ref.1, bf16[8,16,256]{2,1,0:T(8,128)(2,1)} %left_ref.1), custom_call_target="tpu_custom_call" | custom-call | bytes 1048576 | tf_op jit(solution)/shard_map/pack/pallas_call | solution.py:212
  1.3 0.1 pad_add_fusion.place_ref
  1.4 1.6 %collective-permute-start = (bf16[640,256]{1,0:T(8,128)(2,1)S(1)}, bf16[640,256]{1,0:T(8,128)(2,1)S(1)}, u32[]{:S(2)}, u32[]{:S(2)}) collective-permute-start(bf16[640,256]{1,0:T(8,128)(2,1)S(1)} %get-tuple-element.26.own), channel_id=1, source_target_pairs={{0,1},{1,2},{2,3},{3,4},{4,5},{5,6},{6,7},{7,8},{8,9},{9,10},{10,1... | collective-permute-start | bytes 983048 | tf_op jit(solution)/shard_map/ppermute | solution.py:36
  3.0 3.8 %collective-permute-start.1 = (bf16[640,256]{1,0:T(8,128)(2,1)S(1)}, bf16[640,256]{1,0:T(8,128)(2,1)S(1)}, u32[]{:S(2)}, u32[]{:S(2)}) collective-permute-start(bf16[640,256]{1,0:T(8,128)(2,1)S(1)} %get-tuple-element.27), channel_id=1, source_target_pairs={{0,15},{1,0},{2,1},{3,2},{4,3},{5,4},{6,5},{7,6},{8,7},{9,8},{10,9... | collective-permute-start | bytes 983048 | tf_op jit(solution)/shard_map/ppermute | solution.py:36
  6.8 0.0 collective-permute-start.2
  6.9 5.2 %first_operators.1 = (bf16[16,256,256]{2,1,0:T(8,128)(2,1)S(1)}, bf16[8,5120,256]{2,1,0:T(8,128)(2,1)S(1)}, f32[8,128]{1,0:T(8,128)S(1)}) custom-call(s32[16]{0:T(128)} %dims_ref.3, bf16[16,256,256]{2,1,0:T(8,128)(2,1)S(1)} %copy-done, bf16[8,256,256]{2,1,0:T(8,128)(2,1)S(1)} %copy-done.1), custom_call_target="tpu_custom_call" | custom-call | flops 3221225472 | bytes 4194304 | tf_op jit(solution)/shard_map/first_operators/pallas_call | solution.py:223
  12.1 2.8 %collective-permute-done.2.second_below = bf16[8,16,256]{2,1,0:T(8,128)(2,1)S(1)} collective-permute-done((bf16[8,16,256]{2,1,0:T(8,128)(2,1)S(1)}, bf16[8,16,256]{2,1,0:T(8,128)(2,1)S(1)}, u32[]{:S(2)}, u32[]{:S(2)}) %collective-permute-start.2) | collective-permute-done | bytes 65568 | tf_op jit(solution)/shard_map/ppermute | solution.py:36
  14.9 0.1 collective-permute-start.6
  15.0 0.5 collective-permute-start.7
  15.5 0.0 collective-permute-start.3
  15.5 2.0 %collective-permute-start.4 = (bf16[4,8,16,256]{3,2,1,0:T(8,128)(2,1)S(1)}, bf16[4,8,16,256]{3,2,1,0:T(8,128)(2,1)S(1)}, u32[]{:S(2)}, u32[]{:S(2)}) collective-permute-start(bf16[4,8,16,256]{3,2,1,0:T(8,128)(2,1)S(1)} %unpack.1.t0), channel_id=1, source_target_pairs={{0,8},{1,9},{2,10},{3,11},{4,12},{5,13},{6,14},{7,15},{8,0},{9,1},... | collective-permute-start | bytes 786440 | tf_op jit(solution)/shard_map/ppermute | solution.py:36
  17.5 1.3 %collective-permute-start.5 = (bf16[4,8,16,256]{3,2,1,0:T(8,128)(2,1)S(1)}, bf16[4,8,16,256]{3,2,1,0:T(8,128)(2,1)S(1)}, u32[]{:S(2)}, u32[]{:S(2)}) collective-permute-start(bf16[4,8,16,256]{3,2,1,0:T(8,128)(2,1)S(1)} %unpack.1.t0), channel_id=1, source_target_pairs={{0,12},{1,13},{2,14},{3,15},{4,0},{5,1},{6,2},{7,3},{8,4},{9,5},{1... | collective-permute-start | bytes 786440 | tf_op jit(solution)/shard_map/ppermute | solution.py:36
  18.8 2.4 %other_sectors.1.h_ref = bf16[8,5120,256]{2,1,0:T(8,128)(2,1)S(1)} custom-call(s32[8]{0:T(128)S(1)} %copy-done.2, s32[4]{0:T(128)S(1)} %pad_add_fusion.place_ref, bf16[640,256]{1,0:T(8,128)(2,1)S(1)} %collective-permute-done.from_below.below_0, bf16[640,256]{1,0:T(8,128)(2,1)S(1)} %collective-permute-done.1.from_above.above_0, ...), custom_call_target="tpu_custom_call", output_to_operand_aliasing={{}: (8, {})} | custom-call | tf_op jit(solution)/shard_map/other_sectors/pallas_call | solution.py:233
  21.3 4.6 %collective-permute-done.3.t1 = bf16[4,8,16,256]{3,2,1,0:T(8,128)(2,1)S(1)} collective-permute-done((bf16[4,8,16,256]{3,2,1,0:T(8,128)(2,1)S(1)}, bf16[4,8,16,256]{3,2,1,0:T(8,128)(2,1)S(1)}, u32[]{:S(2)}, u32[]{:S(2)}) %collective-permute-start.3) | collective-permute-done | bytes 262176 | tf_op jit(solution)/shard_map/ppermute | solution.py:36
  25.8 0.0 collective-permute-done.4.t2
  25.8 0.9 %collective-permute-done.5.t3 = bf16[4,8,16,256]{3,2,1,0:T(8,128)(2,1)S(1)} collective-permute-done((bf16[4,8,16,256]{3,2,1,0:T(8,128)(2,1)S(1)}, bf16[4,8,16,256]{3,2,1,0:T(8,128)(2,1)S(1)}, u32[]{:S(2)}, u32[]{:S(2)}) %collective-permute-start.5) | collective-permute-done | bytes 262176 | tf_op jit(solution)/shard_map/ppermute | solution.py:36
  26.7 4.6 %first_targets.1 = (f32[4,12,32,256]{3,2,1,0:T(8,128)S(1)}, bf16[4,12,32,256]{3,2,1,0:T(8,128)(2,1)S(1)}, bf16[256,2048]{1,0:T(8,128)(2,1)S(1)}) custom-call(s32[8]{0:T(128)S(1)} %copy-done.2, s32[4]{0:T(128)S(1)} %pad_add_fusion.place_ref, bf16[4,8,16,256]{3,2,1,0:T(8,128)(2,1)S(1)} %unpack.1.t0, bf16[4,8,16,256]{3,2,1,0:T(8,128)(2,1)S(1)} %collective-permute-done.3.t1, ...), custom_call_target="tpu_custom_call" | custom-call | flops 3221225472 | bytes 4194304 | tf_op jit(solution)/shard_map/first_targets/pallas_call | solution.py:239
  31.4 0.1 collective-permute-start.8
  31.5 1.8 %last_targets.1 = (f32[4,4,32,256]{3,2,1,0:T(8,128)S(1)}, bf16[4,4,32,256]{3,2,1,0:T(8,128)(2,1)S(1)}) custom-call(s32[8]{0:T(128)S(1)} %copy-done.2, bf16[256,2048]{1,0:T(8,128)(2,1)S(1)} %get-tuple-element.35.left_ref, bf16[8,5120,256]{2,1,0:T(8,128)(2,1)S(1)} %other_sectors.1.h_ref), custom_call_target="tpu_custom_call" | custom-call | flops 1073741824 | bytes 4194304 | tf_op jit(solution)/shard_map/last_targets/pallas_call | solution.py:242
  33.3 0.6 %collective-permute-start.9 = (bf16[4,4,32,256]{3,2,1,0:T(8,128)(2,1)S(1)}, bf16[4,4,32,256]{3,2,1,0:T(8,128)(2,1)S(1)}, u32[]{:S(2)}, u32[]{:S(2)}) collective-permute-start(bf16[4,4,32,256]{3,2,1,0:T(8,128)(2,1)S(1)} %get-tuple-element.38), channel_id=1, source_target_pairs={{0,16},{1,17},{2,18},{3,19},{4,20},{5,21},{6,22},{7,23},{8,24},{9,... | collective-permute-start | bytes 786440 | tf_op jit(solution)/shard_map/ppermute | solution.py:36
  33.9 1.2 %collective-permute-done.9.got_b = bf16[4,4,32,256]{3,2,1,0:T(8,128)(2,1)S(1)} collective-permute-done((bf16[4,4,32,256]{3,2,1,0:T(8,128)(2,1)S(1)}, bf16[4,4,32,256]{3,2,1,0:T(8,128)(2,1)S(1)}, u32[]{:S(2)}, u32[]{:S(2)}) %collective-permute-start.9) | collective-permute-done | bytes 262176 | tf_op jit(solution)/shard_map/ppermute | solution.py:36
  35.0 0.0 collective-permute-done.8.got_a
  35.1 0.2 add_cores.1
  35.3 2.0 %collective-permute-start.11 = (bf16[16,32,256]{2,1,0:T(8,128)(2,1)S(1)}, bf16[16,32,256]{2,1,0:T(8,128)(2,1)S(1)}, u32[]{:S(2)}, u32[]{:S(2)}) collective-permute-start(bf16[16,32,256]{2,1,0:T(8,128)(2,1)S(1)} %get-tuple-element.42), channel_id=1, source_target_pairs={{0,32},{1,33},{2,34},{3,35},{4,36},{5,37},{6,38},{7,39},{8,40},{9,... | collective-permute-start | bytes 786440 | tf_op jit(solution)/shard_map/ppermute | solution.py:36
  37.3 2.2 %collective-permute-start.10 = (bf16[16,32,256]{2,1,0:T(8,128)(2,1)S(1)}, bf16[16,32,256]{2,1,0:T(8,128)(2,1)S(1)}, u32[]{:S(2)}, u32[]{:S(2)}) collective-permute-start(bf16[16,32,256]{2,1,0:T(8,128)(2,1)S(1)} %get-tuple-element.40), channel_id=1, source_target_pairs={{0,96},{1,97},{2,98},{3,99},{4,100},{5,101},{6,102},{7,103},{8,104... | collective-permute-start | bytes 786440 | tf_op jit(solution)/shard_map/ppermute | solution.py:36
  39.5 4.6 %collective-permute-done.11 = bf16[16,32,256]{2,1,0:T(8,128)(2,1)S(1)} collective-permute-done((bf16[16,32,256]{2,1,0:T(8,128)(2,1)S(1)}, bf16[16,32,256]{2,1,0:T(8,128)(2,1)S(1)}, u32[]{:S(2)}, u32[]{:S(2)}) %collective-permute-start.11) | collective-permute-done | bytes 262176 | tf_op jit(solution)/shard_map/ppermute | solution.py:36
  44.1 0.1 add_convert_fusion
  44.2 1.3 %collective-permute-start.12 = (bf16[16,32,256]{2,1,0:T(8,128)(2,1)S(1)}, bf16[16,32,256]{2,1,0:T(8,128)(2,1)S(1)}, u32[]{:S(2)}, u32[]{:S(2)}) collective-permute-start(bf16[16,32,256]{2,1,0:T(8,128)(2,1)S(1)} %add_convert_fusion), channel_id=1, source_target_pairs={{0,32},{1,33},{2,34},{3,35},{4,36},{5,37},{6,38},{7,39},{8,40},{9,... | collective-permute-start | bytes 786440 | tf_op jit(solution)/shard_map/ppermute | solution.py:36
  45.5 0.1 broadcast_compare_fusion
  45.6 0.1 iota_compare_fusion
  45.7 6.9 %collective-permute-done.12 = bf16[16,32,256]{2,1,0:T(8,128)(2,1)S(1)} collective-permute-done((bf16[16,32,256]{2,1,0:T(8,128)(2,1)S(1)}, bf16[16,32,256]{2,1,0:T(8,128)(2,1)S(1)}, u32[]{:S(2)}, u32[]{:S(2)}) %collective-permute-start.12) | collective-permute-done | bytes 262176 | tf_op jit(solution)/shard_map/ppermute | solution.py:36
  52.6 0.9 %select_convert_fusion = bf16[16,32,256]{2,1,0:T(8,128)(2,1)} fusion(bf16[16,32,256]{2,1,0:T(8,128)(2,1)S(1)} %collective-permute-done.12, f32[16,32,256]{2,1,0:T(8,128)S(1)} %get-tuple-element.39, bf16[16,32,256]{2,1,0:T(8,128)(2,1)S(1)} %collective-permute-done.10, pred[16,256]{1,0:T(8,128)(4,1)S(1)} %iota_compare_fusion, ...), kind=kLoop, calls=%fused_computation | loop fusion | flops 917504 | bytes 1315328 | tf_op jit(solution)/shard_map/convert_element_type | solution.py:258
  (17 shorter events, 0.1 us)
Async XLA Ops:
  0.0 6.8 %copy-start.3 = (bf16[8,16,256]{2,1,0:T(8,128)(2,1)S(1)}, bf16[8,16,256]{2,1,0:T(8,128)(2,1)}, u32[]{:S(2)}) copy-start(bf16[8,16,256]{2,1,0:T(8,128)(2,1)} %left_ref.1) | copy-start | bytes 196612
  0.0 6.8 %copy-start = (bf16[16,256,256]{2,1,0:T(8,128)(2,1)S(1)}, bf16[16,256,256]{2,1,0:T(8,128)(2,1)}, u32[]{:S(2)}) copy-start(bf16[16,256,256]{2,1,0:T(8,128)(2,1)} %psi_ref.1) | copy-start | bytes 6291460
  0.0 6.8 %copy-start.1 = (bf16[8,256,256]{2,1,0:T(8,128)(2,1)S(1)}, bf16[8,256,256]{2,1,0:T(8,128)(2,1)}, u32[]{:S(2)}) copy-start(bf16[8,256,256]{2,1,0:T(8,128)(2,1)} %right_ref.3) | copy-start | bytes 3145732
  1.4 13.4 %collective-permute-start = (bf16[640,256]{1,0:T(8,128)(2,1)S(1)}, bf16[640,256]{1,0:T(8,128)(2,1)S(1)}, u32[]{:S(2)}, u32[]{:S(2)}) collective-permute-start(bf16[640,256]{1,0:T(8,128)(2,1)S(1)} %get-tuple-element.26.own), channel_id=1, source_target_pairs={{0,1},{1,2},{2,3},{3,4},{4,5},{5,6},{6,7},{7,8},{8,9},{9,10},{10,1... | collective-permute-start | bytes 983048 | tf_op jit(solution)/shard_map/ppermute | solution.py:36
  3.0 15.8 %copy-start.2 = (s32[8]{0:T(128)S(1)}, s32[8]{0:T(128)}, u32[]{:S(2)}) copy-start(s32[8]{0:T(128)} %shift_ref.5) | copy-start | bytes 100
  3.0 11.8 %collective-permute-start.1 = (bf16[640,256]{1,0:T(8,128)(2,1)S(1)}, bf16[640,256]{1,0:T(8,128)(2,1)S(1)}, u32[]{:S(2)}, u32[]{:S(2)}) collective-permute-start(bf16[640,256]{1,0:T(8,128)(2,1)S(1)} %get-tuple-element.27), channel_id=1, source_target_pairs={{0,15},{1,0},{2,1},{3,2},{4,3},{5,4},{6,5},{7,6},{8,7},{9,8},{10,9... | collective-permute-start | bytes 983048 | tf_op jit(solution)/shard_map/ppermute | solution.py:36
  6.8 8.0 %collective-permute-start.2 = (bf16[8,16,256]{2,1,0:T(8,128)(2,1)S(1)}, bf16[8,16,256]{2,1,0:T(8,128)(2,1)S(1)}, u32[]{:S(2)}, u32[]{:S(2)}) collective-permute-start(bf16[8,16,256]{2,1,0:T(8,128)(2,1)S(1)} %copy-done.3), channel_id=1, source_target_pairs={{0,2},{1,3},{2,4},{3,5},{4,6},{5,7},{6,8},{7,9},{8,10},{9,11},{10,... | collective-permute-start | bytes 196616 | tf_op jit(solution)/shard_map/ppermute | solution.py:36
  14.9 4.0 %collective-permute-start.6 = (bf16[640,256]{1,0:T(8,128)(2,1)S(1)}, bf16[640,256]{1,0:T(8,128)(2,1)S(1)}, u32[]{:S(2)}, u32[]{:S(2)}) collective-permute-start(bf16[640,256]{1,0:T(8,128)(2,1)S(1)} %collective-permute-done.from_below.below_0), channel_id=1, source_target_pairs={{0,16},{1,17},{2,18},{3,19},{4,20},{5,21},{6,22},{7,23},{8,24},{9,... | collective-permute-start | bytes 983048 | tf_op jit(solution)/shard_map/ppermute | solution.py:36
  15.0 3.9 %collective-permute-start.7 = (bf16[640,256]{1,0:T(8,128)(2,1)S(1)}, bf16[640,256]{1,0:T(8,128)(2,1)S(1)}, u32[]{:S(2)}, u32[]{:S(2)}) collective-permute-start(bf16[640,256]{1,0:T(8,128)(2,1)S(1)} %collective-permute-done.1.from_above.above_0), channel_id=1, source_target_pairs={{0,16},{1,17},{2,18},{3,19},{4,20},{5,21},{6,22},{7,23},{8,24},{9,... | collective-permute-start | bytes 983048 | tf_op jit(solution)/shard_map/ppermute | solution.py:36
  15.5 10.4 %collective-permute-start.3 = (bf16[4,8,16,256]{3,2,1,0:T(8,128)(2,1)S(1)}, bf16[4,8,16,256]{3,2,1,0:T(8,128)(2,1)S(1)}, u32[]{:S(2)}, u32[]{:S(2)}) collective-permute-start(bf16[4,8,16,256]{3,2,1,0:T(8,128)(2,1)S(1)} %unpack.1.t0), channel_id=1, source_target_pairs={{0,4},{1,5},{2,6},{3,7},{4,8},{5,9},{6,10},{7,11},{8,12},{9,13},{1... | collective-permute-start | bytes 786440 | tf_op jit(solution)/shard_map/ppermute | solution.py:36
  15.5 10.4 %collective-permute-start.4 = (bf16[4,8,16,256]{3,2,1,0:T(8,128)(2,1)S(1)}, bf16[4,8,16,256]{3,2,1,0:T(8,128)(2,1)S(1)}, u32[]{:S(2)}, u32[]{:S(2)}) collective-permute-start(bf16[4,8,16,256]{3,2,1,0:T(8,128)(2,1)S(1)} %unpack.1.t0), channel_id=1, source_target_pairs={{0,8},{1,9},{2,10},{3,11},{4,12},{5,13},{6,14},{7,15},{8,0},{9,1},... | collective-permute-start | bytes 786440 | tf_op jit(solution)/shard_map/ppermute | solution.py:36
  17.5 9.3 %collective-permute-start.5 = (bf16[4,8,16,256]{3,2,1,0:T(8,128)(2,1)S(1)}, bf16[4,8,16,256]{3,2,1,0:T(8,128)(2,1)S(1)}, u32[]{:S(2)}, u32[]{:S(2)}) collective-permute-start(bf16[4,8,16,256]{3,2,1,0:T(8,128)(2,1)S(1)} %unpack.1.t0), channel_id=1, source_target_pairs={{0,12},{1,13},{2,14},{3,15},{4,0},{5,1},{6,2},{7,3},{8,4},{9,5},{1... | collective-permute-start | bytes 786440 | tf_op jit(solution)/shard_map/ppermute | solution.py:36
  31.4 3.7 %collective-permute-start.8 = (bf16[4,12,32,256]{3,2,1,0:T(8,128)(2,1)S(1)}, bf16[4,12,32,256]{3,2,1,0:T(8,128)(2,1)S(1)}, u32[]{:S(2)}, u32[]{:S(2)}) collective-permute-start(bf16[4,12,32,256]{3,2,1,0:T(8,128)(2,1)S(1)} %get-tuple-element.37), channel_id=1, source_target_pairs={{0,16},{1,17},{2,18},{3,19},{4,20},{5,21},{6,22},{7,23},{8,24},{9,... | collective-permute-start | bytes 2359304 | tf_op jit(solution)/shard_map/ppermute | solution.py:36
  33.3 1.7 %collective-permute-start.9 = (bf16[4,4,32,256]{3,2,1,0:T(8,128)(2,1)S(1)}, bf16[4,4,32,256]{3,2,1,0:T(8,128)(2,1)S(1)}, u32[]{:S(2)}, u32[]{:S(2)}) collective-permute-start(bf16[4,4,32,256]{3,2,1,0:T(8,128)(2,1)S(1)} %get-tuple-element.38), channel_id=1, source_target_pairs={{0,16},{1,17},{2,18},{3,19},{4,20},{5,21},{6,22},{7,23},{8,24},{9,... | collective-permute-start | bytes 786440 | tf_op jit(solution)/shard_map/ppermute | solution.py:36
  35.1 10.5 %copy-start.4 = (s32[16]{0:T(128)S(1)}, s32[16]{0:T(128)}, u32[]{:S(2)}) copy-start(s32[16]{0:T(128)} %dims_ref.3) | copy-start | bytes 196
  35.3 8.8 %collective-permute-start.11 = (bf16[16,32,256]{2,1,0:T(8,128)(2,1)S(1)}, bf16[16,32,256]{2,1,0:T(8,128)(2,1)S(1)}, u32[]{:S(2)}, u32[]{:S(2)}) collective-permute-start(bf16[16,32,256]{2,1,0:T(8,128)(2,1)S(1)} %get-tuple-element.42), channel_id=1, source_target_pairs={{0,32},{1,33},{2,34},{3,35},{4,36},{5,37},{6,38},{7,39},{8,40},{9,... | collective-permute-start | bytes 786440 | tf_op jit(solution)/shard_map/ppermute | solution.py:36
  37.3 8.4 %collective-permute-start.10 = (bf16[16,32,256]{2,1,0:T(8,128)(2,1)S(1)}, bf16[16,32,256]{2,1,0:T(8,128)(2,1)S(1)}, u32[]{:S(2)}, u32[]{:S(2)}) collective-permute-start(bf16[16,32,256]{2,1,0:T(8,128)(2,1)S(1)} %get-tuple-element.40), channel_id=1, source_target_pairs={{0,96},{1,97},{2,98},{3,99},{4,100},{5,101},{6,102},{7,103},{8,104... | collective-permute-start | bytes 786440 | tf_op jit(solution)/shard_map/ppermute | solution.py:36
  44.2 8.4 %collective-permute-start.12 = (bf16[16,32,256]{2,1,0:T(8,128)(2,1)S(1)}, bf16[16,32,256]{2,1,0:T(8,128)(2,1)S(1)}, u32[]{:S(2)}, u32[]{:S(2)}) collective-permute-start(bf16[16,32,256]{2,1,0:T(8,128)(2,1)S(1)} %add_convert_fusion), channel_id=1, source_target_pairs={{0,32},{1,33},{2,34},{3,35},{4,36},{5,37},{6,38},{7,39},{8,40},{9,... | collective-permute-start | bytes 786440 | tf_op jit(solution)/shard_map/ppermute | solution.py:36

commit v8 on v6

--- a/solution.py
+++ b/solution.py
@@ -15,7 +15,7 @@
 HELD = SECS + 2 * QMAX
 STRIP = OPS * 16
 EARLY = 4
-SPLIT = 12
+SPLIT = 8
 BF = jnp.bfloat16
 F32 = jnp.float32
 
@@ -168,7 +168,7 @@
 
 def some_targets(first, shift_ref, left_ref, h_ref, mine_ref, other_ref):
     count = mine_ref.shape[1]
-    at_once = min(count, 6)
+    at_once = min(count, 8)
 
     def several_targets(i, _):
         for u in range(at_once):

time: 53.5 us -> 53.8 us (level)
  local copies, waits for them, and re-layouts: 0.01 us -> 0.66 us
  waiting for transfers between devices: 19.3 us -> 19.9 us
    pallas_call x1, Pallas kernels: 4.56 us -> 3.19 us  [on_device(): call(first_targets, 'first_targets', [smem, smem] + [vmem] * 5, first_a,...]
    pallas_call x1, Pallas kernels: 1.79 us -> 2.87 us  [on_device(): call(functools.partial(some_targets, SPLIT), 'last_targets', [smem, vmem,...]
    unnamed x6, local copies, waits for them, and re-layouts: 0.01 us -> 0.66 us
    ppermute x13, waiting for transfers between devices: 19.3 us -> 19.9 us  [move(): return lax.ppermute(block, ('op', 'sec'), route)]
  transfers between devices with their start and end apart: 13 -> 13, of which waited for: 6 -> 7; matrix products, arithmetic and copies ran while one was open for 0% -> 0% of each run, Pallas kernels for 21% -> 17%
where the time goes in v8:
time: 53.8 us; the launch traced here: 53.6 us
  waiting for transfers between devices  19.9 us (37%)
  Pallas kernels  16.7 us (31%)
  starting transfers between devices  15.1 us (28%)
  other arithmetic  1.16 us (2%)
  local copies, waits for them, and re-layouts  0.66 us (1%)
    ppermute x13, waiting for transfers between devices, move(): return lax.ppermute(block, ('op', 'sec'), route)  19.9 us
    ppermute x13, starting transfers between devices, move(): return lax.ppermute(block, ('op', 'sec'), route)  15.1 us
    pallas_call x1, Pallas kernels, on_device(): call(first_operators, 'first_operators', [smem, hbm, hbm], [((SECS, B, B)...  5.37 us
    pallas_call x1, Pallas kernels, on_device(): call(other_sectors, 'other_sectors', [smem, smem] + [vmem] * 7, [((OPS, H...  3.91 us
    pallas_call x1, Pallas kernels, on_device(): call(first_targets, 'first_targets', [smem, smem] + [vmem] * 5, first_a,...  3.19 us
    pallas_call x1, Pallas kernels, on_device(): call(functools.partial(some_targets, SPLIT), 'last_targets', [smem, vmem,...  2.87 us
    pallas_call x1, Pallas kernels, on_device(): pl.pallas_call(pack, grid=(1,), in_specs=[smem, *ends, pl.BlockSpec((OPS,...  1.18 us
  transfers between devices with their start and end apart: 13, of which 7 were waited for; matrix products, arithmetic and copies ran while one was open for 0% of the time, Pallas kernels for 17%

profile of v8, /device:TPU:0, one launch (start us, length us, event | category | flops | bytes accessed | tf_op | source)
XLA Modules:
  0.0 53.6 jit_solution(12146125965048501409)
XLA Ops:
  0.0 1.2 %pack.1 = (bf16[640,256]{1,0:T(8,128)(2,1)S(1)}, bf16[640,256]{1,0:T(8,128)(2,1)S(1)}) custom-call(s32[16]{0:T(128)} %dims_ref.3, bf16[16,256,256]{2,1,0:T(8,128)(2,1)} %psi_hbm.1, bf16[16,256,256]{2,1,0:T(8,128)(2,1)} %psi_hbm.1, bf16[8,16,256]{2,1,0:T(8,128)(2,1)} %left_ref.1), custom_call_target="tpu_custom_call" | custom-call | bytes 1048576 | tf_op jit(solution)/shard_map/pack/pallas_call | solution.py:223
  1.2 0.1 pad_add_fusion.place_ref
  1.3 1.6 %collective-permute-start = (bf16[640,256]{1,0:T(8,128)(2,1)S(1)}, bf16[640,256]{1,0:T(8,128)(2,1)S(1)}, u32[]{:S(2)}, u32[]{:S(2)}) collective-permute-start(bf16[640,256]{1,0:T(8,128)(2,1)S(1)} %get-tuple-element.27.own), channel_id=1, source_target_pairs={{0,1},{1,2},{2,3},{3,4},{4,5},{5,6},{6,7},{7,8},{8,9},{9,10},{10,1... | collective-permute-start | bytes 983048 | tf_op jit(solution)/shard_map/ppermute | solution.py:36
  2.9 3.8 %collective-permute-start.1 = (bf16[640,256]{1,0:T(8,128)(2,1)S(1)}, bf16[640,256]{1,0:T(8,128)(2,1)S(1)}, u32[]{:S(2)}, u32[]{:S(2)}) collective-permute-start(bf16[640,256]{1,0:T(8,128)(2,1)S(1)} %get-tuple-element.28), channel_id=1, source_target_pairs={{0,15},{1,0},{2,1},{3,2},{4,3},{5,4},{6,5},{7,6},{8,7},{9,8},{10,9... | collective-permute-start | bytes 983048 | tf_op jit(solution)/shard_map/ppermute | solution.py:36
  6.7 0.0 collective-permute-start.2
  6.7 5.4 %first_operators.1 = (bf16[16,256,256]{2,1,0:T(8,128)(2,1)S(1)}, bf16[8,256,256]{2,1,0:T(8,128)(2,1)S(1)}, bf16[8,5120,256]{2,1,0:T(8,128)(2,1)S(1)}, f32[8,128]{1,0:T(8,128)S(1)}) custom-call(s32[16]{0:T(128)} %dims_ref.3, bf16[16,256,256]{2,1,0:T(8,128)(2,1)} %psi_hbm.1, bf16[8,256,256]{2,1,0:T(8,128)(2,1)} %right_hbm.1), custom_call_target="tpu_custom_call" | custom-call | flops 2147483648 | bytes 4194304 | tf_op jit(solution)/shard_map/first_operators/pallas_call | solution.py:234
  12.0 2.7 %collective-permute-done.2.second_below = bf16[8,16,256]{2,1,0:T(8,128)(2,1)S(1)} collective-permute-done((bf16[8,16,256]{2,1,0:T(8,128)(2,1)}, bf16[8,16,256]{2,1,0:T(8,128)(2,1)S(1)}, u32[]{:S(2)}, u32[]{:S(2)}) %collective-permute-start.2) | collective-permute-done | bytes 65568 | tf_op jit(solution)/shard_map/ppermute | solution.py:36
  14.8 0.1 collective-permute-start.6
  14.9 0.5 collective-permute-start.7
  15.4 2.1 %collective-permute-start.4 = (bf16[4,8,16,256]{3,2,1,0:T(8,128)(2,1)S(1)}, bf16[4,8,16,256]{3,2,1,0:T(8,128)(2,1)S(1)}, u32[]{:S(2)}, u32[]{:S(2)}) collective-permute-start(bf16[4,8,16,256]{3,2,1,0:T(8,128)(2,1)S(1)} %unpack.1.t0), channel_id=1, source_target_pairs={{0,8},{1,9},{2,10},{3,11},{4,12},{5,13},{6,14},{7,15},{8,0},{9,1},... | collective-permute-start | bytes 786440 | tf_op jit(solution)/shard_map/ppermute | solution.py:36
  17.5 1.3 %collective-permute-start.5 = (bf16[4,8,16,256]{3,2,1,0:T(8,128)(2,1)S(1)}, bf16[4,8,16,256]{3,2,1,0:T(8,128)(2,1)S(1)}, u32[]{:S(2)}, u32[]{:S(2)}) collective-permute-start(bf16[4,8,16,256]{3,2,1,0:T(8,128)(2,1)S(1)} %unpack.1.t0), channel_id=1, source_target_pairs={{0,12},{1,13},{2,14},{3,15},{4,0},{5,1},{6,2},{7,3},{8,4},{9,5},{1... | collective-permute-start | bytes 786440 | tf_op jit(solution)/shard_map/ppermute | solution.py:36
  18.8 0.7 %copy-done = s32[8]{0:T(128)S(1)} copy-done((s32[8]{0:T(128)S(1)}, s32[8]{0:T(128)}, u32[]{:S(2)}) %copy-start) | copy-done | bytes 56
  19.5 3.9 %other_sectors.1.h_ref = bf16[8,5120,256]{2,1,0:T(8,128)(2,1)S(1)} custom-call(s32[8]{0:T(128)S(1)} %copy-done, s32[4]{0:T(128)S(1)} %pad_add_fusion.place_ref, bf16[640,256]{1,0:T(8,128)(2,1)S(1)} %collective-permute-done.from_below.below_0, bf16[640,256]{1,0:T(8,128)(2,1)S(1)} %collective-permute-done.1.from_above.above_0, ...), custom_call_target="tpu_custom_call", output_to_operand_aliasing={{}: (8, {})} | custom-call | tf_op jit(solution)/shard_map/other_sectors/pallas_call | solution.py:245
  23.4 0.0 copy-start.2
  23.4 2.3 %collective-permute-done.3.t1 = bf16[4,8,16,256]{3,2,1,0:T(8,128)(2,1)S(1)} collective-permute-done((bf16[4,8,16,256]{3,2,1,0:T(8,128)(2,1)S(1)}, bf16[4,8,16,256]{3,2,1,0:T(8,128)(2,1)S(1)}, u32[]{:S(2)}, u32[]{:S(2)}) %collective-permute-start.3) | collective-permute-done | bytes 262176 | tf_op jit(solution)/shard_map/ppermute | solution.py:36
  25.8 0.9 %collective-permute-done.5.t3 = bf16[4,8,16,256]{3,2,1,0:T(8,128)(2,1)S(1)} collective-permute-done((bf16[4,8,16,256]{3,2,1,0:T(8,128)(2,1)S(1)}, bf16[4,8,16,256]{3,2,1,0:T(8,128)(2,1)S(1)}, u32[]{:S(2)}, u32[]{:S(2)}) %collective-permute-start.5) | collective-permute-done | bytes 262176 | tf_op jit(solution)/shard_map/ppermute | solution.py:36
  26.7 3.2 %first_targets.1 = (f32[4,8,32,256]{3,2,1,0:T(8,128)S(1)}, bf16[4,8,32,256]{3,2,1,0:T(8,128)(2,1)S(1)}, bf16[256,2048]{1,0:T(8,128)(2,1)S(1)}) custom-call(s32[8]{0:T(128)S(1)} %copy-done.1, s32[4]{0:T(128)S(1)} %pad_add_fusion.place_ref, bf16[4,8,16,256]{3,2,1,0:T(8,128)(2,1)S(1)} %unpack.1.t0, bf16[4,8,16,256]{3,2,1,0:T(8,128)(2,1)S(1)} %collective-permute-done.3.t1, ...), custom_call_target="tpu_custom_call" | custom-call | flops 2147483648 | bytes 4194304 | tf_op jit(solution)/shard_map/first_targets/pallas_call | solution.py:251
  29.9 2.9 %last_targets.1 = (f32[4,8,32,256]{3,2,1,0:T(8,128)S(1)}, bf16[4,8,32,256]{3,2,1,0:T(8,128)(2,1)S(1)}) custom-call(s32[8]{0:T(128)S(1)} %copy-done.1, bf16[256,2048]{1,0:T(8,128)(2,1)S(1)} %get-tuple-element.37.left_ref, bf16[8,5120,256]{2,1,0:T(8,128)(2,1)S(1)} %other_sectors.1.h_ref), custom_call_target="tpu_custom_call" | custom-call | flops 2147483648 | bytes 4194304 | tf_op jit(solution)/shard_map/last_targets/pallas_call | solution.py:254
  32.7 0.1 collective-permute-start.9
  32.8 0.5 collective-permute-start.8
  33.3 1.4 %collective-permute-done.9.got_b = bf16[4,8,32,256]{3,2,1,0:T(8,128)(2,1)S(1)} collective-permute-done((bf16[4,8,32,256]{3,2,1,0:T(8,128)(2,1)S(1)}, bf16[4,8,32,256]{3,2,1,0:T(8,128)(2,1)S(1)}, u32[]{:S(2)}, u32[]{:S(2)}) %collective-permute-start.9) | collective-permute-done | bytes 524320 | tf_op jit(solution)/shard_map/ppermute | solution.py:36
  34.7 0.7 %collective-permute-done.8.got_a = bf16[4,8,32,256]{3,2,1,0:T(8,128)(2,1)S(1)} collective-permute-done((bf16[4,8,32,256]{3,2,1,0:T(8,128)(2,1)S(1)}, bf16[4,8,32,256]{3,2,1,0:T(8,128)(2,1)S(1)}, u32[]{:S(2)}, u32[]{:S(2)}) %collective-permute-start.8) | collective-permute-done | bytes 524320 | tf_op jit(solution)/shard_map/ppermute | solution.py:36
  35.5 0.2 add_cores.1
  35.7 2.0 %collective-permute-start.11 = (bf16[16,32,256]{2,1,0:T(8,128)(2,1)S(1)}, bf16[16,32,256]{2,1,0:T(8,128)(2,1)S(1)}, u32[]{:S(2)}, u32[]{:S(2)}) collective-permute-start(bf16[16,32,256]{2,1,0:T(8,128)(2,1)S(1)} %get-tuple-element.44), channel_id=1, source_target_pairs={{0,32},{1,33},{2,34},{3,35},{4,36},{5,37},{6,38},{7,39},{8,40},{9,... | collective-permute-start | bytes 786440 | tf_op jit(solution)/shard_map/ppermute | solution.py:36
  37.7 2.2 %collective-permute-start.10 = (bf16[16,32,256]{2,1,0:T(8,128)(2,1)S(1)}, bf16[16,32,256]{2,1,0:T(8,128)(2,1)S(1)}, u32[]{:S(2)}, u32[]{:S(2)}) collective-permute-start(bf16[16,32,256]{2,1,0:T(8,128)(2,1)S(1)} %get-tuple-element.42), channel_id=1, source_target_pairs={{0,96},{1,97},{2,98},{3,99},{4,100},{5,101},{6,102},{7,103},{8,104... | collective-permute-start | bytes 786440 | tf_op jit(solution)/shard_map/ppermute | solution.py:36
  39.9 4.9 %collective-permute-done.11 = bf16[16,32,256]{2,1,0:T(8,128)(2,1)S(1)} collective-permute-done((bf16[16,32,256]{2,1,0:T(8,128)(2,1)S(1)}, bf16[16,32,256]{2,1,0:T(8,128)(2,1)S(1)}, u32[]{:S(2)}, u32[]{:S(2)}) %collective-permute-start.11) | collective-permute-done | bytes 262176 | tf_op jit(solution)/shard_map/ppermute | solution.py:36
  44.8 0.1 add_convert_fusion
  44.9 0.9 %collective-permute-start.12 = (bf16[16,32,256]{2,1,0:T(8,128)(2,1)S(1)}, bf16[16,32,256]{2,1,0:T(8,128)(2,1)S(1)}, u32[]{:S(2)}, u32[]{:S(2)}) collective-permute-start(bf16[16,32,256]{2,1,0:T(8,128)(2,1)S(1)} %add_convert_fusion), channel_id=1, source_target_pairs={{0,32},{1,33},{2,34},{3,35},{4,36},{5,37},{6,38},{7,39},{8,40},{9,... | collective-permute-start | bytes 786440 | tf_op jit(solution)/shard_map/ppermute | solution.py:36
  45.7 0.1 broadcast_compare_fusion
  45.8 0.1 iota_compare_fusion
  45.9 6.9 %collective-permute-done.12 = bf16[16,32,256]{2,1,0:T(8,128)(2,1)S(1)} collective-permute-done((bf16[16,32,256]{2,1,0:T(8,128)(2,1)S(1)}, bf16[16,32,256]{2,1,0:T(8,128)(2,1)S(1)}, u32[]{:S(2)}, u32[]{:S(2)}) %collective-permute-start.12) | collective-permute-done | bytes 262176 | tf_op jit(solution)/shard_map/ppermute | solution.py:36
  52.8 0.9 %select_convert_fusion = bf16[16,32,256]{2,1,0:T(8,128)(2,1)} fusion(bf16[16,32,256]{2,1,0:T(8,128)(2,1)S(1)} %collective-permute-done.12, f32[16,32,256]{2,1,0:T(8,128)S(1)} %get-tuple-element.41, bf16[16,32,256]{2,1,0:T(8,128)(2,1)S(1)} %collective-permute-done.10, pred[16,256]{1,0:T(8,128)(4,1)S(1)} %iota_compare_fusion, ...), kind=kLoop, calls=%fused_computation | loop fusion | flops 917504 | bytes 1315328 | tf_op jit(solution)/shard_map/convert_element_type | solution.py:270
  (13 shorter events, 0.0 us)
Async XLA Ops:
  1.3 13.5 %collective-permute-start = (bf16[640,256]{1,0:T(8,128)(2,1)S(1)}, bf16[640,256]{1,0:T(8,128)(2,1)S(1)}, u32[]{:S(2)}, u32[]{:S(2)}) collective-permute-start(bf16[640,256]{1,0:T(8,128)(2,1)S(1)} %get-tuple-element.27.own), channel_id=1, source_target_pairs={{0,1},{1,2},{2,3},{3,4},{4,5},{5,6},{6,7},{7,8},{8,9},{9,10},{10,1... | collective-permute-start | bytes 983048 | tf_op jit(solution)/shard_map/ppermute | solution.py:36
  2.9 11.9 %collective-permute-start.1 = (bf16[640,256]{1,0:T(8,128)(2,1)S(1)}, bf16[640,256]{1,0:T(8,128)(2,1)S(1)}, u32[]{:S(2)}, u32[]{:S(2)}) collective-permute-start(bf16[640,256]{1,0:T(8,128)(2,1)S(1)} %get-tuple-element.28), channel_id=1, source_target_pairs={{0,15},{1,0},{2,1},{3,2},{4,3},{5,4},{6,5},{7,6},{8,7},{9,8},{10,9... | collective-permute-start | bytes 983048 | tf_op jit(solution)/shard_map/ppermute | solution.py:36
  6.7 8.1 %collective-permute-start.2 = (bf16[8,16,256]{2,1,0:T(8,128)(2,1)}, bf16[8,16,256]{2,1,0:T(8,128)(2,1)S(1)}, u32[]{:S(2)}, u32[]{:S(2)}) collective-permute-start(bf16[8,16,256]{2,1,0:T(8,128)(2,1)} %left_ref.1), channel_id=1, source_target_pairs={{0,2},{1,3},{2,4},{3,5},{4,6},{5,7},{6,8},{7,9},{8,10},{9,11},{10,... | collective-permute-start | bytes 196616 | tf_op jit(solution)/shard_map/ppermute | solution.py:36
  14.8 4.1 %collective-permute-start.6 = (bf16[640,256]{1,0:T(8,128)(2,1)S(1)}, bf16[640,256]{1,0:T(8,128)(2,1)S(1)}, u32[]{:S(2)}, u32[]{:S(2)}) collective-permute-start(bf16[640,256]{1,0:T(8,128)(2,1)S(1)} %collective-permute-done.from_below.below_0), channel_id=1, source_target_pairs={{0,16},{1,17},{2,18},{3,19},{4,20},{5,21},{6,22},{7,23},{8,24},{9,... | collective-permute-start | bytes 983048 | tf_op jit(solution)/shard_map/ppermute | solution.py:36
  14.9 4.0 %collective-permute-start.7 = (bf16[640,256]{1,0:T(8,128)(2,1)S(1)}, bf16[640,256]{1,0:T(8,128)(2,1)S(1)}, u32[]{:S(2)}, u32[]{:S(2)}) collective-permute-start(bf16[640,256]{1,0:T(8,128)(2,1)S(1)} %collective-permute-done.1.from_above.above_0), channel_id=1, source_target_pairs={{0,16},{1,17},{2,18},{3,19},{4,20},{5,21},{6,22},{7,23},{8,24},{9,... | collective-permute-start | bytes 983048 | tf_op jit(solution)/shard_map/ppermute | solution.py:36
  15.4 10.4 %collective-permute-start.3 = (bf16[4,8,16,256]{3,2,1,0:T(8,128)(2,1)S(1)}, bf16[4,8,16,256]{3,2,1,0:T(8,128)(2,1)S(1)}, u32[]{:S(2)}, u32[]{:S(2)}) collective-permute-start(bf16[4,8,16,256]{3,2,1,0:T(8,128)(2,1)S(1)} %unpack.1.t0), channel_id=1, source_target_pairs={{0,4},{1,5},{2,6},{3,7},{4,8},{5,9},{6,10},{7,11},{8,12},{9,13},{1... | collective-permute-start | bytes 786440 | tf_op jit(solution)/shard_map/ppermute | solution.py:36
  15.4 10.4 %collective-permute-start.4 = (bf16[4,8,16,256]{3,2,1,0:T(8,128)(2,1)S(1)}, bf16[4,8,16,256]{3,2,1,0:T(8,128)(2,1)S(1)}, u32[]{:S(2)}, u32[]{:S(2)}) collective-permute-start(bf16[4,8,16,256]{3,2,1,0:T(8,128)(2,1)S(1)} %unpack.1.t0), channel_id=1, source_target_pairs={{0,8},{1,9},{2,10},{3,11},{4,12},{5,13},{6,14},{7,15},{8,0},{9,1},... | collective-permute-start | bytes 786440 | tf_op jit(solution)/shard_map/ppermute | solution.py:36
  17.5 9.2 %collective-permute-start.5 = (bf16[4,8,16,256]{3,2,1,0:T(8,128)(2,1)S(1)}, bf16[4,8,16,256]{3,2,1,0:T(8,128)(2,1)S(1)}, u32[]{:S(2)}, u32[]{:S(2)}) collective-permute-start(bf16[4,8,16,256]{3,2,1,0:T(8,128)(2,1)S(1)} %unpack.1.t0), channel_id=1, source_target_pairs={{0,12},{1,13},{2,14},{3,15},{4,0},{5,1},{6,2},{7,3},{8,4},{9,5},{1... | collective-permute-start | bytes 786440 | tf_op jit(solution)/shard_map/ppermute | solution.py:36
  18.8 0.7 %copy-start = (s32[8]{0:T(128)S(1)}, s32[8]{0:T(128)}, u32[]{:S(2)}) copy-start(s32[8]{0:T(128)} %shift_ref.5) | copy-start | bytes 100
  19.5 7.2 %copy-start.1 = (s32[8]{0:T(128)S(1)}, s32[8]{0:T(128)}, u32[]{:S(2)}) copy-start(s32[8]{0:T(128)} %shift_ref.5) | copy-start | bytes 100
  23.4 22.3 %copy-start.2 = (s32[16]{0:T(128)S(1)}, s32[16]{0:T(128)}, u32[]{:S(2)}) copy-start(s32[16]{0:T(128)} %dims_ref.3) | copy-start | bytes 196
  32.7 2.0 %collective-permute-start.9 = (bf16[4,8,32,256]{3,2,1,0:T(8,128)(2,1)S(1)}, bf16[4,8,32,256]{3,2,1,0:T(8,128)(2,1)S(1)}, u32[]{:S(2)}, u32[]{:S(2)}) collective-permute-start(bf16[4,8,32,256]{3,2,1,0:T(8,128)(2,1)S(1)} %get-tuple-element.40), channel_id=1, source_target_pairs={{0,16},{1,17},{2,18},{3,19},{4,20},{5,21},{6,22},{7,23},{8,24},{9,... | collective-permute-start | bytes 1572872 | tf_op jit(solution)/shard_map/ppermute | solution.py:36
  32.8 2.6 %collective-permute-start.8 = (bf16[4,8,32,256]{3,2,1,0:T(8,128)(2,1)S(1)}, bf16[4,8,32,256]{3,2,1,0:T(8,128)(2,1)S(1)}, u32[]{:S(2)}, u32[]{:S(2)}) collective-permute-start(bf16[4,8,32,256]{3,2,1,0:T(8,128)(2,1)S(1)} %get-tuple-element.39), channel_id=1, source_target_pairs={{0,16},{1,17},{2,18},{3,19},{4,20},{5,21},{6,22},{7,23},{8,24},{9,... | collective-permute-start | bytes 1572872 | tf_op jit(solution)/shard_map/ppermute | solution.py:36
  35.7 9.1 %collective-permute-start.11 = (bf16[16,32,256]{2,1,0:T(8,128)(2,1)S(1)}, bf16[16,32,256]{2,1,0:T(8,128)(2,1)S(1)}, u32[]{:S(2)}, u32[]{:S(2)}) collective-permute-start(bf16[16,32,256]{2,1,0:T(8,128)(2,1)S(1)} %get-tuple-element.44), channel_id=1, source_target_pairs={{0,32},{1,33},{2,34},{3,35},{4,36},{5,37},{6,38},{7,39},{8,40},{9,... | collective-permute-start | bytes 786440 | tf_op jit(solution)/shard_map/ppermute | solution.py:36
  37.7 8.2 %collective-permute-start.10 = (bf16[16,32,256]{2,1,0:T(8,128)(2,1)S(1)}, bf16[16,32,256]{2,1,0:T(8,128)(2,1)S(1)}, u32[]{:S(2)}, u32[]{:S(2)}) collective-permute-start(bf16[16,32,256]{2,1,0:T(8,128)(2,1)S(1)} %get-tuple-element.42), channel_id=1, source_target_pairs={{0,96},{1,97},{2,98},{3,99},{4,100},{5,101},{6,102},{7,103},{8,104... | collective-permute-start | bytes 786440 | tf_op jit(solution)/shard_map/ppermute | solution.py:36
  44.9 7.9 %collective-permute-start.12 = (bf16[16,32,256]{2,1,0:T(8,128)(2,1)S(1)}, bf16[16,32,256]{2,1,0:T(8,128)(2,1)S(1)}, u32[]{:S(2)}, u32[]{:S(2)}) collective-permute-start(bf16[16,32,256]{2,1,0:T(8,128)(2,1)S(1)} %add_convert_fusion), channel_id=1, source_target_pairs={{0,32},{1,33},{2,34},{3,35},{4,36},{5,37},{6,38},{7,39},{8,40},{9,... | collective-permute-start | bytes 786440 | tf_op jit(solution)/shard_map/ppermute | solution.py:36

commit v9 on v6

--- a/solution.py
+++ b/solution.py
@@ -261,13 +261,18 @@
     )(mine_a, mine_b, move(away_a, other_core), move(away_b, other_core))
     far = move(far, along_z(1))
     back = move(back, along_z(-1))
-    near = move((near + far.astype(F32)).astype(BF), along_z(1))
-    summed = own + back.astype(F32) + near.astype(F32)
     index = jnp.arange(B, dtype=jnp.int32)
-    live = index[None, :] < sector_dims[:, None]
-    mine_rows = p * 32 + jnp.arange(32, dtype=jnp.int32)
-    live_rows = mine_rows[None, :] < sector_dims[:, None]
-    return jnp.where(live_rows[:, :, None] & live[:, None, :], summed, 0.0).astype(BF)
+    live_columns = (index[None, :] < sector_dims[:, None])[:, None, :]
+
+    def live_at(chip):
+        rows = (chip * NC + core) * 32 + jnp.arange(32, dtype=jnp.int32)
+        return (rows[None, :] < sector_dims[:, None])[:, :, None] & live_columns
+
+    next_chip = (place[0] + jnp.where(core == 0, 1, NZ - 1)) % NZ
+    near = move(jnp.where(live_at(next_chip), near + far.astype(F32), 0.0).astype(BF), along_z(1))
+    here = jnp.where(live_at(place[0]), own + back.astype(F32), 0.0)
+    here = lax.optimization_barrier(here)
+    return (here + near.astype(F32)).astype(BF)
 
 
 def solution(mesh):

time: 53.5 us -> 56.3 us (1.052)
  waiting for transfers between devices: 19.3 us -> 22.7 us
  starting transfers between devices: 15.5 us -> 14.1 us
  Pallas kernels: 17.1 us -> 17.9 us
    ppermute x13, waiting for transfers between devices: 19.3 us -> 22.7 us  [move(): return lax.ppermute(block, ('op', 'sec'), route)]
    ppermute x13, starting transfers between devices: 15.5 us -> 14.1 us  [move(): return lax.ppermute(block, ('op', 'sec'), route)]
    pallas_call x1, Pallas kernels: 4.56 us -> 5.45 us  [on_device(): call(first_targets, 'first_targets', [smem, smem] + [vmem] * 5, first_a,...]
  transfers between devices with their start and end apart: 13 -> 13, of which waited for: 6 -> 7; matrix products, arithmetic and copies ran while one was open for 0% -> 0% of each run, Pallas kernels for 21% -> 20%
where the time goes in v9:
time: 56.3 us; the launch traced here: 56.2 us
  waiting for transfers between devices  22.7 us (40%)
  Pallas kernels  17.9 us (32%)
  starting transfers between devices  14.1 us (25%)
  other arithmetic  1.26 us (2%)
    ppermute x13, waiting for transfers between devices, move(): return lax.ppermute(block, ('op', 'sec'), route)  22.7 us
    ppermute x13, starting transfers between devices, move(): return lax.ppermute(block, ('op', 'sec'), route)  14.1 us
    pallas_call x1, Pallas kernels, on_device(): call(first_targets, 'first_targets', [smem, smem] + [vmem] * 5, first_a,...  5.45 us
    pallas_call x1, Pallas kernels, on_device(): call(first_operators, 'first_operators', [smem, hbm, hbm], [((SECS, B, B)...  5.36 us
    pallas_call x1, Pallas kernels, on_device(): call(other_sectors, 'other_sectors', [smem, smem] + [vmem] * 7, [((OPS, H...  3.91 us
    pallas_call x1, Pallas kernels, on_device(): call(functools.partial(some_targets, SPLIT), 'last_targets', [smem, vmem,...  1.79 us
    pallas_call x1, Pallas kernels, on_device(): pl.pallas_call(pack, grid=(1,), in_specs=[smem, *ends, pl.BlockSpec((OPS,...  1.22 us
  transfers between devices with their start and end apart: 13, of which 7 were waited for; matrix products, arithmetic and copies ran while one was open for 0% of the time, Pallas kernels for 20%

profile of v9, /device:TPU:0, one launch (start us, length us, event | category | flops | bytes accessed | tf_op | source)
XLA Modules:
  0.0 56.2 jit_solution(13123276667745352732)
XLA Ops:
  0.0 1.2 %pack.1 = (bf16[640,256]{1,0:T(8,128)(2,1)S(1)}, bf16[640,256]{1,0:T(8,128)(2,1)S(1)}) custom-call(s32[16]{0:T(128)} %dims_ref.3, bf16[16,256,256]{2,1,0:T(8,128)(2,1)} %psi_hbm.1, bf16[16,256,256]{2,1,0:T(8,128)(2,1)} %psi_hbm.1, bf16[8,16,256]{2,1,0:T(8,128)(2,1)} %left_ref.1), custom_call_target="tpu_custom_call" | custom-call | bytes 1048576 | tf_op jit(solution)/shard_map/pack/pallas_call | solution.py:223
  1.2 0.1 pad_add_fusion.place_ref
  1.3 1.6 %collective-permute-start = (bf16[640,256]{1,0:T(8,128)(2,1)S(1)}, bf16[640,256]{1,0:T(8,128)(2,1)S(1)}, u32[]{:S(2)}, u32[]{:S(2)}) collective-permute-start(bf16[640,256]{1,0:T(8,128)(2,1)S(1)} %get-tuple-element.27.own), channel_id=1, source_target_pairs={{0,1},{1,2},{2,3},{3,4},{4,5},{5,6},{6,7},{7,8},{8,9},{9,10},{10,1... | collective-permute-start | bytes 983048 | tf_op jit(solution)/shard_map/ppermute | solution.py:36
  2.9 3.8 %collective-permute-start.1 = (bf16[640,256]{1,0:T(8,128)(2,1)S(1)}, bf16[640,256]{1,0:T(8,128)(2,1)S(1)}, u32[]{:S(2)}, u32[]{:S(2)}) collective-permute-start(bf16[640,256]{1,0:T(8,128)(2,1)S(1)} %get-tuple-element.28), channel_id=1, source_target_pairs={{0,15},{1,0},{2,1},{3,2},{4,3},{5,4},{6,5},{7,6},{8,7},{9,8},{10,9... | collective-permute-start | bytes 983048 | tf_op jit(solution)/shard_map/ppermute | solution.py:36
  6.7 0.0 collective-permute-start.2
  6.7 5.4 %first_operators.1 = (bf16[16,256,256]{2,1,0:T(8,128)(2,1)S(1)}, bf16[8,256,256]{2,1,0:T(8,128)(2,1)S(1)}, bf16[8,5120,256]{2,1,0:T(8,128)(2,1)S(1)}, f32[8,128]{1,0:T(8,128)S(1)}) custom-call(s32[16]{0:T(128)} %dims_ref.3, bf16[16,256,256]{2,1,0:T(8,128)(2,1)} %psi_hbm.1, bf16[8,256,256]{2,1,0:T(8,128)(2,1)} %right_hbm.1), custom_call_target="tpu_custom_call" | custom-call | flops 2147483648 | bytes 4194304 | tf_op jit(solution)/shard_map/first_operators/pallas_call | solution.py:234
  12.1 2.6 %collective-permute-done.2.second_below = bf16[8,16,256]{2,1,0:T(8,128)(2,1)S(1)} collective-permute-done((bf16[8,16,256]{2,1,0:T(8,128)(2,1)S(1)}, bf16[8,16,256]{2,1,0:T(8,128)(2,1)S(1)}, u32[]{:S(2)}, u32[]{:S(2)}) %collective-permute-start.2) | collective-permute-done | bytes 65568 | tf_op jit(solution)/shard_map/ppermute | solution.py:36
  14.7 0.1 collective-permute-start.6
  14.8 0.5 collective-permute-start.7
  15.3 0.0 collective-permute-start.3
  15.3 2.0 %collective-permute-start.4 = (bf16[4,8,16,256]{3,2,1,0:T(8,128)(2,1)S(1)}, bf16[4,8,16,256]{3,2,1,0:T(8,128)(2,1)S(1)}, u32[]{:S(2)}, u32[]{:S(2)}) collective-permute-start(bf16[4,8,16,256]{3,2,1,0:T(8,128)(2,1)S(1)} %unpack.1.t0), channel_id=1, source_target_pairs={{0,8},{1,9},{2,10},{3,11},{4,12},{5,13},{6,14},{7,15},{8,0},{9,1},... | collective-permute-start | bytes 786440 | tf_op jit(solution)/shard_map/ppermute | solution.py:36
  17.4 1.3 %collective-permute-start.5 = (bf16[4,8,16,256]{3,2,1,0:T(8,128)(2,1)S(1)}, bf16[4,8,16,256]{3,2,1,0:T(8,128)(2,1)S(1)}, u32[]{:S(2)}, u32[]{:S(2)}) collective-permute-start(bf16[4,8,16,256]{3,2,1,0:T(8,128)(2,1)S(1)} %unpack.1.t0), channel_id=1, source_target_pairs={{0,12},{1,13},{2,14},{3,15},{4,0},{5,1},{6,2},{7,3},{8,4},{9,5},{1... | collective-permute-start | bytes 786440 | tf_op jit(solution)/shard_map/ppermute | solution.py:36
  18.7 0.0 collective-permute-done.6.below_1
  18.7 0.0 collective-permute-done.7.above_1
  18.7 3.9 %other_sectors.1.h_ref = bf16[8,5120,256]{2,1,0:T(8,128)(2,1)S(1)} custom-call(s32[8]{0:T(128)S(1)} %copy-done, s32[4]{0:T(128)S(1)} %pad_add_fusion.place_ref, bf16[640,256]{1,0:T(8,128)(2,1)S(1)} %collective-permute-done.from_below.below_0, bf16[640,256]{1,0:T(8,128)(2,1)S(1)} %collective-permute-done.1.from_above.above_0, ...), custom_call_target="tpu_custom_call", output_to_operand_aliasing={{}: (8, {})} | custom-call | tf_op jit(solution)/shard_map/other_sectors/pallas_call | solution.py:245
  22.6 3.1 %collective-permute-done.3.t1 = bf16[4,8,16,256]{3,2,1,0:T(8,128)(2,1)S(1)} collective-permute-done((bf16[4,8,16,256]{3,2,1,0:T(8,128)(2,1)S(1)}, bf16[4,8,16,256]{3,2,1,0:T(8,128)(2,1)S(1)}, u32[]{:S(2)}, u32[]{:S(2)}) %collective-permute-start.3) | collective-permute-done | bytes 262176 | tf_op jit(solution)/shard_map/ppermute | solution.py:36
  25.7 0.0 collective-permute-done.4.t2
  25.7 0.9 %collective-permute-done.5.t3 = bf16[4,8,16,256]{3,2,1,0:T(8,128)(2,1)S(1)} collective-permute-done((bf16[4,8,16,256]{3,2,1,0:T(8,128)(2,1)S(1)}, bf16[4,8,16,256]{3,2,1,0:T(8,128)(2,1)S(1)}, u32[]{:S(2)}, u32[]{:S(2)}) %collective-permute-start.5) | collective-permute-done | bytes 262176 | tf_op jit(solution)/shard_map/ppermute | solution.py:36
  26.6 5.5 %first_targets.1 = (f32[4,12,32,256]{3,2,1,0:T(8,128)S(1)}, bf16[4,12,32,256]{3,2,1,0:T(8,128)(2,1)}, bf16[256,2048]{1,0:T(8,128)(2,1)S(1)}) custom-call(s32[8]{0:T(128)S(1)} %copy-done, s32[4]{0:T(128)S(1)} %pad_add_fusion.place_ref, bf16[4,8,16,256]{3,2,1,0:T(8,128)(2,1)S(1)} %unpack.1.t0, bf16[4,8,16,256]{3,2,1,0:T(8,128)(2,1)S(1)} %collective-permute-done.3.t1, ...), custom_call_target="tpu_custom_call" | custom-call | flops 3221225472 | bytes 4194304 | tf_op jit(solution)/shard_map/first_targets/pallas_call | solution.py:251
  32.1 1.8 %last_targets.1 = (f32[4,4,32,256]{3,2,1,0:T(8,128)S(1)}, bf16[4,4,32,256]{3,2,1,0:T(8,128)(2,1)S(1)}) custom-call(s32[8]{0:T(128)S(1)} %copy-done, bf16[256,2048]{1,0:T(8,128)(2,1)S(1)} %get-tuple-element.37.left_ref, bf16[8,5120,256]{2,1,0:T(8,128)(2,1)S(1)} %other_sectors.1.h_ref), custom_call_target="tpu_custom_call" | custom-call | flops 1073741824 | bytes 4194304 | tf_op jit(solution)/shard_map/last_targets/pallas_call | solution.py:254
  33.9 0.6 %collective-permute-start.9 = (bf16[4,4,32,256]{3,2,1,0:T(8,128)(2,1)S(1)}, bf16[4,4,32,256]{3,2,1,0:T(8,128)(2,1)S(1)}, u32[]{:S(2)}, u32[]{:S(2)}) collective-permute-start(bf16[4,4,32,256]{3,2,1,0:T(8,128)(2,1)S(1)} %get-tuple-element.40), channel_id=1, source_target_pairs={{0,16},{1,17},{2,18},{3,19},{4,20},{5,21},{6,22},{7,23},{8,24},{9,... | collective-permute-start | bytes 786440 | tf_op jit(solution)/shard_map/ppermute | solution.py:36
  34.6 0.1 iota_compare_fusion
  34.6 1.0 %collective-permute-done.9.got_b = bf16[4,4,32,256]{3,2,1,0:T(8,128)(2,1)S(1)} collective-permute-done((bf16[4,4,32,256]{3,2,1,0:T(8,128)(2,1)S(1)}, bf16[4,4,32,256]{3,2,1,0:T(8,128)(2,1)S(1)}, u32[]{:S(2)}, u32[]{:S(2)}) %collective-permute-start.9) | collective-permute-done | bytes 262176 | tf_op jit(solution)/shard_map/ppermute | solution.py:36
  35.6 0.2 add_cores.1
  35.8 4.1 %collective-permute-start.10 = (bf16[16,32,256]{2,1,0:T(8,128)(2,1)S(1)}, bf16[16,32,256]{2,1,0:T(8,128)(2,1)S(1)}, u32[]{:S(2)}, u32[]{:S(2)}) collective-permute-start(bf16[16,32,256]{2,1,0:T(8,128)(2,1)S(1)} %get-tuple-element.42), channel_id=1, source_target_pairs={{0,96},{1,97},{2,98},{3,99},{4,100},{5,101},{6,102},{7,103},{8,104... | collective-permute-start | bytes 786440 | tf_op jit(solution)/shard_map/ppermute | solution.py:36
  39.9 0.1 broadcast_compare_fusion
  40.0 6.1 %collective-permute-done.10 = bf16[16,32,256]{2,1,0:T(8,128)(2,1)S(1)} collective-permute-done((bf16[16,32,256]{2,1,0:T(8,128)(2,1)S(1)}, bf16[16,32,256]{2,1,0:T(8,128)(2,1)S(1)}, u32[]{:S(2)}, u32[]{:S(2)}) %collective-permute-start.10) | collective-permute-done | bytes 262176 | tf_op jit(solution)/shard_map/ppermute | solution.py:36
  46.1 1.4 %collective-permute-done.11 = bf16[16,32,256]{2,1,0:T(8,128)(2,1)S(1)} collective-permute-done((bf16[16,32,256]{2,1,0:T(8,128)(2,1)S(1)}, bf16[16,32,256]{2,1,0:T(8,128)(2,1)S(1)}, u32[]{:S(2)}, u32[]{:S(2)}) %collective-permute-start.11) | collective-permute-done | bytes 262176 | tf_op jit(solution)/shard_map/ppermute | solution.py:36
  47.5 0.2 select_convert_fusion
  47.7 0.1 collective-permute-start.12
  47.8 7.6 %collective-permute-done.12 = bf16[16,32,256]{2,1,0:T(8,128)(2,1)S(1)} collective-permute-done((bf16[16,32,256]{2,1,0:T(8,128)(2,1)S(1)}, bf16[16,32,256]{2,1,0:T(8,128)(2,1)S(1)}, u32[]{:S(2)}, u32[]{:S(2)}) %collective-permute-start.12) | collective-permute-done | bytes 262176 | tf_op jit(solution)/shard_map/ppermute | solution.py:36
  55.4 0.8 %add_convert_fusion = bf16[16,32,256]{2,1,0:T(8,128)(2,1)} fusion(f32[16,32,256]{2,1,0:T(8,128)S(1)} %get-tuple-element.46, bf16[16,32,256]{2,1,0:T(8,128)(2,1)S(1)} %collective-permute-done.12), kind=kLoop, calls=%fused_computation | loop fusion | flops 393216 | bytes 1048576 | tf_op jit(solution)/shard_map/convert_element_type | solution.py:275
  (13 shorter events, 0.0 us)
Async XLA Ops:
  0.0 6.7 %copy-start.1 = (bf16[8,16,256]{2,1,0:T(8,128)(2,1)S(1)}, bf16[8,16,256]{2,1,0:T(8,128)(2,1)}, u32[]{:S(2)}) copy-start(bf16[8,16,256]{2,1,0:T(8,128)(2,1)} %left_ref.1) | copy-start | bytes 196612
  1.3 13.4 %collective-permute-start = (bf16[640,256]{1,0:T(8,128)(2,1)S(1)}, bf16[640,256]{1,0:T(8,128)(2,1)S(1)}, u32[]{:S(2)}, u32[]{:S(2)}) collective-permute-start(bf16[640,256]{1,0:T(8,128)(2,1)S(1)} %get-tuple-element.27.own), channel_id=1, source_target_pairs={{0,1},{1,2},{2,3},{3,4},{4,5},{5,6},{6,7},{7,8},{8,9},{9,10},{10,1... | collective-permute-start | bytes 983048 | tf_op jit(solution)/shard_map/ppermute | solution.py:36
  2.9 15.8 %copy-start = (s32[8]{0:T(128)S(1)}, s32[8]{0:T(128)}, u32[]{:S(2)}) copy-start(s32[8]{0:T(128)} %shift_ref.5) | copy-start | bytes 100
  2.9 11.8 %collective-permute-start.1 = (bf16[640,256]{1,0:T(8,128)(2,1)S(1)}, bf16[640,256]{1,0:T(8,128)(2,1)S(1)}, u32[]{:S(2)}, u32[]{:S(2)}) collective-permute-start(bf16[640,256]{1,0:T(8,128)(2,1)S(1)} %get-tuple-element.28), channel_id=1, source_target_pairs={{0,15},{1,0},{2,1},{3,2},{4,3},{5,4},{6,5},{7,6},{8,7},{9,8},{10,9... | collective-permute-start | bytes 983048 | tf_op jit(solution)/shard_map/ppermute | solution.py:36
  6.7 8.0 %collective-permute-start.2 = (bf16[8,16,256]{2,1,0:T(8,128)(2,1)S(1)}, bf16[8,16,256]{2,1,0:T(8,128)(2,1)S(1)}, u32[]{:S(2)}, u32[]{:S(2)}) collective-permute-start(bf16[8,16,256]{2,1,0:T(8,128)(2,1)S(1)} %copy-done.1), channel_id=1, source_target_pairs={{0,2},{1,3},{2,4},{3,5},{4,6},{5,7},{6,8},{7,9},{8,10},{9,11},{10,... | collective-permute-start | bytes 196616 | tf_op jit(solution)/shard_map/ppermute | solution.py:36
  14.7 4.0 %collective-permute-start.6 = (bf16[640,256]{1,0:T(8,128)(2,1)S(1)}, bf16[640,256]{1,0:T(8,128)(2,1)S(1)}, u32[]{:S(2)}, u32[]{:S(2)}) collective-permute-start(bf16[640,256]{1,0:T(8,128)(2,1)S(1)} %collective-permute-done.from_below.below_0), channel_id=1, source_target_pairs={{0,16},{1,17},{2,18},{3,19},{4,20},{5,21},{6,22},{7,23},{8,24},{9,... | collective-permute-start | bytes 983048 | tf_op jit(solution)/shard_map/ppermute | solution.py:36
  14.8 3.9 %collective-permute-start.7 = (bf16[640,256]{1,0:T(8,128)(2,1)S(1)}, bf16[640,256]{1,0:T(8,128)(2,1)S(1)}, u32[]{:S(2)}, u32[]{:S(2)}) collective-permute-start(bf16[640,256]{1,0:T(8,128)(2,1)S(1)} %collective-permute-done.1.from_above.above_0), channel_id=1, source_target_pairs={{0,16},{1,17},{2,18},{3,19},{4,20},{5,21},{6,22},{7,23},{8,24},{9,... | collective-permute-start | bytes 983048 | tf_op jit(solution)/shard_map/ppermute | solution.py:36
  15.3 10.4 %collective-permute-start.3 = (bf16[4,8,16,256]{3,2,1,0:T(8,128)(2,1)S(1)}, bf16[4,8,16,256]{3,2,1,0:T(8,128)(2,1)S(1)}, u32[]{:S(2)}, u32[]{:S(2)}) collective-permute-start(bf16[4,8,16,256]{3,2,1,0:T(8,128)(2,1)S(1)} %unpack.1.t0), channel_id=1, source_target_pairs={{0,4},{1,5},{2,6},{3,7},{4,8},{5,9},{6,10},{7,11},{8,12},{9,13},{1... | collective-permute-start | bytes 786440 | tf_op jit(solution)/shard_map/ppermute | solution.py:36
  15.3 10.4 %collective-permute-start.4 = (bf16[4,8,16,256]{3,2,1,0:T(8,128)(2,1)S(1)}, bf16[4,8,16,256]{3,2,1,0:T(8,128)(2,1)S(1)}, u32[]{:S(2)}, u32[]{:S(2)}) collective-permute-start(bf16[4,8,16,256]{3,2,1,0:T(8,128)(2,1)S(1)} %unpack.1.t0), channel_id=1, source_target_pairs={{0,8},{1,9},{2,10},{3,11},{4,12},{5,13},{6,14},{7,15},{8,0},{9,1},... | collective-permute-start | bytes 786440 | tf_op jit(solution)/shard_map/ppermute | solution.py:36
  17.4 9.3 %collective-permute-start.5 = (bf16[4,8,16,256]{3,2,1,0:T(8,128)(2,1)S(1)}, bf16[4,8,16,256]{3,2,1,0:T(8,128)(2,1)S(1)}, u32[]{:S(2)}, u32[]{:S(2)}) collective-permute-start(bf16[4,8,16,256]{3,2,1,0:T(8,128)(2,1)S(1)} %unpack.1.t0), channel_id=1, source_target_pairs={{0,12},{1,13},{2,14},{3,15},{4,0},{5,1},{6,2},{7,3},{8,4},{9,5},{1... | collective-permute-start | bytes 786440 | tf_op jit(solution)/shard_map/ppermute | solution.py:36
  32.1 3.6 %collective-permute-start.8 = (bf16[4,12,32,256]{3,2,1,0:T(8,128)(2,1)}, bf16[4,12,32,256]{3,2,1,0:T(8,128)(2,1)S(1)}, u32[]{:S(2)}, u32[]{:S(2)}) collective-permute-start(bf16[4,12,32,256]{3,2,1,0:T(8,128)(2,1)} %get-tuple-element.39), channel_id=1, source_target_pairs={{0,16},{1,17},{2,18},{3,19},{4,20},{5,21},{6,22},{7,23},{8,24},{9,... | collective-permute-start | bytes 2359304 | tf_op jit(solution)/shard_map/ppermute | solution.py:36
  32.1 2.5 %copy-start.2 = (s32[16]{0:T(128)S(1)}, s32[16]{0:T(128)}, u32[]{:S(2)}) copy-start(s32[16]{0:T(128)} %dims_ref.3) | copy-start | bytes 196
  33.9 1.7 %collective-permute-start.9 = (bf16[4,4,32,256]{3,2,1,0:T(8,128)(2,1)S(1)}, bf16[4,4,32,256]{3,2,1,0:T(8,128)(2,1)S(1)}, u32[]{:S(2)}, u32[]{:S(2)}) collective-permute-start(bf16[4,4,32,256]{3,2,1,0:T(8,128)(2,1)S(1)} %get-tuple-element.40), channel_id=1, source_target_pairs={{0,16},{1,17},{2,18},{3,19},{4,20},{5,21},{6,22},{7,23},{8,24},{9,... | collective-permute-start | bytes 786440 | tf_op jit(solution)/shard_map/ppermute | solution.py:36
  35.8 10.3 %collective-permute-start.10 = (bf16[16,32,256]{2,1,0:T(8,128)(2,1)S(1)}, bf16[16,32,256]{2,1,0:T(8,128)(2,1)S(1)}, u32[]{:S(2)}, u32[]{:S(2)}) collective-permute-start(bf16[16,32,256]{2,1,0:T(8,128)(2,1)S(1)} %get-tuple-element.42), channel_id=1, source_target_pairs={{0,96},{1,97},{2,98},{3,99},{4,100},{5,101},{6,102},{7,103},{8,104... | collective-permute-start | bytes 786440 | tf_op jit(solution)/shard_map/ppermute | solution.py:36
  39.9 7.6 %collective-permute-start.11 = (bf16[16,32,256]{2,1,0:T(8,128)(2,1)S(1)}, bf16[16,32,256]{2,1,0:T(8,128)(2,1)S(1)}, u32[]{:S(2)}, u32[]{:S(2)}) collective-permute-start(bf16[16,32,256]{2,1,0:T(8,128)(2,1)S(1)} %get-tuple-element.44), channel_id=1, source_target_pairs={{0,32},{1,33},{2,34},{3,35},{4,36},{5,37},{6,38},{7,39},{8,40},{9,... | collective-permute-start | bytes 786440 | tf_op jit(solution)/shard_map/ppermute | solution.py:36
  47.7 7.7 %collective-permute-start.12 = (bf16[16,32,256]{2,1,0:T(8,128)(2,1)S(1)}, bf16[16,32,256]{2,1,0:T(8,128)(2,1)S(1)}, u32[]{:S(2)}, u32[]{:S(2)}) collective-permute-start(bf16[16,32,256]{2,1,0:T(8,128)(2,1)S(1)} %get-tuple-element.45), channel_id=1, source_target_pairs={{0,32},{1,33},{2,34},{3,35},{4,36},{5,37},{6,38},{7,39},{8,40},{9,... | collective-permute-start | bytes 786440 | tf_op jit(solution)/shard_map/ppermute | solution.py:36
